TPU v7x, 32 devices: a whole 2x2x4 slice. The times are simulated.
32 devices in a mesh: tok: 16 (over z, x, core), mem: 2 (over y).
Axes of the slice: x: 2, y: 2, z: 4, core: 2. Of those that a mesh axis runs over, the one named last changes fastest.
Arguments:
- queries: bfloat16 [8192, 1024], P('tok', 'mem'), may hold values from -6 to 6
- keys: bfloat16 [8192, 1024], P('tok', 'mem'), may hold values from -6 to 6
- values: bfloat16 [8192, 1024], P('tok', 'mem'), may hold values from -6 to 6
- step_sizes: float32 [4, 8192], P(None, 'tok'), may hold values from 0.05 to 0.5
- fast_weights: float32 [4, 256, 768], P(None, 'mem'), may hold values from -0.375 to 0.375
- view_lengths: int32 [32], replicated, may hold values from 1 to 512, 8192 in all
Outputs:
- layer_out: bfloat16 [8192, 1024], P('tok', 'mem')
Inputs may be any that keep to these rules, and one draw needn't show every extreme that they name: `view_lengths`: the lengths sum to 8192 and the longest view has exactly 512 tokens.
All inputs are finite; a program needn't handle non-finite values.
Results may differ from a plain program's by a relative error of at most 0.011.
Values may be sent and summed in bfloat16 or wider, within the bound.
No kernel may reach another device: no remote copies, remote signals or barrier semaphores. Data moves between devices by JAX's collectives and lax.ppermute only.
A program may use at most 64 MiB of HBM per device.

v0:
```python
import math

import jax
import jax.numpy as jnp
from jax import lax
from jax.sharding import PartitionSpec as P

DM = 256
HD = 128


norm_epsilon = 1e-06


def extended(cells, sides, width):
    for axis, dim in sides:
        count = lax.axis_size(axis)
        ends = count - 1
        head = lax.slice_in_dim(cells, 0, width, axis=dim)
        tail = lax.slice_in_dim(cells, cells.shape[dim] - width, cells.shape[dim], axis=dim)
        cells = jnp.concatenate(
            [
                lax.ppermute(tail, axis, [(i, (i + 1) % count) for i in range(ends)]),
                cells,
                lax.ppermute(head, axis, [((i + 1) % count, i) for i in range(ends)]),
            ],
            axis=dim,
        )
    return cells


def silu_pair(pre_act):
    sigmoid_val = jax.nn.sigmoid(pre_act)
    return (pre_act * sigmoid_val, sigmoid_val * (1.0 + pre_act * (1.0 - sigmoid_val)))


def attend(queries, beside_all, same_view):
    tok_rows = queries.shape[0]
    feat_width = queries.shape[1]
    head_count = feat_width // HD
    score_scale = 1.0 / math.sqrt(HD)

    def one_head(head_index, result):
        offset = head_index * HD
        query_head = lax.dynamic_slice_in_dim(queries, offset, HD, 1)
        key_head = lax.dynamic_slice_in_dim(beside_all[0], offset, HD, 1)
        value_head = lax.dynamic_slice_in_dim(beside_all[1], offset, HD, 1)
        scores = (
            jnp.einsum("qd,kd->qk", query_head, key_head, preferred_element_type=jnp.float32)
            * score_scale
        )
        scores = jnp.where(same_view, scores, -1e30)
        row_peak = jnp.max(scores, axis=1, keepdims=True)
        exponent = jnp.exp(scores - row_peak)
        probs = (exponent / jnp.sum(exponent, axis=1, keepdims=True)).astype(jnp.bfloat16)
        output = jnp.dot(probs, value_head, preferred_element_type=jnp.float32)
        return lax.dynamic_update_slice_in_dim(result, output, offset, 1)

    return lax.fori_loop(0, head_count, one_head, jnp.zeros((tok_rows, feat_width), jnp.float32))


def memory_grads(key_part, value_part, token_rates, weights):
    rounded = weights.astype(jnp.bfloat16)
    weight_in = rounded[:, :DM]
    weight_up = rounded[:, DM : 2 * DM]
    weight_out = rounded[:, 2 * DM :]
    gate_pre = jnp.einsum("td,fd->tf", key_part, weight_in, preferred_element_type=jnp.float32)
    up_pre = jnp.einsum("td,fd->tf", key_part, weight_up, preferred_element_type=jnp.float32)
    swish_val, slope_val = silu_pair(gate_pre)
    hidden = (swish_val * up_pre).astype(jnp.bfloat16)
    scaled = (token_rates[:, None] * value_part.astype(jnp.float32)).astype(jnp.bfloat16)
    grad_out = -jnp.einsum("tf,td->fd", hidden, scaled, preferred_element_type=jnp.float32)
    back_flow = -jnp.einsum("td,fd->tf", scaled, weight_out, preferred_element_type=jnp.float32)
    gate_back = (back_flow * up_pre * slope_val).astype(jnp.bfloat16)
    up_back = (back_flow * swish_val).astype(jnp.bfloat16)
    grad_in = jnp.einsum("tf,td->fd", gate_back, key_part, preferred_element_type=jnp.float32)
    grad_up = jnp.einsum("tf,td->fd", up_back, key_part, preferred_element_type=jnp.float32)
    return jnp.concatenate([grad_in, grad_up, grad_out], axis=1)


def memory_read(query_part, weights):
    rounded = weights.astype(jnp.bfloat16)
    gate_pre = jnp.einsum(
        "td,fd->tf", query_part, rounded[:, :DM], preferred_element_type=jnp.float32
    )
    up_pre = jnp.einsum(
        "td,fd->tf", query_part, rounded[:, DM : 2 * DM], preferred_element_type=jnp.float32
    )
    swish_val, slope_val = silu_pair(gate_pre)
    read_hidden = (swish_val * up_pre).astype(jnp.bfloat16)
    return jnp.dot(read_hidden, rounded[:, 2 * DM :], preferred_element_type=jnp.float32)


def renormed(weights, gradient, step_rate):
    stepped = weights - gradient * step_rate
    shaped = stepped.reshape(stepped.shape[0], 3, DM)
    before = weights.reshape(weights.shape[0], 3, DM)
    old_norm = jnp.sqrt(jnp.sum(before * before, axis=2))
    new_norm = jnp.sqrt(jnp.sum(shaped * shaped, axis=2) + norm_epsilon)
    return (shaped * (old_norm / new_norm)[:, :, None]).reshape(stepped.shape)


def reduce_update(gradient, weights, step_rate):
    unit_count = gradient.shape[0] * gradient.shape[1]
    flat_grad = gradient.reshape(unit_count, 3 * DM)
    flat_weight = weights.reshape(unit_count, 3 * DM)
    summed = lax.psum(flat_grad, "tok")
    updated = renormed(flat_weight, summed, step_rate)
    return updated.reshape(weights.shape)


def on_device(queries, keys, values, step_sizes, fast_weights, view_lengths):
    tok_rows = queries.shape[0]
    all_tokens = tok_rows * lax.axis_size("tok")
    stacked = jnp.stack([keys, values])
    beside_all = extended(stacked, (("tok", 1),), tok_rows)
    view_ends = jnp.cumsum(view_lengths)
    row_start = lax.axis_index("tok") * tok_rows
    key_spots = row_start - tok_rows + jnp.arange(3 * tok_rows, dtype=jnp.int32)
    key_views = jnp.sum((view_ends[None, :] <= key_spots[:, None]).astype(jnp.int32), axis=1)
    key_views = jnp.where((key_spots >= 0) & (key_spots < all_tokens), key_views, -1)
    query_views = key_views[tok_rows : 2 * tok_rows]
    same_view = query_views[:, None] == key_views[None, :]
    attended = attend(queries, beside_all, same_view)
    step_rate = 1.0 / math.sqrt(all_tokens)
    weights = lax.all_to_all(fast_weights, "mem", split_axis=0, concat_axis=1, tiled=True)
    features = (queries, keys, values)
    owned_count = weights.shape[0]
    token_rates = lax.dynamic_slice_in_dim(
        step_sizes, lax.axis_index("mem") * owned_count, owned_count, 0
    )
    gradient = jnp.stack(
        [
            memory_grads(
                features[1][:, memory * DM : (memory + 1) * DM],
                features[2][:, memory * DM : (memory + 1) * DM],
                token_rates[memory],
                weights[memory],
            )
            for memory in range(weights.shape[0])
        ]
    )
    updated = reduce_update(gradient, weights, step_rate)
    memory_out = jnp.concatenate(
        [
            memory_read(features[0][:, memory * DM : (memory + 1) * DM], updated[memory])
            for memory in range(weights.shape[0])
        ],
        axis=1,
    )
    return (attended + memory_out).astype(jnp.bfloat16)


def solution(mesh):
    placed = (
        P("tok", "mem"),
        P("tok", "mem"),
        P("tok", "mem"),
        P(None, "tok"),
        P(None, "mem", None),
        P(),
    )
    return jax.shard_map(
        on_device, mesh=mesh, in_specs=placed, out_specs=P("tok", "mem"), check_vma=False
    )
```

profile of v0, /device:TPU:0, one launch (start us, length us, event | category | flops | bytes accessed | tf_op | source)
XLA Modules:
  0.0 151.1 jit_solution(8777962691744361782)
XLA Ops:
  6.5 4.4 %all-to-all-start = ((f32[4,128,768]{2,1,0:T(8,128)}), f32[4,128,768]{2,1,0:T(8,128)S(1)}, u32[]{:S(2)}, u32[]{:S(2)}) async-start(f32[4,128,768]{2,1,0:T(8,128)} %param.12), calls=%async_computation | async-start | bytes 3145728 | tf_op jit(solution)/shard_map/all_to_all | solution.py:126
  10.9 1.1 pad_maximum_fusion.2
  12.0 1.3 collective-permute-start.1
  13.3 4.1 %collective-permute-start = (bf16[2,512,512]{2,1,0:T(8,128)(2,1)}, bf16[2,512,512]{2,1,0:T(8,128)(2,1)}, u32[]{:S(2)}, u32[]{:S(2)}) collective-permute-start(bf16[2,512,512]{2,1,0:T(8,128)(2,1)} %pad_maximum_fusion.2), channel_id=1, source_target_pairs={{0,2},{2,4},{4,6},{6,8},{8,10},{10,12},{12,14},{14,16},{16,18},{18... | collective-permute-start | bytes 3145736 | tf_op jit(solution)/shard_map/ppermute | solution.py:23
  17.9 13.2 %all-to-all-done = f32[4,128,768]{2,1,0:T(8,128)S(1)} async-done(((f32[4,128,768]{2,1,0:T(8,128)}), f32[4,128,768]{2,1,0:T(8,128)S(1)}, u32[]{:S(2)}, u32[]{:S(2)}) %all-to-all-start) | async-done | bytes 1572896 | tf_op jit(solution)/shard_map/all_to_all | solution.py:126
  31.0 1.3 copy.32
  32.5 0.2 fusion.54
  32.7 0.3 fusion.52
  33.0 0.3 fusion.48
  33.3 0.3 fusion.46
  33.5 1.4 mul.141
  34.9 0.3 convolution_negate_fusion.1
  35.2 0.4 convolution_negate_fusion.3
  35.6 0.4 fusion.32
  36.0 0.3 convolution_negate_fusion
  36.3 0.4 convolution_negate_fusion.2
  36.7 0.4 fusion.33
  37.1 0.4 fusion.36
  37.6 0.5 fusion.37
  38.3 1.6 %copy.33 = f32[2,256,768]{2,1,0:T(8,128)} copy(f32[2,256,768]{1,2,0:T(8,128)S(1)} %pad_maximum_fusion.1) | data formatting | bytes 3145728 | tf_op jit(solution)/shard_map/stack | solution.py:132
  39.9 1.4 copy-done.1
  41.3 1.1 copy.35
  42.4 1.3 mul.142
  43.8 2.0 %pad_maximum_fusion = bf16[2,1536,512]{2,1,0:T(8,128)(2,1)S(1)} fusion(bf16[2,512,512]{2,1,0:T(8,128)(2,1)} %collective-permute-done.1, bf16[1,512,512]{2,1,0:T(8,128)(2,1)} %bitcast.63, bf16[1,512,512]{2,1,0:T(8,128)(2,1)} %bitcast.60, bf16[2,512,512]{2,1,0:T(8,128)(2,1)} %collective-permute-done), kind=kLoop, calls=%fused_computation.15 | loop fusion | flops 12582912 | bytes 6291456 | tf_op jit(solution)/shard_map/concatenate | solution.py:21
  45.8 1.1 broadcast_in_dim.26.clone
  47.0 16.2 %while.14 = (s32[]{:T(128)}, f32[512,512]{0,1:T(8,128)}, bf16[512,512]{1,0:T(8,128)(2,1)}, bf16[2,1536,512]{2,1,0:T(8,128)(2,1)S(1)}, s32[1536]{0:T(1024)S(1)}, ...) while((s32[]{:T(128)}, f32[512,512]{0,1:T(8,128)}, ...), condition=%wide.region_5.6_spmd.clone, body=%wide.region_2.5_spmd.clone.sunk | while | flops 409730048 | bytes 16930972 | solution.py:59
  47.2 1.6 %fusion.93 = (f32[512]{0:T(512)S(1)}, f32[512,1536]{1,0:T(8,128)S(1)}) fusion(bf16[1,1536,512]{2,1,0:T(8,128)(2,1)S(1)} %get-tuple-element.181, s32[]{:T(128)S(6)} %select_n.36, bf16[512,512]{1,0:T(8,128)(2,1)} %get-tuple-element.207, s32[1536]{0:T(1024)S(1)} %get-tuple-element.209, s32[512]{0:T(512)S(1)} %get-tuple-element.210), kind=kOutput, calls=%fused_computation.110.clone.1 | convolution fusion | flops 204471808 | bytes 3683328 | tf_op jit(solution)/shard_map/while/body/eval_jaxpr/qd,kd->qk/dot_general | solution.py:49
  48.8 0.6 fusion.94
  49.4 1.6 %fusion.95 = f32[512,512]{0,1:T(8,128)} fusion(f32[512,512]{0,1:T(8,128)} %get-tuple-element.196, s32[]{:T(128)S(6)} %select_n.36, f32[512,1536]{1,0:T(8,128)S(1)} %get-tuple-element.182, f32[512]{0:T(512)S(1)} %fusion.94, f32[512]{0:T(512)S(1)} %get-tuple-element.183, bf16[1,1536,512]{2,1,0:T(8,128)(2,1)S(1)} %get-tuple-element.184), kind=kOutput, calls=%fused_computation.7.clone.1 | convolution fusion | flops 203685888 | bytes 3806208 | tf_op jit(solution)/shard_map/while/body/eval_jaxpr/dynamic_update_slice | solution.py:57
  51.3 1.6 %fusion.93 = (f32[512]{0:T(512)S(1)}, f32[512,1536]{1,0:T(8,128)S(1)}) fusion(bf16[1,1536,512]{2,1,0:T(8,128)(2,1)S(1)} %get-tuple-element.181, s32[]{:T(128)S(6)} %select_n.36, bf16[512,512]{1,0:T(8,128)(2,1)} %get-tuple-element.207, s32[1536]{0:T(1024)S(1)} %get-tuple-element.209, s32[512]{0:T(512)S(1)} %get-tuple-element.210), kind=kOutput, calls=%fused_computation.110.clone.1 | convolution fusion | flops 204471808 | bytes 3683328 | tf_op jit(solution)/shard_map/while/body/eval_jaxpr/qd,kd->qk/dot_general | solution.py:49
  52.9 0.6 fusion.94
  53.5 1.7 %fusion.95 = f32[512,512]{0,1:T(8,128)} fusion(f32[512,512]{0,1:T(8,128)} %get-tuple-element.196, s32[]{:T(128)S(6)} %select_n.36, f32[512,1536]{1,0:T(8,128)S(1)} %get-tuple-element.182, f32[512]{0:T(512)S(1)} %fusion.94, f32[512]{0:T(512)S(1)} %get-tuple-element.183, bf16[1,1536,512]{2,1,0:T(8,128)(2,1)S(1)} %get-tuple-element.184), kind=kOutput, calls=%fused_computation.7.clone.1 | convolution fusion | flops 203685888 | bytes 3806208 | tf_op jit(solution)/shard_map/while/body/eval_jaxpr/dynamic_update_slice | solution.py:57
  55.3 1.6 %fusion.93 = (f32[512]{0:T(512)S(1)}, f32[512,1536]{1,0:T(8,128)S(1)}) fusion(bf16[1,1536,512]{2,1,0:T(8,128)(2,1)S(1)} %get-tuple-element.181, s32[]{:T(128)S(6)} %select_n.36, bf16[512,512]{1,0:T(8,128)(2,1)} %get-tuple-element.207, s32[1536]{0:T(1024)S(1)} %get-tuple-element.209, s32[512]{0:T(512)S(1)} %get-tuple-element.210), kind=kOutput, calls=%fused_computation.110.clone.1 | convolution fusion | flops 204471808 | bytes 3683328 | tf_op jit(solution)/shard_map/while/body/eval_jaxpr/qd,kd->qk/dot_general | solution.py:49
  57.0 0.6 fusion.94
  57.6 1.6 %fusion.95 = f32[512,512]{0,1:T(8,128)} fusion(f32[512,512]{0,1:T(8,128)} %get-tuple-element.196, s32[]{:T(128)S(6)} %select_n.36, f32[512,1536]{1,0:T(8,128)S(1)} %get-tuple-element.182, f32[512]{0:T(512)S(1)} %fusion.94, f32[512]{0:T(512)S(1)} %get-tuple-element.183, bf16[1,1536,512]{2,1,0:T(8,128)(2,1)S(1)} %get-tuple-element.184), kind=kOutput, calls=%fused_computation.7.clone.1 | convolution fusion | flops 203685888 | bytes 3806208 | tf_op jit(solution)/shard_map/while/body/eval_jaxpr/dynamic_update_slice | solution.py:57
  59.4 1.6 %fusion.93 = (f32[512]{0:T(512)S(1)}, f32[512,1536]{1,0:T(8,128)S(1)}) fusion(bf16[1,1536,512]{2,1,0:T(8,128)(2,1)S(1)} %get-tuple-element.181, s32[]{:T(128)S(6)} %select_n.36, bf16[512,512]{1,0:T(8,128)(2,1)} %get-tuple-element.207, s32[1536]{0:T(1024)S(1)} %get-tuple-element.209, s32[512]{0:T(512)S(1)} %get-tuple-element.210), kind=kOutput, calls=%fused_computation.110.clone.1 | convolution fusion | flops 204471808 | bytes 3683328 | tf_op jit(solution)/shard_map/while/body/eval_jaxpr/qd,kd->qk/dot_general | solution.py:49
  61.0 0.6 fusion.94
  61.6 1.6 %fusion.95 = f32[512,512]{0,1:T(8,128)} fusion(f32[512,512]{0,1:T(8,128)} %get-tuple-element.196, s32[]{:T(128)S(6)} %select_n.36, f32[512,1536]{1,0:T(8,128)S(1)} %get-tuple-element.182, f32[512]{0:T(512)S(1)} %fusion.94, f32[512]{0:T(512)S(1)} %get-tuple-element.183, bf16[1,1536,512]{2,1,0:T(8,128)(2,1)S(1)} %get-tuple-element.184), kind=kOutput, calls=%fused_computation.7.clone.1 | convolution fusion | flops 203685888 | bytes 3806208 | tf_op jit(solution)/shard_map/while/body/eval_jaxpr/dynamic_update_slice | solution.py:57
  63.2 72.7 %all-reduce.2.cloned.1.call-done = f32[512,768]{1,0:T(8,128)} async-done(((f32[512,768]{1,0:T(8,128)}), f32[512,768]{1,0:T(8,128)}) %all-reduce.2.cloned.1.call-update) | async-done | bytes 1572880 | tf_op jit(solution)/shard_map/psum | solution.py:107
  135.9 2.1 %bitcast_subtract_fusion = f32[512,768]{1,0:T(8,128)S(1)} fusion(f32[2,2,128,768]{3,2,1,0:T(8,128)} %copy.32, f32[512,768]{1,0:T(8,128)} %all-reduce.2.cloned.1.call-done), kind=kLoop, calls=%fused_computation.17 | loop fusion | flops 786432 | bytes 4718592 | tf_op jit(solution)/shard_map/sub | solution.py:95
  138.0 0.5 copy.34
  138.9 0.8 copy-done.4
  139.7 0.2 convolution_bitcast_fusion.1
  139.9 0.5 fusion.18
  140.4 1.0 convolution_bitcast_fusion.3
  141.4 1.6 %fusion.17 = f32[512,256]{0,1:T(8,128)S(1)} fusion(f32[512,256]{1,0:T(8,128)} %convolution_bitcast_fusion.3, bf16[512,512]{1,0:T(8,128)(2,1)S(1)} %copy-done.4, bf16[256,768]{0,1:T(8,128)(2,1)S(1)} %bitcast.72), kind=kOutput, calls=%fused_computation.32 | convolution fusion | flops 135004160 | bytes 1572864 | tf_op jit(solution)/shard_map/dot_general | solution.py:91
  143.0 0.3 fusion.19
  143.3 1.0 copy.41
  (37 shorter events, 2.2 us)
Async XLA Ops:
  6.5 4.4 %copy-start.2 = (bf16[512,512]{1,0:T(8,128)(2,1)S(1)}, bf16[512,512]{1,0:T(8,128)(2,1)}, u32[]{:S(2)}) copy-start(bf16[512,512]{1,0:T(8,128)(2,1)} %param.10) | copy-start | bytes 1572868
  6.5 4.4 %copy-start = (bf16[512,512]{1,0:T(8,128)(2,1)S(1)}, bf16[512,512]{1,0:T(8,128)(2,1)}, u32[]{:S(2)}) copy-start(bf16[512,512]{1,0:T(8,128)(2,1)} %param.9) | copy-start | bytes 1572868
  6.5 24.5 %all-to-all-start = ((f32[4,128,768]{2,1,0:T(8,128)}), f32[4,128,768]{2,1,0:T(8,128)S(1)}, u32[]{:S(2)}, u32[]{:S(2)}) async-start(f32[4,128,768]{2,1,0:T(8,128)} %param.12), calls=%async_computation | async-start | bytes 3145728 | tf_op jit(solution)/shard_map/all_to_all | solution.py:126
  10.9 6.5 %copy-start.6 = (s32[32]{0:T(128)S(1)}, s32[32]{0:T(128)}, u32[]{:S(2)}) copy-start(s32[32]{0:T(128)} %param.13) | copy-start | bytes 388
  10.9 6.9 %copy-start.5 = (f32[4,512]{1,0:T(4,128)S(1)}, f32[4,512]{1,0:T(4,128)}, u32[]{:S(2)}) copy-start(f32[4,512]{1,0:T(4,128)} %param.11) | copy-start | bytes 24580
  10.9 125.0 %all-reduce.2.cloned.1.call-start = ((), (), s32[]{:S(2)}) async-start(), calls=%async_computation.1 | async-start | bytes 3145728 | tf_op jit(solution)/shard_map/psum | solution.py:107
  12.0 31.8 %collective-permute-start.1 = (bf16[2,512,512]{2,1,0:T(8,128)(2,1)}, bf16[2,512,512]{2,1,0:T(8,128)(2,1)}, u32[]{:S(2)}, u32[]{:S(2)}) collective-permute-start(bf16[2,512,512]{2,1,0:T(8,128)(2,1)} %pad_maximum_fusion.2), channel_id=1, source_target_pairs={{2,0},{4,2},{6,4},{8,6},{10,8},{12,10},{14,12},{16,14},{18,16},{20... | collective-permute-start | bytes 3145736 | tf_op jit(solution)/shard_map/ppermute | solution.py:25
  13.3 30.5 %collective-permute-start = (bf16[2,512,512]{2,1,0:T(8,128)(2,1)}, bf16[2,512,512]{2,1,0:T(8,128)(2,1)}, u32[]{:S(2)}, u32[]{:S(2)}) collective-permute-start(bf16[2,512,512]{2,1,0:T(8,128)(2,1)} %pad_maximum_fusion.2), channel_id=1, source_target_pairs={{0,2},{2,4},{4,6},{6,8},{8,10},{10,12},{12,14},{14,16},{16,18},{18... | collective-permute-start | bytes 3145736 | tf_op jit(solution)/shard_map/ppermute | solution.py:23
  39.9 1.4 copy-start.1
  138.6 1.0 copy-start.4
  141.4 1.6 %copy-start.3 = (f32[512,512]{0,1:T(8,128)S(1)}, f32[512,512]{0,1:T(8,128)}, u32[]{:S(2)}) copy-start(f32[512,512]{0,1:T(8,128)} %get-tuple-element.99) | copy-start | bytes 3145732
Sparse Core Ops, SparseCore 0:
  40.0 95.8 all-reduce.1
where the time goes:
time: 152 us; the launch traced here: 151 us
  waiting for transfers between devices  85.9 us (57%)
  matrix products  20.5 us (13%)
  between operations  13.7 us (9%)
  local copies, waits for them, and re-layouts  11.1 us (7%)
  other arithmetic  10.2 us (7%)
  starting transfers between devices  9.76 us (6%)
    psum x1, waiting for transfers between devices, reduce_update(): summed = lax.psum(flat_grad, 'tok')  72.7 us
    all_to_all x1, waiting for transfers between devices, on_device(): lax.all_to_all(fast_weights, 'mem', split_axis=0, concat_axis=1, tiled=True)  13.2 us
    dot_general x4, matrix products, one_head(): jnp.einsum('qd,kd->qk', query_head, key_head, preferred_element_type=jnp....  6.58 us
    dynamic_update_slice x4, matrix products, one_head(): return lax.dynamic_update_slice_in_dim(result, output, offset, 1)  6.53 us
    all_to_all x1, starting transfers between devices, on_device(): lax.all_to_all(fast_weights, 'mem', split_axis=0, concat_axis=1, tiled=True)  4.37 us
    ppermute x1, starting transfers between devices, extended(): lax.ppermute(tail, axis, [(i, (i + 1) % count) for i in range(ends)])  4.11 us
  transfers between devices with their start and end apart: 4, of which 2 were waited for; matrix products, arithmetic and copies ran while one was open for 21% of the time, Pallas kernels for 0%

commit v1 on v0

v1 whole, which is shorter than its diff:
```python
import functools
import math

import jax
import jax.numpy as jnp
from jax import lax
from jax.experimental import pallas as pl
from jax.experimental.pallas import tpu as pltpu
from jax.sharding import PartitionSpec as P

DM = 256
HD = 128
CORES = 2
NORM_EPS = 1e-06
VMEM_BYTES = 40 * 2**20
MASKED = -1e30

BF16 = jnp.bfloat16
F32 = jnp.float32


def in_vmem(count):
    return [pl.BlockSpec(memory_space=pltpu.VMEM)] * count


def in_smem():
    return pl.BlockSpec(memory_space=pltpu.SMEM)


def params():
    return pltpu.CompilerParams(vmem_limit_bytes=VMEM_BYTES)


def dot_nt(a, b):
    return lax.dot_general(a, b, (((1,), (1,)), ((), ())), preferred_element_type=F32)


def dot_tn(a, b):
    return lax.dot_general(a, b, (((0,), (0,)), ((), ())), preferred_element_type=F32)


def dot_nn(a, b):
    return jnp.dot(a, b, preferred_element_type=F32)


def chip_digits(chips):
    digits = []
    while chips % 4 == 0:
        digits.append(4)
        chips //= 4
    if chips > 1:
        digits.append(chips)
    return digits[::-1]


def pick_kernel(chips, spots, weights_ref, rounded_ref, owned_ref):
    base, chip = spots[0], spots[1]
    memories, hidden, _ = rounded_ref.shape
    rows = hidden // chips
    for memory in range(memories):
        for block in range(chips):
            start = pl.multiple_of((chip ^ block) * rows, rows)
            part = weights_ref[base + memory, pl.ds(start, rows), :]
            rounded_ref[memory, pl.ds(block * rows, rows), :] = part.astype(BF16)
            if block == 0:
                owned_ref[memory] = part


def pick_weights(spots, weights, memories, chips):
    hidden = weights.shape[1]
    rows = hidden // chips
    shapes = (
        jax.ShapeDtypeStruct((memories, hidden, 3 * DM), BF16),
        jax.ShapeDtypeStruct((memories, rows, 3 * DM), F32),
    )
    if rows % 16:
        part = lax.dynamic_slice_in_dim(weights, spots[0], memories, 0)
        part = part.reshape(memories, chips, rows, 3 * DM)
        part = jnp.take(part, jnp.arange(chips, dtype=jnp.int32) ^ spots[1], axis=1)
        return part.reshape(shapes[0].shape).astype(BF16), part[:, 0]
    return pl.pallas_call(
        functools.partial(pick_kernel, chips),
        out_shape=shapes,
        in_specs=[in_smem()] + in_vmem(1),
        out_specs=tuple(in_vmem(2)),
        compiler_params=params(),
    )(spots, weights)


def grads_kernel(spots, own_k, own_v, mate_kv, own_rate, mate_rate, local_w, sent_w, grad_ref):
    core = spots[2]
    tokens = own_k.shape[0]
    memories, hidden, _ = local_w.shape
    for memory in range(memories):
        features = pl.ds(memory * DM, DM)
        weights = jnp.where(core == 0, local_w[memory], sent_w[memory])
        gate_up_w = jnp.concatenate([weights[:, :DM], weights[:, DM : 2 * DM]], axis=0)
        out_w = weights[:, 2 * DM :]
        grad_pair = jnp.zeros((2 * hidden, DM), F32)
        grad_out = jnp.zeros((hidden, DM), F32)
        for side in range(2):
            if side == 0:
                key, value, rate = own_k[:, features], own_v[:, features], own_rate
            else:
                key = mate_kv[pl.ds(0, tokens), features]
                value = mate_kv[pl.ds(tokens, tokens), features]
                rate = mate_rate
            rates = jnp.transpose(rate[...])[:, memory : memory + 1]
            scaled = (rates * value.astype(F32)).astype(BF16)
            gate_up = dot_nt(key, gate_up_w)
            gate, up = gate_up[:, :hidden], gate_up[:, hidden:]
            sigmoid = jax.nn.sigmoid(gate)
            swish = gate * sigmoid
            slope = sigmoid * (1.0 + gate * (1.0 - sigmoid))
            back = -dot_nt(scaled, out_w)
            pair = jnp.concatenate(
                [(back * up * slope).astype(BF16), (back * swish).astype(BF16)], axis=1
            )
            grad_pair += dot_tn(pair, key)
            grad_out -= dot_tn((swish * up).astype(BF16), scaled)
        grad_ref[memory, :, :DM] = grad_pair[:hidden].astype(BF16)
        grad_ref[memory, :, DM : 2 * DM] = grad_pair[hidden:].astype(BF16)
        grad_ref[memory, :, 2 * DM :] = grad_out.astype(BF16)


def half_grads(spots, own_k, own_v, mate_kv, own_rate, mate_rate, local_w, sent_w):
    return pl.pallas_call(
        grads_kernel,
        out_shape=jax.ShapeDtypeStruct(local_w.shape, BF16),
        in_specs=[in_smem()] + in_vmem(7),
        out_specs=in_vmem(1)[0],
        compiler_params=params(),
    )(spots, own_k, own_v, mate_kv, own_rate, mate_rate, local_w, sent_w)


def update_kernel(step_rate, parts, spots, *refs):
    grads, local_w, sent_w, new_ref = refs[:parts], refs[parts], refs[parts + 1], refs[parts + 2]
    total = grads[0][...].astype(F32)
    for part in grads[1:]:
        total += part[...].astype(F32)
    before = jnp.where(spots[2] == 0, local_w[...], sent_w[...])
    stepped = before - total * step_rate
    for block in range(3):
        columns = slice(block * DM, (block + 1) * DM)
        old, new = before[..., columns], stepped[..., columns]
        old_norm = jnp.sqrt(jnp.sum(old * old, axis=-1, keepdims=True))
        new_norm = jnp.sqrt(jnp.sum(new * new, axis=-1, keepdims=True) + NORM_EPS)
        new_ref[:, :, columns] = (new * (old_norm / new_norm)).astype(BF16)


def update_rows(spots, step_rate, grads, local_w, sent_w):
    return pl.pallas_call(
        functools.partial(update_kernel, step_rate, len(grads)),
        out_shape=jax.ShapeDtypeStruct(local_w.shape, BF16),
        in_specs=[in_smem()] + in_vmem(len(grads) + 2),
        out_specs=in_vmem(1)[0],
        compiler_params=params(),
    )(spots, *grads, local_w, sent_w)


def attend_kernel(spots, lengths, q_ref, own_k, own_v, mate_kv, far_kv, out_ref):
    tokens, width = q_ref.shape
    views = lengths.shape[0]
    own = spots[3]
    bases = (own, spots[4], spots[5])
    upto = lax.broadcasted_iota(jnp.int32, (views, views), 0) <= lax.broadcasted_iota(
        jnp.int32, (views, views), 1
    )
    ends = jnp.sum(jnp.where(upto, lengths[...], 0), axis=0, keepdims=True)
    spot = own + lax.broadcasted_iota(jnp.int32, (tokens, 1), 0)
    stop = jnp.min(jnp.where(ends > spot, ends, jnp.int32(2**30)), axis=1, keepdims=True)
    start = jnp.max(jnp.where(ends <= spot, ends, 0), axis=1, keepdims=True)
    scale = math.log2(math.e) / math.sqrt(HD)
    block_rows = tokens // 2
    for block in range(2):
        rows = pl.ds(block * block_rows, block_rows)
        first = start[block * block_rows : (block + 1) * block_rows]
        last = stop[block * block_rows : (block + 1) * block_rows]
        masks = []
        for base in bases:
            place = base + lax.broadcasted_iota(jnp.int32, (1, tokens), 1)
            masks.append((place >= first) & (place < last))
        for head in range(width // HD):
            lanes = pl.ds(head * HD, HD)
            query = q_ref[rows, lanes]
            key_parts = (own_k[:, lanes], mate_kv[:tokens, lanes], far_kv[:tokens, lanes])
            scores = [
                jnp.where(mask, dot_nt(query, key) * scale, MASKED)
                for mask, key in zip(masks, key_parts)
            ]
            peak = functools.reduce(
                jnp.maximum, [jnp.max(s, axis=1, keepdims=True) for s in scores]
            )
            weights = [jnp.exp2(s - peak) for s in scores]
            total = sum(jnp.sum(w, axis=1, keepdims=True) for w in weights)
            value_parts = (own_v[:, lanes], mate_kv[tokens:, lanes], far_kv[tokens:, lanes])
            mixed = sum(dot_nn(w.astype(BF16), v) for w, v in zip(weights, value_parts))
            out_ref[rows, lanes] = mixed / total


def attend(spots, lengths, queries, keys, values, mate_kv, far_kv):
    return pl.pallas_call(
        attend_kernel,
        out_shape=jax.ShapeDtypeStruct(queries.shape, F32),
        in_specs=[in_smem()] + in_vmem(6),
        out_specs=in_vmem(1)[0],
        compiler_params=params(),
    )(spots, lengths, queries, keys, values, mate_kv, far_kv)


def read_kernel(q_ref, own_w, mate_w, attended_ref, out_ref):
    chips, memories, rows, _ = own_w.shape
    for memory in range(memories):
        features = pl.ds(memory * DM, DM)
        query = q_ref[:, features]
        total = attended_ref[:, features]
        for half in (own_w, mate_w):
            weights = half[:, memory].reshape(chips * rows, 3 * DM)
            gate = dot_nt(query, weights[:, :DM])
            up = dot_nt(query, weights[:, DM : 2 * DM])
            hidden = (gate * jax.nn.sigmoid(gate) * up).astype(BF16)
            total += dot_nn(hidden, weights[:, 2 * DM :])
        out_ref[:, features] = total.astype(BF16)


def read_out(queries, own_w, mate_w, attended):
    return pl.pallas_call(
        read_kernel,
        out_shape=jax.ShapeDtypeStruct(queries.shape, BF16),
        in_specs=in_vmem(4),
        out_specs=in_vmem(1)[0],
        compiler_params=params(),
    )(queries, own_w, mate_w, attended)


def on_device(queries, keys, values, step_sizes, fast_weights, view_lengths):
    tokens = queries.shape[0]
    memories = queries.shape[1] // DM
    devices = lax.axis_size("tok")
    planes = lax.axis_size("mem")
    chips = devices // CORES
    digits = chip_digits(chips)
    spot, plane = lax.axis_index("tok"), lax.axis_index("mem")
    core, chip = spot % CORES, spot // CORES
    mate = spot ^ 1
    far = jnp.where(core == 0, spot - 1, spot + 1)
    source = jnp.where(core == 0, plane, planes - 1 - plane) * memories
    spots = jnp.stack([source, chip, core, spot * tokens, mate * tokens, far * tokens]).astype(
        jnp.int32
    )

    def to_core(x):
        return lax.ppermute(x, "tok", [(i, i ^ 1) for i in range(devices)])

    def to_far(x):
        pairs = [(i, i + 1) for i in range(1, devices - 1, 2)]
        pairs += [(i + 1, i) for i in range(1, devices - 1, 2)]
        return lax.ppermute(x, "tok", pairs)

    def to_chip(x, flip):
        pairs = [(i, (((i // CORES) ^ flip) * CORES) + i % CORES) for i in range(devices)]
        return lax.ppermute(x, "tok", pairs)

    def to_plane(x):
        pairs = [
            (i * planes + p, i * planes + planes - 1 - p)
            for i in range(1, devices, CORES)
            for p in range(planes)
        ]
        return lax.ppermute(x, ("tok", "mem"), pairs)

    local_w, local_rows = pick_weights(spots, fast_weights, memories, chips)
    sent_w = to_plane(local_w)
    pair = jnp.concatenate([keys, values], axis=0)
    mate_kv = to_core(pair)
    far_kv = to_far(pair)
    rates = lax.dynamic_slice_in_dim(step_sizes, plane * memories, memories, 0)
    rates = jnp.pad(rates, ((0, -memories % 8), (0, 0)))
    mate_rates = to_core(rates)
    sent_rows = to_plane(local_rows)

    grads = half_grads(spots, keys, values, mate_kv, rates, mate_rates, local_w, sent_w)
    rows = grads.shape[1] // chips
    held = grads.reshape(memories, chips, rows, 3 * DM).transpose(1, 0, 2, 3)
    stride = 1
    for place, radix in enumerate(digits):
        held = held.reshape((held.shape[0] // radix, radix) + held.shape[1:])
        kept = held[:, 0]
        came = [to_chip(held[:, step], step * stride) for step in range(1, radix)]
        stride *= radix
        if place < len(digits) - 1:
            held = sum([part.astype(F32) for part in came], kept.astype(F32)).astype(BF16)
    parts = [part.reshape(memories, rows, 3 * DM) for part in [kept] + came]
    all_tokens = tokens * devices
    fresh = update_rows(spots, 1.0 / math.sqrt(all_tokens), parts, local_rows, sent_rows)

    gathered = fresh[None]
    stride = 1
    for radix in digits:
        came = [to_chip(gathered, step * stride) for step in range(1, radix)]
        gathered = jnp.concatenate([gathered] + came, axis=0)
        stride *= radix
    mate_w = to_core(gathered)

    attended = attend(
        spots, view_lengths.reshape(-1, 1), queries, keys, values, mate_kv, far_kv
    )
    return read_out(queries, gathered, mate_w, attended)


def solution(mesh):
    placed = (
        P("tok", "mem"),
        P("tok", "mem"),
        P("tok", "mem"),
        P(None, "tok"),
        P(None, "mem", None),
        P(),
    )
    return jax.shard_map(
        on_device, mesh=mesh, in_specs=placed, out_specs=P("tok", "mem"), check_vma=False
    )
```

time: 152 us -> 75.1 us (0.49)
  waiting for transfers between devices: 85.9 us -> 26.4 us
  matrix products: 20.5 us -> 0 us
  starting transfers between devices: 9.76 us -> 29.4 us
  between operations: 13.7 us -> 0.17 us
  Pallas kernels: 0 us -> 13.2 us
  other arithmetic: 10.2 us -> 0.06 us
  local copies, waits for them, and re-layouts: 11.1 us -> 5.56 us
    psum x1 -> x0, waiting for transfers between devices: 72.7 us -> none  [reduce_update(): summed = lax.psum(flat_grad, 'tok')]
    ppermute x2 -> x14, waiting for transfers between devices: 0.01 us -> 26.4 us  [the longest x8 25.6 us: to_chip(): return lax.ppermute(x, 'tok', pairs)]
    ppermute x2 -> x14, starting transfers between devices: 5.39 us -> 29.4 us  [the longest x8 21.9 us: to_chip(): return lax.ppermute(x, 'tok', pairs)]
    dot_general x20 -> x0, matrix products: 14 us -> none  [the longest x4 6.58 us: one_head(): jnp.einsum('qd,kd->qk', query_head, key_head, preferred_element_type=jnp....]
    pallas_call x0 -> x5, Pallas kernels: none -> 13.2 us  [the longest x1 7.14 us: attend(): pl.pallas_call(attend_kernel, out_shape=jax.ShapeDtypeStruct(queries.shap...]
    all_to_all x1 -> x0, waiting for transfers between devices: 13.2 us -> none  [on_device(): lax.all_to_all(fast_weights, 'mem', split_axis=0, concat_axis=1, tiled=True)]
    dynamic_update_slice x4 -> x0, matrix products: 6.53 us -> none  [one_head(): return lax.dynamic_update_slice_in_dim(result, output, offset, 1)]
    all_to_all x1 -> x0, starting transfers between devices: 4.37 us -> none  [on_device(): lax.all_to_all(fast_weights, 'mem', split_axis=0, concat_axis=1, tiled=True)]
  transfers between devices with their start and end apart: 4 -> 14, of which waited for: 2 -> 8; matrix products, arithmetic and copies ran while one was open for 21% -> 0% of each run, Pallas kernels for 0% -> 11%
where the time goes in v1:
time: 75.1 us; the launch traced here: 74.8 us
  starting transfers between devices  29.4 us (39%)
  waiting for transfers between devices  26.4 us (35%)
  Pallas kernels  13.2 us (18%)
  local copies, waits for them, and re-layouts  5.56 us (7%)
    ppermute x8, waiting for transfers between devices, to_chip(): return lax.ppermute(x, 'tok', pairs)  25.6 us
    ppermute x8, starting transfers between devices, to_chip(): return lax.ppermute(x, 'tok', pairs)  21.9 us
    pallas_call x1, Pallas kernels, attend(): pl.pallas_call(attend_kernel, out_shape=jax.ShapeDtypeStruct(queries.shap...  7.14 us
    ppermute x3, starting transfers between devices, to_core(): return lax.ppermute(x, 'tok', [(i, i ^ 1) for i in range(devices)])  4.56 us
    unnamed x18, local copies, waits for them, and re-layouts  3.37 us
    pallas_call x1, Pallas kernels, half_grads(): pl.pallas_call(grads_kernel, out_shape=jax.ShapeDtypeStruct(local_w.shape...  2.77 us
    pallas_call x1, Pallas kernels, read_out(): pl.pallas_call(read_kernel, out_shape=jax.ShapeDtypeStruct(queries.shape,...  2.03 us
    concatenate x1, local copies, waits for them, and re-layouts, on_device(): pair = jnp.concatenate([keys, values], axis=0)  1.96 us
  transfers between devices with their start and end apart: 14, of which 8 were waited for; matrix products, arithmetic and copies ran while one was open for 0% of the time, Pallas kernels for 11%

profile of v1, /device:TPU:0, one launch (start us, length us, event | category | flops | bytes accessed | tf_op | source)
XLA Modules:
  0.0 74.8 jit_solution(7218401896728790545)
XLA Ops:
  0.0 0.0 copy-start
  0.0 1.9 %constant_dynamic-update-slice_fusion.1 = bf16[1024,512]{1,0:T(8,128)(2,1)} fusion(bf16[512,512]{1,0:T(8,128)(2,1)} %own_k.3), kind=kLoop, calls=%fused_computation.11 | loop fusion | bytes 1048576
  1.9 0.0 copy-start.1
  1.9 2.0 %constant_dynamic-update-slice_fusion = bf16[1024,512]{1,0:T(8,128)(2,1)} fusion(bf16[1024,512]{1,0:T(8,128)(2,1)} %constant_dynamic-update-slice_fusion.1, bf16[512,512]{1,0:T(8,128)(2,1)} %own_v.3), kind=kLoop, calls=%fused_computation.10 | loop fusion | bytes 1048576 | tf_op jit(solution)/shard_map/concatenate | solution.py:274
  3.9 0.5 collective-permute-start
  4.3 0.1 stack.27.spots
  4.4 1.4 %copy-done.4 = f32[4,128,768]{2,1,0:T(8,128)S(1)} copy-done((f32[4,128,768]{2,1,0:T(8,128)S(1)}, f32[4,128,768]{2,1,0:T(8,128)}, u32[]{:S(2)}) %copy-start.4) | copy-done | bytes 1572888
  5.8 0.6 shard_map.64
  6.4 0.7 collective-permute-start.2
  7.1 0.0 copy-done
  7.1 4.0 %collective-permute-start.1 = (f32[8,512]{1,0:T(8,128)S(1)}, f32[8,512]{1,0:T(8,128)S(1)}, u32[]{:S(2)}, u32[]{:S(2)}) collective-permute-start(f32[8,512]{1,0:T(8,128)S(1)} %pad.4.own_rate), channel_id=1, source_target_pairs={{0,2},{2,0},{4,6},{6,4},{8,10},{10,8},{12,14},{14,12},{16,18},{18,... | collective-permute-start | bytes 49160 | tf_op jit(solution)/shard_map/ppermute | solution.py:253
  11.2 0.8 %collective-permute-done.1.mate_rate = f32[8,512]{1,0:T(8,128)S(1)} collective-permute-done((f32[8,512]{1,0:T(8,128)S(1)}, f32[8,512]{1,0:T(8,128)S(1)}, u32[]{:S(2)}, u32[]{:S(2)}) %collective-permute-start.1) | collective-permute-done | bytes 16416 | tf_op jit(solution)/shard_map/ppermute | solution.py:253
  12.0 0.0 collective-permute-done.2.sent_w
  12.0 0.0 collective-permute-done.mate_kv
  12.0 0.0 copy-done.1
  12.0 0.0 copy-done.2
  12.0 2.8 %shard_map.65 = bf16[2,128,768]{2,1,0:T(8,128)(2,1)S(1)} custom-call(s32[6]{0:T(128)S(1)} %stack.27.spots, bf16[512,512]{1,0:T(8,128)(2,1)S(1)} %copy-done.1, bf16[512,512]{1,0:T(8,128)(2,1)S(1)} %copy-done.2, bf16[1024,512]{1,0:T(8,128)(2,1)S(1)} %collective-permute-done.mate_kv, f32[8,512]{1,0:T(8,128)S(1)} %pad.4.own_rate, ...), custom_call_target="tpu_custom_call" | custom-call | tf_op jit(solution)/shard_map/pallas_call | solution.py:127
  14.8 0.0 copy-start.5
  14.9 0.0 copy-start.3
  14.9 1.6 %collective-permute-start.3 = (bf16[4,2,16,768]{3,2,1,0:T(8,128)(2,1)S(1)}, bf16[4,2,16,768]{3,2,1,0:T(8,128)(2,1)S(1)}, u32[]{:S(2)}, u32[]{:S(2)}) collective-permute-start(bf16[4,2,16,768]{3,2,1,0:T(8,128)(2,1)S(1)} %bitcast.41), channel_id=1, source_target_pairs={{0,4},{2,6},{4,0},{6,2},{8,12},{10,14},{12,8},{14,10},{16,20},{18,... | collective-permute-start | bytes 589832 | tf_op jit(solution)/shard_map/ppermute | solution.py:262
  16.5 0.7 collective-permute-start.7
  17.1 3.5 %collective-permute-done.3 = bf16[4,2,16,768]{3,2,1,0:T(8,128)(2,1)S(1)} collective-permute-done((bf16[4,2,16,768]{3,2,1,0:T(8,128)(2,1)S(1)}, bf16[4,2,16,768]{3,2,1,0:T(8,128)(2,1)S(1)}, u32[]{:S(2)}, u32[]{:S(2)}) %collective-permute-start.3) | collective-permute-done | bytes 196640 | tf_op jit(solution)/shard_map/ppermute | solution.py:262
  20.6 0.1 fusion.1
  20.7 1.6 %collective-permute-start.4 = (bf16[1,2,16,768]{3,2,1,0:T(8,128)(2,1)S(1)}, bf16[1,2,16,768]{3,2,1,0:T(8,128)(2,1)S(1)}, u32[]{:S(2)}, u32[]{:S(2)}) collective-permute-start(bf16[1,2,16,768]{3,2,1,0:T(8,128)(2,1)S(1)} %get-tuple-element.13), channel_id=1, source_target_pairs={{0,8},{2,10},{4,12},{6,14},{8,0},{10,2},{12,4},{14,6},{16,24},{18,... | collective-permute-start | bytes 147464 | tf_op jit(solution)/shard_map/ppermute | solution.py:262
  22.3 2.6 %collective-permute-start.5 = (bf16[1,2,16,768]{3,2,1,0:T(8,128)(2,1)S(1)}, bf16[1,2,16,768]{3,2,1,0:T(8,128)(2,1)S(1)}, u32[]{:S(2)}, u32[]{:S(2)}) collective-permute-start(bf16[1,2,16,768]{3,2,1,0:T(8,128)(2,1)S(1)} %get-tuple-element.12), channel_id=1, source_target_pairs={{0,16},{2,18},{4,20},{6,22},{8,24},{10,26},{12,28},{14,30},{16,0},... | collective-permute-start | bytes 147464 | tf_op jit(solution)/shard_map/ppermute | solution.py:262
  24.9 0.2 collective-permute-start.6
  25.2 1.6 %collective-permute-start.13 = (bf16[1024,512]{1,0:T(8,128)(2,1)}, bf16[1024,512]{1,0:T(8,128)(2,1)}, u32[]{:S(2)}, u32[]{:S(2)}) collective-permute-start(bf16[1024,512]{1,0:T(8,128)(2,1)} %constant_dynamic-update-slice_fusion), channel_id=1, source_target_pairs={{2,4},{6,8},{10,12},{14,16},{18,20},{22,24},{26,28},{4,2},{8,6},{1... | collective-permute-start | bytes 3145736 | tf_op jit(solution)/shard_map/ppermute | solution.py:258
  26.8 0.0 collective-permute-done.7.refs_5_
  26.8 0.0 collective-permute-done.4
  26.8 1.1 %collective-permute-done.5 = bf16[1,2,16,768]{3,2,1,0:T(8,128)(2,1)S(1)} collective-permute-done((bf16[1,2,16,768]{3,2,1,0:T(8,128)(2,1)S(1)}, bf16[1,2,16,768]{3,2,1,0:T(8,128)(2,1)S(1)}, u32[]{:S(2)}, u32[]{:S(2)}) %collective-permute-start.5) | collective-permute-done | bytes 49184 | tf_op jit(solution)/shard_map/ppermute | solution.py:262
  27.9 3.1 %collective-permute-done.6 = bf16[1,2,16,768]{3,2,1,0:T(8,128)(2,1)S(1)} collective-permute-done((bf16[1,2,16,768]{3,2,1,0:T(8,128)(2,1)S(1)}, bf16[1,2,16,768]{3,2,1,0:T(8,128)(2,1)S(1)}, u32[]{:S(2)}, u32[]{:S(2)}) %collective-permute-start.6) | collective-permute-done | bytes 49184 | tf_op jit(solution)/shard_map/ppermute | solution.py:262
  30.9 0.7 shard_map.66
  31.6 1.6 %collective-permute-start.8 = (bf16[1,2,16,768]{3,2,1,0:T(8,128)(2,1)S(1)}, bf16[1,2,16,768]{3,2,1,0:T(8,128)(2,1)S(1)}, u32[]{:S(2)}, u32[]{:S(2)}) collective-permute-start(bf16[1,2,16,768]{3,2,1,0:T(8,128)(2,1)S(1)} %bitcast.36), channel_id=1, source_target_pairs={{0,4},{2,6},{4,0},{6,2},{8,12},{10,14},{12,8},{14,10},{16,20},{18,... | collective-permute-start | bytes 147464 | tf_op jit(solution)/shard_map/ppermute | solution.py:262
  33.2 12.1 %collective-permute-done.8 = bf16[1,2,16,768]{3,2,1,0:T(8,128)(2,1)S(1)} collective-permute-done((bf16[1,2,16,768]{3,2,1,0:T(8,128)(2,1)S(1)}, bf16[1,2,16,768]{3,2,1,0:T(8,128)(2,1)S(1)}, u32[]{:S(2)}, u32[]{:S(2)}) %collective-permute-start.8) | collective-permute-done | bytes 49184 | tf_op jit(solution)/shard_map/ppermute | solution.py:262
  45.3 11.8 %collective-permute-start.9 = (bf16[2,2,16,768]{3,2,1,0:T(8,128)(2,1)S(1)}, bf16[2,2,16,768]{3,2,1,0:T(8,128)(2,1)S(1)}, u32[]{:S(2)}, u32[]{:S(2)}) collective-permute-start(bf16[2,2,16,768]{3,2,1,0:T(8,128)(2,1)S(1)} %pad_maximum_fusion), channel_id=1, source_target_pairs={{0,8},{2,10},{4,12},{6,14},{8,0},{10,2},{12,4},{14,6},{16,24},{18,... | collective-permute-start | bytes 294920 | tf_op jit(solution)/shard_map/ppermute | solution.py:262
  57.1 1.8 %collective-permute-start.10 = (bf16[2,2,16,768]{3,2,1,0:T(8,128)(2,1)S(1)}, bf16[2,2,16,768]{3,2,1,0:T(8,128)(2,1)S(1)}, u32[]{:S(2)}, u32[]{:S(2)}) collective-permute-start(bf16[2,2,16,768]{3,2,1,0:T(8,128)(2,1)S(1)} %pad_maximum_fusion), channel_id=1, source_target_pairs={{0,16},{2,18},{4,20},{6,22},{8,24},{10,26},{12,28},{14,30},{16,0},... | collective-permute-start | bytes 294920 | tf_op jit(solution)/shard_map/ppermute | solution.py:262
  58.9 0.7 collective-permute-start.11
  59.6 0.3 collective-permute-done.9
  59.9 4.1 %collective-permute-done.10 = bf16[2,2,16,768]{3,2,1,0:T(8,128)(2,1)S(1)} collective-permute-done((bf16[2,2,16,768]{3,2,1,0:T(8,128)(2,1)S(1)}, bf16[2,2,16,768]{3,2,1,0:T(8,128)(2,1)S(1)}, u32[]{:S(2)}, u32[]{:S(2)}) %collective-permute-start.10) | collective-permute-done | bytes 98336 | tf_op jit(solution)/shard_map/ppermute | solution.py:262
  64.0 1.4 %collective-permute-done.11 = bf16[2,2,16,768]{3,2,1,0:T(8,128)(2,1)S(1)} collective-permute-done((bf16[2,2,16,768]{3,2,1,0:T(8,128)(2,1)S(1)}, bf16[2,2,16,768]{3,2,1,0:T(8,128)(2,1)S(1)}, u32[]{:S(2)}, u32[]{:S(2)}) %collective-permute-start.11) | collective-permute-done | bytes 98336 | tf_op jit(solution)/shard_map/ppermute | solution.py:262
  65.4 0.1 collective-permute-start.12
  65.5 0.0 copy-done.5
  65.5 0.1 copy.11.lengths
  65.6 0.0 collective-permute-done.13.far_kv
  65.6 0.0 copy-done.3
  65.6 7.1 %shard_map.67.attended_ref = f32[512,512]{1,0:T(8,128)S(1)} custom-call(s32[6]{0:T(128)S(1)} %stack.27.spots, s32[32,1]{1,0:T(8,128)S(1)} %copy.11.lengths, bf16[512,512]{1,0:T(8,128)(2,1)S(1)} %copy-done.3, bf16[512,512]{1,0:T(8,128)(2,1)S(1)} %copy-done.1, bf16[512,512]{1,0:T(8,128)(2,1)S(1)} %copy-done.2, ...), custom_call_target="tpu_custom_call" | custom-call | tf_op jit(solution)/shard_map/pallas_call | solution.py:202
  72.8 0.0 collective-permute-done.12.mate_w
  72.8 2.0 %shard_map.68 = bf16[512,512]{1,0:T(8,128)(2,1)} custom-call(bf16[512,512]{1,0:T(8,128)(2,1)S(1)} %copy-done.3, bf16[8,2,16,768]{3,2,1,0:T(8,128)(2,1)S(1)} %constant_dynamic-update-slice_fusion.2.own_w, bf16[8,2,16,768]{3,2,1,0:T(8,128)(2,1)S(1)} %collective-permute-done.12.mate_w, f32[512,512]{1,0:T(8,128)S(1)} %shard_map.67.attended_ref), custom_call_target="tpu_custom_call" | custom-call | tf_op jit(solution)/shard_map/pallas_call | solution.py:227
  (13 shorter events, 0.1 us)
Async XLA Ops:
  0.0 7.1 %copy-start = (f32[4,512]{1,0:T(4,128)S(1)}, f32[4,512]{1,0:T(4,128)}, u32[]{:S(2)}) copy-start(f32[4,512]{1,0:T(4,128)} %param.9) | copy-start | bytes 24580
  1.9 10.1 %copy-start.1 = (bf16[512,512]{1,0:T(8,128)(2,1)S(1)}, bf16[512,512]{1,0:T(8,128)(2,1)}, u32[]{:S(2)}) copy-start(bf16[512,512]{1,0:T(8,128)(2,1)} %own_k.3) | copy-start | bytes 1572868
  1.9 10.1 %copy-start.2 = (bf16[512,512]{1,0:T(8,128)(2,1)S(1)}, bf16[512,512]{1,0:T(8,128)(2,1)}, u32[]{:S(2)}) copy-start(bf16[512,512]{1,0:T(8,128)(2,1)} %own_v.3) | copy-start | bytes 1572868
  3.9 8.2 %collective-permute-start = (bf16[1024,512]{1,0:T(8,128)(2,1)}, bf16[1024,512]{1,0:T(8,128)(2,1)S(1)}, u32[]{:S(2)}, u32[]{:S(2)}) collective-permute-start(bf16[1024,512]{1,0:T(8,128)(2,1)} %constant_dynamic-update-slice_fusion), channel_id=1, source_target_pairs={{0,2},{2,0},{4,6},{6,4},{8,10},{10,8},{12,14},{14,12},{16,18},{18,... | collective-permute-start | bytes 3145736 | tf_op jit(solution)/shard_map/ppermute | solution.py:253
  4.4 1.4 %copy-start.4 = (f32[4,128,768]{2,1,0:T(8,128)S(1)}, f32[4,128,768]{2,1,0:T(8,128)}, u32[]{:S(2)}) copy-start(f32[4,128,768]{2,1,0:T(8,128)} %weights_ref.1) | copy-start | bytes 4718596
  6.4 5.6 %collective-permute-start.2 = (bf16[2,128,768]{2,1,0:T(8,128)(2,1)S(1)}, bf16[2,128,768]{2,1,0:T(8,128)(2,1)S(1)}, u32[]{:S(2)}, u32[]{:S(2)}) collective-permute-start(bf16[2,128,768]{2,1,0:T(8,128)(2,1)S(1)} %get-tuple-element.7.local_w), channel_id=1, source_target_pairs={{2,3},{3,2},{6,7},{7,6},{10,11},{11,10},{14,15},{15,14},{18,19},{1... | collective-permute-start | bytes 1179656 | tf_op jit(solution)/shard_map/ppermute | solution.py:270
  7.1 4.9 %collective-permute-start.1 = (f32[8,512]{1,0:T(8,128)S(1)}, f32[8,512]{1,0:T(8,128)S(1)}, u32[]{:S(2)}, u32[]{:S(2)}) collective-permute-start(f32[8,512]{1,0:T(8,128)S(1)} %pad.4.own_rate), channel_id=1, source_target_pairs={{0,2},{2,0},{4,6},{6,4},{8,10},{10,8},{12,14},{14,12},{16,18},{18,... | collective-permute-start | bytes 49160 | tf_op jit(solution)/shard_map/ppermute | solution.py:253
  14.8 50.7 %copy-start.5 = (s32[32]{0:T(128)S(1)}, s32[32]{0:T(128)}, u32[]{:S(2)}) copy-start(s32[32]{0:T(128)} %param.11) | copy-start | bytes 388
  14.9 50.8 %copy-start.3 = (bf16[512,512]{1,0:T(8,128)(2,1)S(1)}, bf16[512,512]{1,0:T(8,128)(2,1)}, u32[]{:S(2)}) copy-start(bf16[512,512]{1,0:T(8,128)(2,1)} %q_ref.3) | copy-start | bytes 1572868
  14.9 5.7 %collective-permute-start.3 = (bf16[4,2,16,768]{3,2,1,0:T(8,128)(2,1)S(1)}, bf16[4,2,16,768]{3,2,1,0:T(8,128)(2,1)S(1)}, u32[]{:S(2)}, u32[]{:S(2)}) collective-permute-start(bf16[4,2,16,768]{3,2,1,0:T(8,128)(2,1)S(1)} %bitcast.41), channel_id=1, source_target_pairs={{0,4},{2,6},{4,0},{6,2},{8,12},{10,14},{12,8},{14,10},{16,20},{18,... | collective-permute-start | bytes 589832 | tf_op jit(solution)/shard_map/ppermute | solution.py:262
  16.5 10.3 %collective-permute-start.7 = (f32[2,16,768]{2,1,0:T(8,128)S(1)}, f32[2,16,768]{2,1,0:T(8,128)S(1)}, u32[]{:S(2)}, u32[]{:S(2)}) collective-permute-start(f32[2,16,768]{2,1,0:T(8,128)S(1)} %get-tuple-element.8.refs_4_), channel_id=1, source_target_pairs={{2,3},{3,2},{6,7},{7,6},{10,11},{11,10},{14,15},{15,14},{18,19},{1... | collective-permute-start | bytes 294920 | tf_op jit(solution)/shard_map/ppermute | solution.py:270
  20.7 6.1 %collective-permute-start.4 = (bf16[1,2,16,768]{3,2,1,0:T(8,128)(2,1)S(1)}, bf16[1,2,16,768]{3,2,1,0:T(8,128)(2,1)S(1)}, u32[]{:S(2)}, u32[]{:S(2)}) collective-permute-start(bf16[1,2,16,768]{3,2,1,0:T(8,128)(2,1)S(1)} %get-tuple-element.13), channel_id=1, source_target_pairs={{0,8},{2,10},{4,12},{6,14},{8,0},{10,2},{12,4},{14,6},{16,24},{18,... | collective-permute-start | bytes 147464 | tf_op jit(solution)/shard_map/ppermute | solution.py:262
  22.3 5.5 %collective-permute-start.5 = (bf16[1,2,16,768]{3,2,1,0:T(8,128)(2,1)S(1)}, bf16[1,2,16,768]{3,2,1,0:T(8,128)(2,1)S(1)}, u32[]{:S(2)}, u32[]{:S(2)}) collective-permute-start(bf16[1,2,16,768]{3,2,1,0:T(8,128)(2,1)S(1)} %get-tuple-element.12), channel_id=1, source_target_pairs={{0,16},{2,18},{4,20},{6,22},{8,24},{10,26},{12,28},{14,30},{16,0},... | collective-permute-start | bytes 147464 | tf_op jit(solution)/shard_map/ppermute | solution.py:262
  24.9 6.0 %collective-permute-start.6 = (bf16[1,2,16,768]{3,2,1,0:T(8,128)(2,1)S(1)}, bf16[1,2,16,768]{3,2,1,0:T(8,128)(2,1)S(1)}, u32[]{:S(2)}, u32[]{:S(2)}) collective-permute-start(bf16[1,2,16,768]{3,2,1,0:T(8,128)(2,1)S(1)} %get-tuple-element.11), channel_id=1, source_target_pairs={{0,24},{2,26},{4,28},{6,30},{8,16},{10,18},{12,20},{14,22},{16,8},... | collective-permute-start | bytes 147464 | tf_op jit(solution)/shard_map/ppermute | solution.py:262
  25.2 40.5 %collective-permute-start.13 = (bf16[1024,512]{1,0:T(8,128)(2,1)}, bf16[1024,512]{1,0:T(8,128)(2,1)}, u32[]{:S(2)}, u32[]{:S(2)}) collective-permute-start(bf16[1024,512]{1,0:T(8,128)(2,1)} %constant_dynamic-update-slice_fusion), channel_id=1, source_target_pairs={{2,4},{6,8},{10,12},{14,16},{18,20},{22,24},{26,28},{4,2},{8,6},{1... | collective-permute-start | bytes 3145736 | tf_op jit(solution)/shard_map/ppermute | solution.py:258
  31.6 13.6 %collective-permute-start.8 = (bf16[1,2,16,768]{3,2,1,0:T(8,128)(2,1)S(1)}, bf16[1,2,16,768]{3,2,1,0:T(8,128)(2,1)S(1)}, u32[]{:S(2)}, u32[]{:S(2)}) collective-permute-start(bf16[1,2,16,768]{3,2,1,0:T(8,128)(2,1)S(1)} %bitcast.36), channel_id=1, source_target_pairs={{0,4},{2,6},{4,0},{6,2},{8,12},{10,14},{12,8},{14,10},{16,20},{18,... | collective-permute-start | bytes 147464 | tf_op jit(solution)/shard_map/ppermute | solution.py:262
  45.3 14.6 %collective-permute-start.9 = (bf16[2,2,16,768]{3,2,1,0:T(8,128)(2,1)S(1)}, bf16[2,2,16,768]{3,2,1,0:T(8,128)(2,1)S(1)}, u32[]{:S(2)}, u32[]{:S(2)}) collective-permute-start(bf16[2,2,16,768]{3,2,1,0:T(8,128)(2,1)S(1)} %pad_maximum_fusion), channel_id=1, source_target_pairs={{0,8},{2,10},{4,12},{6,14},{8,0},{10,2},{12,4},{14,6},{16,24},{18,... | collective-permute-start | bytes 294920 | tf_op jit(solution)/shard_map/ppermute | solution.py:262
  57.1 6.9 %collective-permute-start.10 = (bf16[2,2,16,768]{3,2,1,0:T(8,128)(2,1)S(1)}, bf16[2,2,16,768]{3,2,1,0:T(8,128)(2,1)S(1)}, u32[]{:S(2)}, u32[]{:S(2)}) collective-permute-start(bf16[2,2,16,768]{3,2,1,0:T(8,128)(2,1)S(1)} %pad_maximum_fusion), channel_id=1, source_target_pairs={{0,16},{2,18},{4,20},{6,22},{8,24},{10,26},{12,28},{14,30},{16,0},... | collective-permute-start | bytes 294920 | tf_op jit(solution)/shard_map/ppermute | solution.py:262
  58.9 6.5 %collective-permute-start.11 = (bf16[2,2,16,768]{3,2,1,0:T(8,128)(2,1)S(1)}, bf16[2,2,16,768]{3,2,1,0:T(8,128)(2,1)S(1)}, u32[]{:S(2)}, u32[]{:S(2)}) collective-permute-start(bf16[2,2,16,768]{3,2,1,0:T(8,128)(2,1)S(1)} %pad_maximum_fusion), channel_id=1, source_target_pairs={{0,24},{2,26},{4,28},{6,30},{8,16},{10,18},{12,20},{14,22},{16,8},... | collective-permute-start | bytes 294920 | tf_op jit(solution)/shard_map/ppermute | solution.py:262
  65.4 7.3 %collective-permute-start.12 = (bf16[8,2,16,768]{3,2,1,0:T(8,128)(2,1)S(1)}, bf16[8,2,16,768]{3,2,1,0:T(8,128)(2,1)S(1)}, u32[]{:S(2)}, u32[]{:S(2)}) collective-permute-start(bf16[8,2,16,768]{3,2,1,0:T(8,128)(2,1)S(1)} %constant_dynamic-update-slice_fusion.2.own_w), channel_id=1, source_target_pairs={{0,2},{2,0},{4,6},{6,4},{8,10},{10,8},{12,14},{14,12},{16,18},{18,... | collective-permute-start | bytes 1179656 | tf_op jit(solution)/shard_map/ppermute | solution.py:253

commit v2 on v1

--- a/solution.py
+++ b/solution.py
@@ -53,58 +53,55 @@
     return digits[::-1]
 
 
-def pick_kernel(chips, spots, weights_ref, rounded_ref, owned_ref):
+def pick_kernel(chips, spots, weights_ref, picked_ref):
     base, chip = spots[0], spots[1]
-    memories, hidden, _ = rounded_ref.shape
+    memories, hidden = picked_ref.shape[0], weights_ref.shape[1]
     rows = hidden // chips
     for memory in range(memories):
         for block in range(chips):
             start = pl.multiple_of((chip ^ block) * rows, rows)
             part = weights_ref[base + memory, pl.ds(start, rows), :]
-            rounded_ref[memory, pl.ds(block * rows, rows), :] = part.astype(BF16)
+            rounded = part.astype(BF16)
+            picked_ref[memory, pl.ds(block * rows, rows), :] = rounded
             if block == 0:
-                owned_ref[memory] = part
+                rest = part - rounded.astype(F32)
+                picked_ref[memory, pl.ds(hidden, rows), :] = rest.astype(BF16)
 
 
 def pick_weights(spots, weights, memories, chips):
     hidden = weights.shape[1]
     rows = hidden // chips
-    shapes = (
-        jax.ShapeDtypeStruct((memories, hidden, 3 * DM), BF16),
-        jax.ShapeDtypeStruct((memories, rows, 3 * DM), F32),
-    )
     if rows % 16:
         part = lax.dynamic_slice_in_dim(weights, spots[0], memories, 0)
         part = part.reshape(memories, chips, rows, 3 * DM)
         part = jnp.take(part, jnp.arange(chips, dtype=jnp.int32) ^ spots[1], axis=1)
-        return part.reshape(shapes[0].shape).astype(BF16), part[:, 0]
+        rounded = part.astype(BF16)
+        rest = (part[:, :1] - rounded[:, :1].astype(F32)).astype(BF16)
+        picked = jnp.concatenate([rounded, rest], axis=1)
+        return picked.reshape(memories, hidden + rows, 3 * DM)
     return pl.pallas_call(
         functools.partial(pick_kernel, chips),
-        out_shape=shapes,
+        out_shape=jax.ShapeDtypeStruct((memories, hidden + rows, 3 * DM), BF16),
         in_specs=[in_smem()] + in_vmem(1),
-        out_specs=tuple(in_vmem(2)),
+        out_specs=in_vmem(1)[0],
         compiler_params=params(),
     )(spots, weights)
 
 
-def grads_kernel(spots, own_k, own_v, mate_kv, own_rate, mate_rate, local_w, sent_w, grad_ref):
+def grads_kernel(
+    spots, own_k, own_v, mate_k, mate_v, own_rate, mate_rate, local_w, sent_w, grad_ref
+):
     core = spots[2]
-    tokens = own_k.shape[0]
-    memories, hidden, _ = local_w.shape
+    memories, hidden, _ = grad_ref.shape
     for memory in range(memories):
         features = pl.ds(memory * DM, DM)
-        weights = jnp.where(core == 0, local_w[memory], sent_w[memory])
+        weights = jnp.where(core == 0, local_w[memory, :hidden], sent_w[memory, :hidden])
         gate_up_w = jnp.concatenate([weights[:, :DM], weights[:, DM : 2 * DM]], axis=0)
         out_w = weights[:, 2 * DM :]
         grad_pair = jnp.zeros((2 * hidden, DM), F32)
         grad_out = jnp.zeros((hidden, DM), F32)
-        for side in range(2):
-            if side == 0:
-                key, value, rate = own_k[:, features], own_v[:, features], own_rate
-            else:
-                key = mate_kv[pl.ds(0, tokens), features]
-                value = mate_kv[pl.ds(tokens, tokens), features]
-                rate = mate_rate
+        for key_ref, value_ref, rate in ((own_k, own_v, own_rate), (mate_k, mate_v, mate_rate)):
+            key, value = key_ref[:, features], value_ref[:, features]
             rates = jnp.transpose(rate[...])[:, memory : memory + 1]
             scaled = (rates * value.astype(F32)).astype(BF16)
             gate_up = dot_nt(key, gate_up_w)
@@ -123,14 +120,15 @@
         grad_ref[memory, :, 2 * DM :] = grad_out.astype(BF16)
 
 
-def half_grads(spots, own_k, own_v, mate_kv, own_rate, mate_rate, local_w, sent_w):
+def half_grads(spots, hidden, own_k, own_v, mate_k, mate_v, own_rate, mate_rate, local_w, sent_w):
+    shape = (local_w.shape[0], hidden, local_w.shape[2])
     return pl.pallas_call(
         grads_kernel,
-        out_shape=jax.ShapeDtypeStruct(local_w.shape, BF16),
-        in_specs=[in_smem()] + in_vmem(7),
-        out_specs=in_vmem(1)[0],
-        compiler_params=params(),
-    )(spots, own_k, own_v, mate_kv, own_rate, mate_rate, local_w, sent_w)
+        out_shape=jax.ShapeDtypeStruct(shape, BF16),
+        in_specs=[in_smem()] + in_vmem(8),
+        out_specs=in_vmem(1)[0],
+        compiler_params=params(),
+    )(spots, own_k, own_v, mate_k, mate_v, own_rate, mate_rate, local_w, sent_w)
 
 
 def update_kernel(step_rate, parts, spots, *refs):
@@ -138,7 +136,9 @@
     total = grads[0][...].astype(F32)
     for part in grads[1:]:
         total += part[...].astype(F32)
-    before = jnp.where(spots[2] == 0, local_w[...], sent_w[...])
+    rows = new_ref.shape[1]
+    picked = jnp.where(spots[2] == 0, local_w[...], sent_w[...]).astype(F32)
+    before = picked[:, :rows] + picked[:, -rows:]
     stepped = before - total * step_rate
     for block in range(3):
         columns = slice(block * DM, (block + 1) * DM)
@@ -151,18 +151,15 @@
 def update_rows(spots, step_rate, grads, local_w, sent_w):
     return pl.pallas_call(
         functools.partial(update_kernel, step_rate, len(grads)),
-        out_shape=jax.ShapeDtypeStruct(local_w.shape, BF16),
+        out_shape=jax.ShapeDtypeStruct(grads[0].shape, BF16),
         in_specs=[in_smem()] + in_vmem(len(grads) + 2),
         out_specs=in_vmem(1)[0],
         compiler_params=params(),
     )(spots, *grads, local_w, sent_w)
 
 
-def attend_kernel(spots, lengths, q_ref, own_k, own_v, mate_kv, far_kv, out_ref):
-    tokens, width = q_ref.shape
+def view_bounds(lengths, own, tokens):
     views = lengths.shape[0]
-    own = spots[3]
-    bases = (own, spots[4], spots[5])
     upto = lax.broadcasted_iota(jnp.int32, (views, views), 0) <= lax.broadcasted_iota(
         jnp.int32, (views, views), 1
     )
@@ -170,42 +167,90 @@
     spot = own + lax.broadcasted_iota(jnp.int32, (tokens, 1), 0)
     stop = jnp.min(jnp.where(ends > spot, ends, jnp.int32(2**30)), axis=1, keepdims=True)
     start = jnp.max(jnp.where(ends <= spot, ends, 0), axis=1, keepdims=True)
-    scale = math.log2(math.e) / math.sqrt(HD)
+    return start, stop
+
+
+def inside(base, count, start, stop):
+    place = base + lax.broadcasted_iota(jnp.int32, (1, count), 1)
+    return (place >= start) & (place < stop)
+
+
+SCORE_SCALE = math.log2(math.e) / math.sqrt(HD)
+
+
+def near_kernel(spots, lengths, q_ref, own_k, own_v, mate_k, mate_v, mixed_ref, peak_ref, sum_ref):
+    tokens, width = q_ref.shape
+    start, stop = view_bounds(lengths, spots[3], tokens)
     block_rows = tokens // 2
     for block in range(2):
-        rows = pl.ds(block * block_rows, block_rows)
-        first = start[block * block_rows : (block + 1) * block_rows]
-        last = stop[block * block_rows : (block + 1) * block_rows]
-        masks = []
-        for base in bases:
-            place = base + lax.broadcasted_iota(jnp.int32, (1, tokens), 1)
-            masks.append((place >= first) & (place < last))
+        rows = slice(block * block_rows, (block + 1) * block_rows)
+        masks = [inside(spots[3 + i], tokens, start[rows], stop[rows]) for i in range(2)]
         for head in range(width // HD):
             lanes = pl.ds(head * HD, HD)
             query = q_ref[rows, lanes]
-            key_parts = (own_k[:, lanes], mate_kv[:tokens, lanes], far_kv[:tokens, lanes])
             scores = [
-                jnp.where(mask, dot_nt(query, key) * scale, MASKED)
-                for mask, key in zip(masks, key_parts)
+                jnp.where(mask, dot_nt(query, key[:, lanes]) * SCORE_SCALE, MASKED)
+                for mask, key in zip(masks, (own_k, mate_k))
             ]
             peak = functools.reduce(
                 jnp.maximum, [jnp.max(s, axis=1, keepdims=True) for s in scores]
             )
             weights = [jnp.exp2(s - peak) for s in scores]
-            total = sum(jnp.sum(w, axis=1, keepdims=True) for w in weights)
-            value_parts = (own_v[:, lanes], mate_kv[tokens:, lanes], far_kv[tokens:, lanes])
-            mixed = sum(dot_nn(w.astype(BF16), v) for w, v in zip(weights, value_parts))
+            peak_ref[rows, head : head + 1] = peak
+            sum_ref[rows, head : head + 1] = sum(
+                jnp.sum(w, axis=1, keepdims=True) for w in weights
+            )
+            mixed_ref[rows, lanes] = sum(
+                dot_nn(w.astype(BF16), v[:, lanes]) for w, v in zip(weights, (own_v, mate_v))
+            )
+
+
+def far_kernel(
+    spots, lengths, q_ref, far_k, far_v, mixed_ref, peak_ref, sum_ref, out_ref
+):
+    tokens, width = q_ref.shape
+    start, stop = view_bounds(lengths, spots[3], tokens)
+    block_rows = tokens // 2
+    for block in range(2):
+        rows = slice(block * block_rows, (block + 1) * block_rows)
+        mask = inside(spots[5], tokens, start[rows], stop[rows])
+        for head in range(width // HD):
+            lanes = pl.ds(head * HD, HD)
+            scores = dot_nt(q_ref[rows, lanes], far_k[:, lanes]) * SCORE_SCALE
+            scores = jnp.where(mask, scores, MASKED)
+            before = peak_ref[rows, head : head + 1]
+            peak = jnp.maximum(before, jnp.max(scores, axis=1, keepdims=True))
+            weights = jnp.exp2(scores - peak)
+            shrink = jnp.exp2(before - peak)
+            total = sum_ref[rows, head : head + 1] * shrink + jnp.sum(
+                weights, axis=1, keepdims=True
+            )
+            mixed = mixed_ref[rows, lanes] * shrink + dot_nn(
+                weights.astype(BF16), far_v[:, lanes]
+            )
             out_ref[rows, lanes] = mixed / total
 
 
-def attend(spots, lengths, queries, keys, values, mate_kv, far_kv):
-    return pl.pallas_call(
-        attend_kernel,
+def attend_near(spots, lengths, queries, keys, values, mate_k, mate_v):
+    tokens, width = queries.shape
+    stats = jax.ShapeDtypeStruct((tokens, width // HD), F32)
+    return pl.pallas_call(
+        near_kernel,
+        out_shape=(jax.ShapeDtypeStruct(queries.shape, F32), stats, stats),
+        in_specs=[in_smem()] + in_vmem(6),
+        out_specs=tuple(in_vmem(3)),
+        compiler_params=params(),
+    )(spots, lengths, queries, keys, values, mate_k, mate_v)
+
+
+def attend_far(spots, lengths, queries, far_k, far_v, near):
+    return pl.pallas_call(
+        far_kernel,
         out_shape=jax.ShapeDtypeStruct(queries.shape, F32),
-        in_specs=[in_smem()] + in_vmem(6),
-        out_specs=in_vmem(1)[0],
-        compiler_params=params(),
-    )(spots, lengths, queries, keys, values, mate_kv, far_kv)
+        in_specs=[in_smem()] + in_vmem(7),
+        out_specs=in_vmem(1)[0],
+        compiler_params=params(),
+    )(spots, lengths, queries, far_k, far_v, *near)
 
 
 def read_kernel(q_ref, own_w, mate_w, attended_ref, out_ref):
@@ -269,42 +314,51 @@
         ]
         return lax.ppermute(x, ("tok", "mem"), pairs)
 
-    local_w, local_rows = pick_weights(spots, fast_weights, memories, chips)
+    hidden = fast_weights.shape[1]
+    rows = hidden // chips
+    local_w = pick_weights(spots, fast_weights, memories, chips)
     sent_w = to_plane(local_w)
-    pair = jnp.concatenate([keys, values], axis=0)
-    mate_kv = to_core(pair)
-    far_kv = to_far(pair)
+    far_k = to_far(keys)
+    mate_k, mate_v = to_core(keys), to_core(values)
     rates = lax.dynamic_slice_in_dim(step_sizes, plane * memories, memories, 0)
     rates = jnp.pad(rates, ((0, -memories % 8), (0, 0)))
     mate_rates = to_core(rates)
-    sent_rows = to_plane(local_rows)
-
-    grads = half_grads(spots, keys, values, mate_kv, rates, mate_rates, local_w, sent_w)
-    rows = grads.shape[1] // chips
+    lengths = view_lengths.reshape(-1, 1)
+
+    near = attend_near(spots, lengths, queries, keys, values, mate_k, mate_v)
+    grads = half_grads(
+        spots, hidden, keys, values, mate_k, mate_v, rates, mate_rates, local_w, sent_w
+    )
+    grads, far_k, near = lax.optimization_barrier((grads, far_k, near))
     held = grads.reshape(memories, chips, rows, 3 * DM).transpose(1, 0, 2, 3)
+    far_v = None
     stride = 1
     for place, radix in enumerate(digits):
         held = held.reshape((held.shape[0] // radix, radix) + held.shape[1:])
         kept = held[:, 0]
         came = [to_chip(held[:, step], step * stride) for step in range(1, radix)]
+        if far_v is None:
+            came, far_v = lax.optimization_barrier((came, values))
+            far_v = to_far(far_v)
         stride *= radix
         if place < len(digits) - 1:
             held = sum([part.astype(F32) for part in came], kept.astype(F32)).astype(BF16)
     parts = [part.reshape(memories, rows, 3 * DM) for part in [kept] + came]
     all_tokens = tokens * devices
-    fresh = update_rows(spots, 1.0 / math.sqrt(all_tokens), parts, local_rows, sent_rows)
+    fresh = update_rows(spots, 1.0 / math.sqrt(all_tokens), parts, local_w, sent_w)
 
     gathered = fresh[None]
-    stride = 1
-    for radix in digits:
+    for place, radix in enumerate(digits[::-1]):
+        stride //= radix
+        if place == len(digits) - 1:
+            gathered, far_v = lax.optimization_barrier((gathered, far_v))
         came = [to_chip(gathered, step * stride) for step in range(1, radix)]
+        if place == len(digits) - 1:
+            attended = attend_far(spots, lengths, queries, far_k, far_v, near)
+            came, attended = lax.optimization_barrier((came, attended))
         gathered = jnp.concatenate([gathered] + came, axis=0)
-        stride *= radix
     mate_w = to_core(gathered)
 
-    attended = attend(
-        spots, view_lengths.reshape(-1, 1), queries, keys, values, mate_kv, far_kv
-    )
     return read_out(queries, gathered, mate_w, attended)
 
 

time: 75.1 us -> 62 us (0.83)
  starting transfers between devices: 29.4 us -> 21.4 us
  waiting for transfers between devices: 26.4 us -> 22.4 us
  local copies, waits for them, and re-layouts: 5.56 us -> 1.7 us
  Pallas kernels: 13.2 us -> 15.9 us
    ppermute x8, starting transfers between devices: 21.9 us -> 11.7 us  [to_chip(): return lax.ppermute(x, 'tok', pairs)]
    ppermute x8, waiting for transfers between devices: 25.6 us -> 20.6 us  [to_chip(): return lax.ppermute(x, 'tok', pairs)]
    pallas_call x3 -> x4, Pallas kernels: 10.5 us -> 13.2 us  [the longest x1 4.87 us: attend_near(): pl.pallas_call(near_kernel, out_shape=(jax.ShapeDtypeStruct(queries.shape...]
    ppermute x3 -> x4, starting transfers between devices: 4.56 us -> 6.71 us  [to_core(): return lax.ppermute(x, 'tok', [(i, i ^ 1) for i in range(devices)])]
    concatenate x1 -> x0, local copies, waits for them, and re-layouts: 1.96 us -> none  [on_device(): pair = jnp.concatenate([keys, values], axis=0)]
    unnamed x18 -> x14, local copies, waits for them, and re-layouts: 3.37 us -> 1.46 us
    ppermute x3 -> x4, waiting for transfers between devices: 0.84 us -> 1.72 us  [to_core(): return lax.ppermute(x, 'tok', [(i, i ^ 1) for i in range(devices)])]
    ppermute x1 -> x2, starting transfers between devices: 1.63 us -> 2.32 us  [to_far(): return lax.ppermute(x, 'tok', pairs)]
  transfers between devices with their start and end apart: 14 -> 15, of which waited for: 8 -> 8; matrix products, arithmetic and copies ran while one was open for 0% -> 0% of each run, Pallas kernels for 11% -> 23%
where the time goes in v2:
time: 62 us; the launch traced here: 61.7 us
  waiting for transfers between devices  22.4 us (36%)
  starting transfers between devices  21.4 us (35%)
  Pallas kernels  15.9 us (26%)
  local copies, waits for them, and re-layouts  1.7 us (3%)
    ppermute x8, waiting for transfers between devices, to_chip(): return lax.ppermute(x, 'tok', pairs)  20.6 us
    ppermute x8, starting transfers between devices, to_chip(): return lax.ppermute(x, 'tok', pairs)  11.7 us
    ppermute x4, starting transfers between devices, to_core(): return lax.ppermute(x, 'tok', [(i, i ^ 1) for i in range(devices)])  6.71 us
    pallas_call x1, Pallas kernels, attend_near(): pl.pallas_call(near_kernel, out_shape=(jax.ShapeDtypeStruct(queries.shape...  4.87 us
    pallas_call x1, Pallas kernels, attend_far(): pl.pallas_call(far_kernel, out_shape=jax.ShapeDtypeStruct(queries.shape,...  4.79 us
    pallas_call x1, Pallas kernels, half_grads(): pl.pallas_call(grads_kernel, out_shape=jax.ShapeDtypeStruct(shape, BF16),...  2.95 us
    ppermute x2, starting transfers between devices, to_far(): return lax.ppermute(x, 'tok', pairs)  2.32 us
    pallas_call x1, Pallas kernels, read_out(): pl.pallas_call(read_kernel, out_shape=jax.ShapeDtypeStruct(queries.shape,...  2.03 us
  transfers between devices with their start and end apart: 15, of which 8 were waited for; matrix products, arithmetic and copies ran while one was open for 0% of the time, Pallas kernels for 23%

profile of v2, /device:TPU:0, one launch (start us, length us, event | category | flops | bytes accessed | tf_op | source)
XLA Modules:
  0.0 61.7 jit_solution(10431486907079180697)
XLA Ops:
  0.0 0.0 copy-start
  0.0 0.0 copy-start.2
  0.0 0.0 copy-start.3
  0.0 0.5 collective-permute-start
  0.5 0.1 collective-permute-start.1
  0.6 1.5 %collective-permute-start.4 = (bf16[512,512]{1,0:T(8,128)(2,1)}, bf16[512,512]{1,0:T(8,128)(2,1)}, u32[]{:S(2)}, u32[]{:S(2)}) collective-permute-start(bf16[512,512]{1,0:T(8,128)(2,1)} %own_k.3), channel_id=1, source_target_pairs={{2,4},{6,8},{10,12},{14,16},{18,20},{22,24},{26,28},{4,2},{8,6},{1... | collective-permute-start | bytes 1572872 | tf_op jit(solution)/shard_map/ppermute | solution.py:303
  2.1 0.1 stack.27.spots
  2.2 0.0 copy-start.4
  2.2 1.4 %copy-done.4 = f32[4,128,768]{2,1,0:T(8,128)S(1)} copy-done((f32[4,128,768]{2,1,0:T(8,128)S(1)}, f32[4,128,768]{2,1,0:T(8,128)}, u32[]{:S(2)}) %copy-start.4) | copy-done | bytes 1572888
  3.6 0.6 shard_map.64.local_w.refs_4_
  4.2 0.7 %collective-permute-start.3 = (bf16[2,144,768]{2,1,0:T(8,128)(2,1)S(1)}, bf16[2,144,768]{2,1,0:T(8,128)(2,1)S(1)}, u32[]{:S(2)}, u32[]{:S(2)}) collective-permute-start(bf16[2,144,768]{2,1,0:T(8,128)(2,1)S(1)} %shard_map.64.local_w.refs_4_), channel_id=1, source_target_pairs={{2,3},{3,2},{6,7},{7,6},{10,11},{11,10},{14,15},{15,14},{18,19},{1... | collective-permute-start | bytes 1327112 | tf_op jit(solution)/shard_map/ppermute | solution.py:315
  4.9 0.0 copy-done
  4.9 6.0 %collective-permute-start.2 = (f32[8,512]{1,0:T(8,128)S(1)}, f32[8,512]{1,0:T(8,128)}, u32[]{:S(2)}, u32[]{:S(2)}) collective-permute-start(f32[8,512]{1,0:T(8,128)S(1)} %pad.4.own_rate), channel_id=1, source_target_pairs={{0,2},{2,0},{4,6},{6,4},{8,10},{10,8},{12,14},{14,12},{16,18},{18,... | collective-permute-start | bytes 49160 | tf_op jit(solution)/shard_map/ppermute | solution.py:298
  10.9 0.0 copy-done.5
  11.0 0.1 copy.9.lengths
  11.0 0.0 collective-permute-done.mate_k
  11.0 0.0 collective-permute-done.1.mate_v
  11.0 0.0 copy-done.2
  11.1 0.0 copy-done.3
  11.1 0.0 copy-done.1
  11.1 4.9 %shard_map.66 = (f32[512,512]{1,0:T(8,128)S(1)}, f32[512,4]{1,0:T(8,128)S(1)}, f32[512,4]{1,0:T(8,128)S(1)}) custom-call(s32[6]{0:T(128)S(1)} %stack.27.spots, s32[32,1]{1,0:T(8,128)S(1)} %copy.9.lengths, bf16[512,512]{1,0:T(8,128)(2,1)S(1)} %copy-done.1, bf16[512,512]{1,0:T(8,128)(2,1)S(1)} %copy-done.2, bf16[512,512]{1,0:T(8,128)(2,1)S(1)} %copy-done.3, ...), custom_call_target="tpu_custom_call" | custom-call | tf_op jit(solution)/shard_map/pallas_call | solution.py:237
  16.0 0.0 collective-permute-done.2.mate_rate
  16.0 0.0 collective-permute-done.3.sent_w.refs_5_
  16.0 3.0 %shard_map.65 = bf16[2,128,768]{2,1,0:T(8,128)(2,1)S(1)} custom-call(s32[6]{0:T(128)S(1)} %stack.27.spots, bf16[512,512]{1,0:T(8,128)(2,1)S(1)} %copy-done.2, bf16[512,512]{1,0:T(8,128)(2,1)S(1)} %copy-done.3, bf16[512,512]{1,0:T(8,128)(2,1)S(1)} %collective-permute-done.mate_k, bf16[512,512]{1,0:T(8,128)(2,1)S(1)} %collective-permute-done.1.mate_v, ...), custom_call_target="tpu_custom_call" | custom-call | tf_op jit(solution)/shard_map/pallas_call | solution.py:125
  18.9 0.0 collective-permute-done.4.far_k
  19.0 1.6 %collective-permute-start.5 = (bf16[4,2,16,768]{3,2,1,0:T(8,128)(2,1)S(1)}, bf16[4,2,16,768]{3,2,1,0:T(8,128)(2,1)S(1)}, u32[]{:S(2)}, u32[]{:S(2)}) collective-permute-start(bf16[4,2,16,768]{3,2,1,0:T(8,128)(2,1)S(1)} %bitcast.42), channel_id=1, source_target_pairs={{0,4},{2,6},{4,0},{6,2},{8,12},{10,14},{12,8},{14,10},{16,20},{18,... | collective-permute-start | bytes 589832 | tf_op jit(solution)/shard_map/ppermute | solution.py:307
  20.6 6.2 %collective-permute-done.5 = bf16[4,2,16,768]{3,2,1,0:T(8,128)(2,1)S(1)} collective-permute-done((bf16[4,2,16,768]{3,2,1,0:T(8,128)(2,1)S(1)}, bf16[4,2,16,768]{3,2,1,0:T(8,128)(2,1)S(1)}, u32[]{:S(2)}, u32[]{:S(2)}) %collective-permute-start.5) | collective-permute-done | bytes 196640 | tf_op jit(solution)/shard_map/ppermute | solution.py:307
  26.8 0.9 %collective-permute-start.12 = (bf16[512,512]{1,0:T(8,128)(2,1)S(1)}, bf16[512,512]{1,0:T(8,128)(2,1)S(1)}, u32[]{:S(2)}, u32[]{:S(2)}) collective-permute-start(bf16[512,512]{1,0:T(8,128)(2,1)S(1)} %copy-done.3), channel_id=1, source_target_pairs={{2,4},{6,8},{10,12},{14,16},{18,20},{22,24},{26,28},{4,2},{8,6},{1... | collective-permute-start | bytes 1572872 | tf_op jit(solution)/shard_map/ppermute | solution.py:303
  27.8 3.8 %collective-permute-start.6 = (bf16[1,2,16,768]{3,2,1,0:T(8,128)(2,1)S(1)}, bf16[1,2,16,768]{3,2,1,0:T(8,128)(2,1)S(1)}, u32[]{:S(2)}, u32[]{:S(2)}) collective-permute-start(bf16[1,2,16,768]{3,2,1,0:T(8,128)(2,1)S(1)} %get-tuple-element.37), channel_id=1, source_target_pairs={{0,8},{2,10},{4,12},{6,14},{8,0},{10,2},{12,4},{14,6},{16,24},{18,... | collective-permute-start | bytes 147464 | tf_op jit(solution)/shard_map/ppermute | solution.py:307
  31.6 2.6 %collective-permute-start.7 = (bf16[1,2,16,768]{3,2,1,0:T(8,128)(2,1)S(1)}, bf16[1,2,16,768]{3,2,1,0:T(8,128)(2,1)S(1)}, u32[]{:S(2)}, u32[]{:S(2)}) collective-permute-start(bf16[1,2,16,768]{3,2,1,0:T(8,128)(2,1)S(1)} %get-tuple-element.36), channel_id=1, source_target_pairs={{0,16},{2,18},{4,20},{6,22},{8,24},{10,26},{12,28},{14,30},{16,0},... | collective-permute-start | bytes 147464 | tf_op jit(solution)/shard_map/ppermute | solution.py:307
  34.2 0.0 collective-permute-start.8
  34.2 6.3 %collective-permute-done.6 = bf16[1,2,16,768]{3,2,1,0:T(8,128)(2,1)S(1)} collective-permute-done((bf16[1,2,16,768]{3,2,1,0:T(8,128)(2,1)S(1)}, bf16[1,2,16,768]{3,2,1,0:T(8,128)(2,1)S(1)}, u32[]{:S(2)}, u32[]{:S(2)}) %collective-permute-start.6) | collective-permute-done | bytes 49184 | tf_op jit(solution)/shard_map/ppermute | solution.py:307
  40.5 1.6 %collective-permute-done.7 = bf16[1,2,16,768]{3,2,1,0:T(8,128)(2,1)S(1)} collective-permute-done((bf16[1,2,16,768]{3,2,1,0:T(8,128)(2,1)S(1)}, bf16[1,2,16,768]{3,2,1,0:T(8,128)(2,1)S(1)}, u32[]{:S(2)}, u32[]{:S(2)}) %collective-permute-start.7) | collective-permute-done | bytes 49184 | tf_op jit(solution)/shard_map/ppermute | solution.py:307
  42.1 2.1 %collective-permute-done.8 = bf16[1,2,16,768]{3,2,1,0:T(8,128)(2,1)S(1)} collective-permute-done((bf16[1,2,16,768]{3,2,1,0:T(8,128)(2,1)S(1)}, bf16[1,2,16,768]{3,2,1,0:T(8,128)(2,1)S(1)}, u32[]{:S(2)}, u32[]{:S(2)}) %collective-permute-start.8) | collective-permute-done | bytes 49184 | tf_op jit(solution)/shard_map/ppermute | solution.py:307
  44.2 0.7 %shard_map.67 = bf16[2,16,768]{2,1,0:T(8,128)(2,1)S(1)} custom-call(s32[6]{0:T(128)S(1)} %stack.27.spots, bf16[2,16,768]{2,1,0:T(8,128)(2,1)S(1)} %get-tuple-element.38.refs_0_, bf16[2,16,768]{2,1,0:T(8,128)(2,1)S(1)} %bitcast.39, bf16[2,16,768]{2,1,0:T(8,128)(2,1)S(1)} %bitcast.40, bf16[2,16,768]{2,1,0:T(8,128)(2,1)S(1)} %bitcast.41, ...), custom_call_target="tpu_custom_call" | custom-call | tf_op jit(solution)/shard_map/pallas_call | solution.py:152
  44.9 0.1 collective-permute-start.10
  45.0 3.0 %collective-permute-start.11 = (bf16[1,2,16,768]{3,2,1,0:T(8,128)(2,1)S(1)}, bf16[1,2,16,768]{3,2,1,0:T(8,128)(2,1)S(1)}, u32[]{:S(2)}, u32[]{:S(2)}) collective-permute-start(bf16[1,2,16,768]{3,2,1,0:T(8,128)(2,1)S(1)} %bitcast.36), channel_id=1, source_target_pairs={{0,24},{2,26},{4,28},{6,30},{8,16},{10,18},{12,20},{14,22},{16,8},... | collective-permute-start | bytes 147464 | tf_op jit(solution)/shard_map/ppermute | solution.py:307
  48.0 0.5 collective-permute-start.9
  48.5 2.6 %collective-permute-done.10 = bf16[1,2,16,768]{3,2,1,0:T(8,128)(2,1)S(1)} collective-permute-done((bf16[1,2,16,768]{3,2,1,0:T(8,128)(2,1)S(1)}, bf16[1,2,16,768]{3,2,1,0:T(8,128)(2,1)S(1)}, u32[]{:S(2)}, u32[]{:S(2)}) %collective-permute-start.10) | collective-permute-done | bytes 49184 | tf_op jit(solution)/shard_map/ppermute | solution.py:307
  51.0 0.0 collective-permute-done.11
  51.0 1.0 %collective-permute-done.9 = bf16[1,2,16,768]{3,2,1,0:T(8,128)(2,1)S(1)} collective-permute-done((bf16[1,2,16,768]{3,2,1,0:T(8,128)(2,1)S(1)}, bf16[1,2,16,768]{3,2,1,0:T(8,128)(2,1)S(1)}, u32[]{:S(2)}, u32[]{:S(2)}) %collective-permute-start.9) | collective-permute-done | bytes 49184 | tf_op jit(solution)/shard_map/ppermute | solution.py:307
  52.1 0.0 collective-permute-done.12.far_v
  52.1 0.1 collective-permute-start.13
  52.2 4.8 %shard_map.68.attended_ref = f32[512,512]{1,0:T(8,128)S(1)} custom-call(s32[6]{0:T(128)S(1)} %stack.27.spots, s32[32,1]{1,0:T(8,128)S(1)} %copy.9.lengths, bf16[512,512]{1,0:T(8,128)(2,1)S(1)} %copy-done.1, bf16[512,512]{1,0:T(8,128)(2,1)} %collective-permute-done.4.far_k, bf16[512,512]{1,0:T(8,128)(2,1)S(1)} %collective-permute-done.12.far_v, ...), custom_call_target="tpu_custom_call" | custom-call | tf_op jit(solution)/shard_map/pallas_call | solution.py:247
  57.0 0.8 %collective-permute-done.13 = bf16[4,2,16,768]{3,2,1,0:T(8,128)(2,1)S(1)} collective-permute-done((bf16[4,2,16,768]{3,2,1,0:T(8,128)(2,1)S(1)}, bf16[4,2,16,768]{3,2,1,0:T(8,128)(2,1)S(1)}, u32[]{:S(2)}, u32[]{:S(2)}) %collective-permute-start.13) | collective-permute-done | bytes 196640 | tf_op jit(solution)/shard_map/ppermute | solution.py:307
  57.9 0.1 collective-permute-start.14
  57.9 1.7 %collective-permute-done.14.mate_w = bf16[8,2,16,768]{3,2,1,0:T(8,128)(2,1)S(1)} collective-permute-done((bf16[8,2,16,768]{3,2,1,0:T(8,128)(2,1)S(1)}, bf16[8,2,16,768]{3,2,1,0:T(8,128)(2,1)S(1)}, u32[]{:S(2)}, u32[]{:S(2)}) %collective-permute-start.14) | collective-permute-done | bytes 393248 | tf_op jit(solution)/shard_map/ppermute | solution.py:298
  59.6 2.0 %shard_map.69 = bf16[512,512]{1,0:T(8,128)(2,1)} custom-call(bf16[512,512]{1,0:T(8,128)(2,1)S(1)} %copy-done.1, bf16[8,2,16,768]{3,2,1,0:T(8,128)(2,1)S(1)} %constant_dynamic-update-slice_fusion.own_w, bf16[8,2,16,768]{3,2,1,0:T(8,128)(2,1)S(1)} %collective-permute-done.14.mate_w, f32[512,512]{1,0:T(8,128)S(1)} %shard_map.68.attended_ref), custom_call_target="tpu_custom_call" | custom-call | tf_op jit(solution)/shard_map/pallas_call | solution.py:272
  (11 shorter events, 0.2 us)
Async XLA Ops:
  0.0 4.9 %copy-start = (f32[4,512]{1,0:T(4,128)S(1)}, f32[4,512]{1,0:T(4,128)}, u32[]{:S(2)}) copy-start(f32[4,512]{1,0:T(4,128)} %param.9) | copy-start | bytes 24580
  0.0 11.0 %copy-start.2 = (bf16[512,512]{1,0:T(8,128)(2,1)S(1)}, bf16[512,512]{1,0:T(8,128)(2,1)}, u32[]{:S(2)}) copy-start(bf16[512,512]{1,0:T(8,128)(2,1)} %own_k.3) | copy-start | bytes 1572868
  0.0 11.1 %copy-start.3 = (bf16[512,512]{1,0:T(8,128)(2,1)S(1)}, bf16[512,512]{1,0:T(8,128)(2,1)}, u32[]{:S(2)}) copy-start(bf16[512,512]{1,0:T(8,128)(2,1)} %own_v.3) | copy-start | bytes 1572868
  0.0 11.1 %copy-start.1 = (bf16[512,512]{1,0:T(8,128)(2,1)S(1)}, bf16[512,512]{1,0:T(8,128)(2,1)}, u32[]{:S(2)}) copy-start(bf16[512,512]{1,0:T(8,128)(2,1)} %q_ref.5) | copy-start | bytes 1572868
  0.0 11.0 %collective-permute-start = (bf16[512,512]{1,0:T(8,128)(2,1)}, bf16[512,512]{1,0:T(8,128)(2,1)S(1)}, u32[]{:S(2)}, u32[]{:S(2)}) collective-permute-start(bf16[512,512]{1,0:T(8,128)(2,1)} %own_k.3), channel_id=1, source_target_pairs={{0,2},{2,0},{4,6},{6,4},{8,10},{10,8},{12,14},{14,12},{16,18},{18,... | collective-permute-start | bytes 1572872 | tf_op jit(solution)/shard_map/ppermute | solution.py:298
  0.5 10.5 %collective-permute-start.1 = (bf16[512,512]{1,0:T(8,128)(2,1)}, bf16[512,512]{1,0:T(8,128)(2,1)S(1)}, u32[]{:S(2)}, u32[]{:S(2)}) collective-permute-start(bf16[512,512]{1,0:T(8,128)(2,1)} %own_v.3), channel_id=1, source_target_pairs={{0,2},{2,0},{4,6},{6,4},{8,10},{10,8},{12,14},{14,12},{16,18},{18,... | collective-permute-start | bytes 1572872 | tf_op jit(solution)/shard_map/ppermute | solution.py:298
  0.6 18.3 %collective-permute-start.4 = (bf16[512,512]{1,0:T(8,128)(2,1)}, bf16[512,512]{1,0:T(8,128)(2,1)}, u32[]{:S(2)}, u32[]{:S(2)}) collective-permute-start(bf16[512,512]{1,0:T(8,128)(2,1)} %own_k.3), channel_id=1, source_target_pairs={{2,4},{6,8},{10,12},{14,16},{18,20},{22,24},{26,28},{4,2},{8,6},{1... | collective-permute-start | bytes 1572872 | tf_op jit(solution)/shard_map/ppermute | solution.py:303
  2.2 1.4 %copy-start.4 = (f32[4,128,768]{2,1,0:T(8,128)S(1)}, f32[4,128,768]{2,1,0:T(8,128)}, u32[]{:S(2)}) copy-start(f32[4,128,768]{2,1,0:T(8,128)} %weights_ref.1) | copy-start | bytes 4718596
  3.6 7.4 %copy-start.5 = (s32[32]{0:T(128)S(1)}, s32[32]{0:T(128)}, u32[]{:S(2)}) copy-start(s32[32]{0:T(128)} %param.11) | copy-start | bytes 388
  4.2 11.8 %collective-permute-start.3 = (bf16[2,144,768]{2,1,0:T(8,128)(2,1)S(1)}, bf16[2,144,768]{2,1,0:T(8,128)(2,1)S(1)}, u32[]{:S(2)}, u32[]{:S(2)}) collective-permute-start(bf16[2,144,768]{2,1,0:T(8,128)(2,1)S(1)} %shard_map.64.local_w.refs_4_), channel_id=1, source_target_pairs={{2,3},{3,2},{6,7},{7,6},{10,11},{11,10},{14,15},{15,14},{18,19},{1... | collective-permute-start | bytes 1327112 | tf_op jit(solution)/shard_map/ppermute | solution.py:315
  4.9 11.0 %collective-permute-start.2 = (f32[8,512]{1,0:T(8,128)S(1)}, f32[8,512]{1,0:T(8,128)}, u32[]{:S(2)}, u32[]{:S(2)}) collective-permute-start(f32[8,512]{1,0:T(8,128)S(1)} %pad.4.own_rate), channel_id=1, source_target_pairs={{0,2},{2,0},{4,6},{6,4},{8,10},{10,8},{12,14},{14,12},{16,18},{18,... | collective-permute-start | bytes 49160 | tf_op jit(solution)/shard_map/ppermute | solution.py:298
  19.0 7.8 %collective-permute-start.5 = (bf16[4,2,16,768]{3,2,1,0:T(8,128)(2,1)S(1)}, bf16[4,2,16,768]{3,2,1,0:T(8,128)(2,1)S(1)}, u32[]{:S(2)}, u32[]{:S(2)}) collective-permute-start(bf16[4,2,16,768]{3,2,1,0:T(8,128)(2,1)S(1)} %bitcast.42), channel_id=1, source_target_pairs={{0,4},{2,6},{4,0},{6,2},{8,12},{10,14},{12,8},{14,10},{16,20},{18,... | collective-permute-start | bytes 589832 | tf_op jit(solution)/shard_map/ppermute | solution.py:307
  26.8 25.3 %collective-permute-start.12 = (bf16[512,512]{1,0:T(8,128)(2,1)S(1)}, bf16[512,512]{1,0:T(8,128)(2,1)S(1)}, u32[]{:S(2)}, u32[]{:S(2)}) collective-permute-start(bf16[512,512]{1,0:T(8,128)(2,1)S(1)} %copy-done.3), channel_id=1, source_target_pairs={{2,4},{6,8},{10,12},{14,16},{18,20},{22,24},{26,28},{4,2},{8,6},{1... | collective-permute-start | bytes 1572872 | tf_op jit(solution)/shard_map/ppermute | solution.py:303
  27.8 12.7 %collective-permute-start.6 = (bf16[1,2,16,768]{3,2,1,0:T(8,128)(2,1)S(1)}, bf16[1,2,16,768]{3,2,1,0:T(8,128)(2,1)S(1)}, u32[]{:S(2)}, u32[]{:S(2)}) collective-permute-start(bf16[1,2,16,768]{3,2,1,0:T(8,128)(2,1)S(1)} %get-tuple-element.37), channel_id=1, source_target_pairs={{0,8},{2,10},{4,12},{6,14},{8,0},{10,2},{12,4},{14,6},{16,24},{18,... | collective-permute-start | bytes 147464 | tf_op jit(solution)/shard_map/ppermute | solution.py:307
  31.6 10.5 %collective-permute-start.7 = (bf16[1,2,16,768]{3,2,1,0:T(8,128)(2,1)S(1)}, bf16[1,2,16,768]{3,2,1,0:T(8,128)(2,1)S(1)}, u32[]{:S(2)}, u32[]{:S(2)}) collective-permute-start(bf16[1,2,16,768]{3,2,1,0:T(8,128)(2,1)S(1)} %get-tuple-element.36), channel_id=1, source_target_pairs={{0,16},{2,18},{4,20},{6,22},{8,24},{10,26},{12,28},{14,30},{16,0},... | collective-permute-start | bytes 147464 | tf_op jit(solution)/shard_map/ppermute | solution.py:307
  34.2 10.0 %collective-permute-start.8 = (bf16[1,2,16,768]{3,2,1,0:T(8,128)(2,1)S(1)}, bf16[1,2,16,768]{3,2,1,0:T(8,128)(2,1)S(1)}, u32[]{:S(2)}, u32[]{:S(2)}) collective-permute-start(bf16[1,2,16,768]{3,2,1,0:T(8,128)(2,1)S(1)} %get-tuple-element.35), channel_id=1, source_target_pairs={{0,24},{2,26},{4,28},{6,30},{8,16},{10,18},{12,20},{14,22},{16,8},... | collective-permute-start | bytes 147464 | tf_op jit(solution)/shard_map/ppermute | solution.py:307
  44.9 6.1 %collective-permute-start.10 = (bf16[1,2,16,768]{3,2,1,0:T(8,128)(2,1)S(1)}, bf16[1,2,16,768]{3,2,1,0:T(8,128)(2,1)S(1)}, u32[]{:S(2)}, u32[]{:S(2)}) collective-permute-start(bf16[1,2,16,768]{3,2,1,0:T(8,128)(2,1)S(1)} %bitcast.35), channel_id=1, source_target_pairs={{0,16},{2,18},{4,20},{6,22},{8,24},{10,26},{12,28},{14,30},{16,0},... | collective-permute-start | bytes 147464 | tf_op jit(solution)/shard_map/ppermute | solution.py:307
  45.0 6.0 %collective-permute-start.11 = (bf16[1,2,16,768]{3,2,1,0:T(8,128)(2,1)S(1)}, bf16[1,2,16,768]{3,2,1,0:T(8,128)(2,1)S(1)}, u32[]{:S(2)}, u32[]{:S(2)}) collective-permute-start(bf16[1,2,16,768]{3,2,1,0:T(8,128)(2,1)S(1)} %bitcast.36), channel_id=1, source_target_pairs={{0,24},{2,26},{4,28},{6,30},{8,16},{10,18},{12,20},{14,22},{16,8},... | collective-permute-start | bytes 147464 | tf_op jit(solution)/shard_map/ppermute | solution.py:307
  48.0 4.1 %collective-permute-start.9 = (bf16[1,2,16,768]{3,2,1,0:T(8,128)(2,1)S(1)}, bf16[1,2,16,768]{3,2,1,0:T(8,128)(2,1)S(1)}, u32[]{:S(2)}, u32[]{:S(2)}) collective-permute-start(bf16[1,2,16,768]{3,2,1,0:T(8,128)(2,1)S(1)} %bitcast.37), channel_id=1, source_target_pairs={{0,8},{2,10},{4,12},{6,14},{8,0},{10,2},{12,4},{14,6},{16,24},{18,... | collective-permute-start | bytes 147464 | tf_op jit(solution)/shard_map/ppermute | solution.py:307
  52.1 5.7 %collective-permute-start.13 = (bf16[4,2,16,768]{3,2,1,0:T(8,128)(2,1)S(1)}, bf16[4,2,16,768]{3,2,1,0:T(8,128)(2,1)S(1)}, u32[]{:S(2)}, u32[]{:S(2)}) collective-permute-start(bf16[4,2,16,768]{3,2,1,0:T(8,128)(2,1)S(1)} %pad_maximum_fusion), channel_id=1, source_target_pairs={{0,4},{2,6},{4,0},{6,2},{8,12},{10,14},{12,8},{14,10},{16,20},{18,... | collective-permute-start | bytes 589832 | tf_op jit(solution)/shard_map/ppermute | solution.py:307
  57.9 1.8 %collective-permute-start.14 = (bf16[8,2,16,768]{3,2,1,0:T(8,128)(2,1)S(1)}, bf16[8,2,16,768]{3,2,1,0:T(8,128)(2,1)S(1)}, u32[]{:S(2)}, u32[]{:S(2)}) collective-permute-start(bf16[8,2,16,768]{3,2,1,0:T(8,128)(2,1)S(1)} %constant_dynamic-update-slice_fusion.own_w), channel_id=1, source_target_pairs={{0,2},{2,0},{4,6},{6,4},{8,10},{10,8},{12,14},{14,12},{16,18},{18,... | collective-permute-start | bytes 1179656 | tf_op jit(solution)/shard_map/ppermute | solution.py:298

commit v3 on v2

--- a/solution.py
+++ b/solution.py
@@ -53,49 +53,14 @@
     return digits[::-1]
 
 
-def pick_kernel(chips, spots, weights_ref, picked_ref):
-    base, chip = spots[0], spots[1]
-    memories, hidden = picked_ref.shape[0], weights_ref.shape[1]
-    rows = hidden // chips
-    for memory in range(memories):
-        for block in range(chips):
-            start = pl.multiple_of((chip ^ block) * rows, rows)
-            part = weights_ref[base + memory, pl.ds(start, rows), :]
-            rounded = part.astype(BF16)
-            picked_ref[memory, pl.ds(block * rows, rows), :] = rounded
-            if block == 0:
-                rest = part - rounded.astype(F32)
-                picked_ref[memory, pl.ds(hidden, rows), :] = rest.astype(BF16)
-
-
-def pick_weights(spots, weights, memories, chips):
-    hidden = weights.shape[1]
-    rows = hidden // chips
-    if rows % 16:
-        part = lax.dynamic_slice_in_dim(weights, spots[0], memories, 0)
-        part = part.reshape(memories, chips, rows, 3 * DM)
-        part = jnp.take(part, jnp.arange(chips, dtype=jnp.int32) ^ spots[1], axis=1)
-        rounded = part.astype(BF16)
-        rest = (part[:, :1] - rounded[:, :1].astype(F32)).astype(BF16)
-        picked = jnp.concatenate([rounded, rest], axis=1)
-        return picked.reshape(memories, hidden + rows, 3 * DM)
-    return pl.pallas_call(
-        functools.partial(pick_kernel, chips),
-        out_shape=jax.ShapeDtypeStruct((memories, hidden + rows, 3 * DM), BF16),
-        in_specs=[in_smem()] + in_vmem(1),
-        out_specs=in_vmem(1)[0],
-        compiler_params=params(),
-    )(spots, weights)
-
-
 def grads_kernel(
     spots, own_k, own_v, mate_k, mate_v, own_rate, mate_rate, local_w, sent_w, grad_ref
 ):
-    core = spots[2]
-    memories, hidden, _ = grad_ref.shape
+    chip, core = spots[1], spots[2]
+    memories, hidden, _ = local_w.shape
     for memory in range(memories):
         features = pl.ds(memory * DM, DM)
-        weights = jnp.where(core == 0, local_w[memory, :hidden], sent_w[memory, :hidden])
+        weights = jnp.where(core == 0, local_w[memory], sent_w[memory])
         gate_up_w = jnp.concatenate([weights[:, :DM], weights[:, DM : 2 * DM]], axis=0)
         out_w = weights[:, 2 * DM :]
         grad_pair = jnp.zeros((2 * hidden, DM), F32)
@@ -115,20 +80,35 @@
             )
             grad_pair += dot_tn(pair, key)
             grad_out -= dot_tn((swish * up).astype(BF16), scaled)
-        grad_ref[memory, :, :DM] = grad_pair[:hidden].astype(BF16)
-        grad_ref[memory, :, DM : 2 * DM] = grad_pair[hidden:].astype(BF16)
-        grad_ref[memory, :, 2 * DM :] = grad_out.astype(BF16)
-
-
-def half_grads(spots, hidden, own_k, own_v, mate_k, mate_v, own_rate, mate_rate, local_w, sent_w):
-    shape = (local_w.shape[0], hidden, local_w.shape[2])
-    return pl.pallas_call(
+        found = (grad_pair[:hidden], grad_pair[hidden:], grad_out)
+        for part, grad in enumerate(found):
+            grad = grad.astype(BF16)
+            columns = pl.ds(part * DM, DM)
+            if grad_ref.ndim == 3:
+                grad_ref[memory, :, columns] = grad
+            else:
+                chips, _, rows, _ = grad_ref.shape
+                for block in range(chips):
+                    piece = grad[block * rows : (block + 1) * rows]
+                    grad_ref[chip ^ block, memory, :, columns] = piece
+
+
+def half_grads(spots, chips, own_k, own_v, mate_k, mate_v, own_rate, mate_rate, local_w, sent_w):
+    memories, hidden, width = local_w.shape
+    rows = hidden // chips
+    placed = rows % 16 == 0
+    shape = (chips, memories, rows, width) if placed else local_w.shape
+    grads = pl.pallas_call(
         grads_kernel,
         out_shape=jax.ShapeDtypeStruct(shape, BF16),
         in_specs=[in_smem()] + in_vmem(8),
         out_specs=in_vmem(1)[0],
         compiler_params=params(),
     )(spots, own_k, own_v, mate_k, mate_v, own_rate, mate_rate, local_w, sent_w)
+    if placed:
+        return grads
+    grads = grads.reshape(memories, chips, rows, width).transpose(1, 0, 2, 3)
+    return jnp.take(grads, jnp.arange(chips, dtype=jnp.int32) ^ spots[1], axis=0)
 
 
 def update_kernel(step_rate, parts, spots, *refs):
@@ -136,9 +116,7 @@
     total = grads[0][...].astype(F32)
     for part in grads[1:]:
         total += part[...].astype(F32)
-    rows = new_ref.shape[1]
-    picked = jnp.where(spots[2] == 0, local_w[...], sent_w[...]).astype(F32)
-    before = picked[:, :rows] + picked[:, -rows:]
+    before = jnp.where(spots[2] == 0, local_w[...], sent_w[...])
     stepped = before - total * step_rate
     for block in range(3):
         columns = slice(block * DM, (block + 1) * DM)
@@ -316,9 +294,10 @@
 
     hidden = fast_weights.shape[1]
     rows = hidden // chips
-    local_w = pick_weights(spots, fast_weights, memories, chips)
+    local_w = lax.dynamic_slice_in_dim(fast_weights, source, memories, 0).astype(BF16)
     sent_w = to_plane(local_w)
-    far_k = to_far(keys)
+    keys, values, local_w = lax.optimization_barrier((keys, values, local_w))
+    far_k, far_v = to_far(keys), to_far(values)
     mate_k, mate_v = to_core(keys), to_core(values)
     rates = lax.dynamic_slice_in_dim(step_sizes, plane * memories, memories, 0)
     rates = jnp.pad(rates, ((0, -memories % 8), (0, 0)))
@@ -326,34 +305,34 @@
     lengths = view_lengths.reshape(-1, 1)
 
     near = attend_near(spots, lengths, queries, keys, values, mate_k, mate_v)
+    near, sent_w = lax.optimization_barrier((near, sent_w))
     grads = half_grads(
-        spots, hidden, keys, values, mate_k, mate_v, rates, mate_rates, local_w, sent_w
-    )
-    grads, far_k, near = lax.optimization_barrier((grads, far_k, near))
-    held = grads.reshape(memories, chips, rows, 3 * DM).transpose(1, 0, 2, 3)
-    far_v = None
-    stride = 1
+        spots, chips, keys, values, mate_k, mate_v, rates, mate_rates, local_w, sent_w
+    )
+    local_rows = lax.dynamic_slice(
+        fast_weights, (source, chip * rows, 0), (memories, rows, 3 * DM)
+    )
+    held, local_rows = lax.optimization_barrier((grads, local_rows))
+    sent_rows = to_plane(local_rows)
+    stride = chips
+    for radix in digits[::-1]:
+        stride //= radix
+        if stride == 1:
+            held, far_k, far_v = lax.optimization_barrier((held, far_k, far_v))
+        held = held.reshape((radix, stride) + held.shape[1:])
+        came = [to_chip(held[step], step * stride) for step in range(1, radix)]
+        if stride > 1:
+            held = sum([part.astype(F32) for part in came], held[0].astype(F32)).astype(BF16)
+    parts = [part[0] for part in [held[0]] + came]
+    all_tokens = tokens * devices
+    fresh = update_rows(spots, 1.0 / math.sqrt(all_tokens), parts, local_rows, sent_rows)
+
+    gathered = fresh[None]
     for place, radix in enumerate(digits):
-        held = held.reshape((held.shape[0] // radix, radix) + held.shape[1:])
-        kept = held[:, 0]
-        came = [to_chip(held[:, step], step * stride) for step in range(1, radix)]
-        if far_v is None:
-            came, far_v = lax.optimization_barrier((came, values))
-            far_v = to_far(far_v)
+        came = [to_chip(gathered, step * stride) for step in range(1, radix)]
         stride *= radix
-        if place < len(digits) - 1:
-            held = sum([part.astype(F32) for part in came], kept.astype(F32)).astype(BF16)
-    parts = [part.reshape(memories, rows, 3 * DM) for part in [kept] + came]
-    all_tokens = tokens * devices
-    fresh = update_rows(spots, 1.0 / math.sqrt(all_tokens), parts, local_w, sent_w)
-
-    gathered = fresh[None]
-    for place, radix in enumerate(digits[::-1]):
-        stride //= radix
         if place == len(digits) - 1:
-            gathered, far_v = lax.optimization_barrier((gathered, far_v))
-        came = [to_chip(gathered, step * stride) for step in range(1, radix)]
-        if place == len(digits) - 1:
+            near, gathered = lax.optimization_barrier((near, gathered))
             attended = attend_far(spots, lengths, queries, far_k, far_v, near)
             came, attended = lax.optimization_barrier((came, attended))
         gathered = jnp.concatenate([gathered] + came, axis=0)

time: 62 us -> 63.9 us (1.031)
  local copies, waits for them, and re-layouts: 1.7 us -> 8.66 us
  waiting for transfers between devices: 22.4 us -> 15.7 us
  starting transfers between devices: 21.4 us -> 23.7 us
  Pallas kernels: 15.9 us -> 15.2 us
    ppermute x8, waiting for transfers between devices: 20.6 us -> 13.9 us  [to_chip(): return lax.ppermute(x, 'tok', pairs)]
    unnamed x14 -> x17, local copies, waits for them, and re-layouts: 1.46 us -> 5.23 us
    ppermute x8, starting transfers between devices: 11.7 us -> 14.9 us  [to_chip(): return lax.ppermute(x, 'tok', pairs)]
    ppermute x4, starting transfers between devices: 6.71 us -> 5.16 us  [to_core(): return lax.ppermute(x, 'tok', [(i, i ^ 1) for i in range(devices)])]
    ppermute x1 -> x2, starting transfers between devices: 0.69 us -> 2.23 us  [to_plane(): return lax.ppermute(x, ('tok', 'mem'), pairs)]
    ppermute x2, starting transfers between devices: 2.32 us -> 1.37 us  [to_far(): return lax.ppermute(x, 'tok', pairs)]
    dynamic_slice x1, local copies, waits for them, and re-layouts: 0.01 us -> 0.71 us  [on_device(): rates = lax.dynamic_slice_in_dim(step_sizes, plane * memories, memories, 0)]
    reshape x1, local copies, waits for them, and re-layouts: 0.09 us -> 0.74 us  [on_device(): lengths = view_lengths.reshape(-1, 1)]
  transfers between devices with their start and end apart: 15 -> 16, of which waited for: 8 -> 6; matrix products, arithmetic and copies ran while one was open for 0% -> 5% of each run, Pallas kernels for 23% -> 20%
where the time goes in v3:
time: 63.9 us; the launch traced here: 63.4 us
  starting transfers between devices  23.7 us (37%)
  waiting for transfers between devices  15.7 us (25%)
  Pallas kernels  15.2 us (24%)
  local copies, waits for them, and re-layouts  8.66 us (14%)
    ppermute x8, starting transfers between devices, to_chip(): return lax.ppermute(x, 'tok', pairs)  14.9 us
    ppermute x8, waiting for transfers between devices, to_chip(): return lax.ppermute(x, 'tok', pairs)  13.9 us
    unnamed x17, local copies, waits for them, and re-layouts  5.23 us
    ppermute x4, starting transfers between devices, to_core(): return lax.ppermute(x, 'tok', [(i, i ^ 1) for i in range(devices)])  5.16 us
    pallas_call x1, Pallas kernels, attend_near(): pl.pallas_call(near_kernel, out_shape=(jax.ShapeDtypeStruct(queries.shape...  4.93 us
    pallas_call x1, Pallas kernels, attend_far(): pl.pallas_call(far_kernel, out_shape=jax.ShapeDtypeStruct(queries.shape,...  4.25 us
    pallas_call x1, Pallas kernels, half_grads(): pl.pallas_call(grads_kernel, out_shape=jax.ShapeDtypeStruct(shape, BF16),...  3.29 us
    ppermute x2, starting transfers between devices, to_plane(): return lax.ppermute(x, ('tok', 'mem'), pairs)  2.23 us
  transfers between devices with their start and end apart: 16, of which 6 were waited for; matrix products, arithmetic and copies ran while one was open for 5% of the time, Pallas kernels for 20%

profile of v3, /device:TPU:0, one launch (start us, length us, event | category | flops | bytes accessed | tf_op | source)
XLA Modules:
  0.0 63.4 jit_solution(13181360204416343210)
XLA Ops:
  0.0 1.4 %copy-done = f32[4,128,768]{2,1,0:T(8,128)S(1)} copy-done((f32[4,128,768]{2,1,0:T(8,128)S(1)}, f32[4,128,768]{2,1,0:T(8,128)}, u32[]{:S(2)}) %copy-start) | copy-done | bytes 1572888
  1.5 0.5 collective-permute-start
  2.0 0.1 collective-permute-start.1
  2.1 1.4 %collective-permute-start.2 = (bf16[2,128,768]{2,1,0:T(8,128)(2,1)S(1)}, bf16[2,128,768]{2,1,0:T(8,128)(2,1)}, u32[]{:S(2)}, u32[]{:S(2)}) collective-permute-start(bf16[2,128,768]{2,1,0:T(8,128)(2,1)S(1)} %dynamic-slice_convert_fusion.local_w), channel_id=1, source_target_pairs={{2,3},{3,2},{6,7},{7,6},{10,11},{11,10},{14,15},{15,14},{18,19},{1... | collective-permute-start | bytes 1179656 | tf_op jit(solution)/shard_map/ppermute | solution.py:293
  3.4 0.7 %collective-permute-start.7 = (bf16[512,512]{1,0:T(8,128)(2,1)}, bf16[512,512]{1,0:T(8,128)(2,1)S(1)}, u32[]{:S(2)}, u32[]{:S(2)}) collective-permute-start(bf16[512,512]{1,0:T(8,128)(2,1)} %own_k.1), channel_id=1, source_target_pairs={{2,4},{6,8},{10,12},{14,16},{18,20},{22,24},{26,28},{4,2},{8,6},{1... | collective-permute-start | bytes 1572872 | tf_op jit(solution)/shard_map/ppermute | solution.py:281
  4.1 0.7 %constant_dynamic-slice_fusion.1 = f32[2,512]{1,0:T(2,128)S(1)} fusion(f32[4,512]{1,0:T(4,128)} %param.9, s32[]{:T(128)S(6)} %select_n.32), kind=kLoop, calls=%fused_computation.9 | loop fusion | bytes 8196 | tf_op jit(solution)/shard_map/dynamic_slice | solution.py:302
  4.8 0.6 pad.4.own_rate
  5.5 4.5 %collective-permute-start.3 = (f32[8,512]{1,0:T(8,128)}, f32[8,512]{1,0:T(8,128)}, u32[]{:S(2)}, u32[]{:S(2)}) collective-permute-start(f32[8,512]{1,0:T(8,128)} %pad.4.own_rate), channel_id=1, source_target_pairs={{0,2},{2,0},{4,6},{6,4},{8,10},{10,8},{12,14},{14,12},{16,18},{18,... | collective-permute-start | bytes 49160 | tf_op jit(solution)/shard_map/ppermute | solution.py:276
  9.9 0.6 %constant_dynamic-slice_fusion.refs_2_ = f32[2,16,768]{2,1,0:T(8,128)} fusion(f32[4,128,768]{2,1,0:T(8,128)S(1)} %copy-done, s32[]{:T(128)S(6)} %select_n.31, s32[]{:T(128)S(6)} %select_n.33), kind=kLoop, calls=%fused_computation.8 | loop fusion | bytes 196616 | tf_op jit(solution)/shard_map/dynamic_slice | solution.py:312
  10.6 0.7 %copy.7.lengths = s32[32,1]{1,0:T(8,128)S(1)} copy(s32[32,1]{0,1:T(1,128)} %bitcast.14) | data formatting | bytes 256 | tf_op jit(solution)/shard_map/reshape | solution.py:305
  11.3 0.7 %stack.27.spots = s32[6]{0:T(128)} concatenate(s32[1]{0:T(128)} %bitcast, s32[1]{0:T(128)} %bitcast.1, s32[1]{0:T(128)} %bitcast.2, s32[1]{0:T(128)} %bitcast.3, s32[1]{0:T(128)} %bitcast.4, s32[1]{0:T(128)} %bitcast.5), dimensions={0} | concatenate | bytes 48 | tf_op jit(solution)/shard_map/stack | solution.py:271
  12.0 0.0 collective-permute-done.mate_k
  12.0 0.7 %collective-permute-start.8 = (bf16[512,512]{1,0:T(8,128)(2,1)}, bf16[512,512]{1,0:T(8,128)(2,1)S(1)}, u32[]{:S(2)}, u32[]{:S(2)}) collective-permute-start(bf16[512,512]{1,0:T(8,128)(2,1)} %own_v.1), channel_id=1, source_target_pairs={{2,4},{6,8},{10,12},{14,16},{18,20},{22,24},{26,28},{4,2},{8,6},{1... | collective-permute-start | bytes 1572872 | tf_op jit(solution)/shard_map/ppermute | solution.py:281
  12.7 0.0 collective-permute-done.1.mate_v
  12.7 0.0 copy-start.1
  12.7 1.0 %copy-done.1 = bf16[512,512]{1,0:T(8,128)(2,1)S(1)} copy-done((bf16[512,512]{1,0:T(8,128)(2,1)S(1)}, bf16[512,512]{1,0:T(8,128)(2,1)}, u32[]{:S(2)}) %copy-start.1) | copy-done | bytes 524312
  13.7 1.0 %copy-done.3 = bf16[512,512]{1,0:T(8,128)(2,1)S(1)} copy-done((bf16[512,512]{1,0:T(8,128)(2,1)S(1)}, bf16[512,512]{1,0:T(8,128)(2,1)}, u32[]{:S(2)}) %copy-start.3) | copy-done | bytes 524312
  14.8 1.0 %copy-done.4 = bf16[512,512]{1,0:T(8,128)(2,1)S(1)} copy-done((bf16[512,512]{1,0:T(8,128)(2,1)S(1)}, bf16[512,512]{1,0:T(8,128)(2,1)}, u32[]{:S(2)}) %copy-start.4) | copy-done | bytes 524312
  15.8 0.7 %copy-done.6 = s32[6]{0:T(128)S(1)} copy-done((s32[6]{0:T(128)S(1)}, s32[6]{0:T(128)}, u32[]{:S(2)}) %copy-start.6) | copy-done | bytes 48
  16.5 4.9 %shard_map.64 = (f32[512,512]{1,0:T(8,128)S(1)}, f32[512,4]{1,0:T(8,128)S(1)}, f32[512,4]{1,0:T(8,128)S(1)}) custom-call(s32[6]{0:T(128)S(1)} %copy-done.6, s32[32,1]{1,0:T(8,128)S(1)} %copy.7.lengths, bf16[512,512]{1,0:T(8,128)(2,1)S(1)} %copy-done.1, bf16[512,512]{1,0:T(8,128)(2,1)S(1)} %copy-done.3, bf16[512,512]{1,0:T(8,128)(2,1)S(1)} %copy-done.4, ...), custom_call_target="tpu_custom_call" | custom-call | tf_op jit(solution)/shard_map/pallas_call | solution.py:215
  21.4 0.0 collective-permute-done.2.sent_w
  21.4 0.0 copy-start.5
  21.4 0.0 collective-permute-done.3.mate_rate
  21.5 3.3 %shard_map.65 = bf16[8,2,16,768]{3,2,1,0:T(8,128)(2,1)S(1)} custom-call(s32[6]{0:T(128)S(1)} %copy-done.6, bf16[512,512]{1,0:T(8,128)(2,1)S(1)} %copy-done.3, bf16[512,512]{1,0:T(8,128)(2,1)S(1)} %copy-done.4, bf16[512,512]{1,0:T(8,128)(2,1)S(1)} %collective-permute-done.mate_k, bf16[512,512]{1,0:T(8,128)(2,1)S(1)} %collective-permute-done.1.mate_v, ...), custom_call_target="tpu_custom_call" | custom-call | tf_op jit(solution)/shard_map/pallas_call | solution.py:101
  24.8 0.0 copy-start.2
  24.8 4.5 %collective-permute-start.4 = (bf16[2,2,16,768]{3,2,1,0:T(8,128)(2,1)S(1)}, bf16[2,2,16,768]{3,2,1,0:T(8,128)(2,1)S(1)}, u32[]{:S(2)}, u32[]{:S(2)}) collective-permute-start(bf16[2,2,16,768]{3,2,1,0:T(8,128)(2,1)S(1)} %get-tuple-element.51), channel_id=1, source_target_pairs={{0,8},{2,10},{4,12},{6,14},{8,0},{10,2},{12,4},{14,6},{16,24},{18,... | collective-permute-start | bytes 294920 | tf_op jit(solution)/shard_map/ppermute | solution.py:285
  29.3 2.6 %collective-permute-start.5 = (bf16[2,2,16,768]{3,2,1,0:T(8,128)(2,1)S(1)}, bf16[2,2,16,768]{3,2,1,0:T(8,128)(2,1)S(1)}, u32[]{:S(2)}, u32[]{:S(2)}) collective-permute-start(bf16[2,2,16,768]{3,2,1,0:T(8,128)(2,1)S(1)} %get-tuple-element.53), channel_id=1, source_target_pairs={{0,16},{2,18},{4,20},{6,22},{8,24},{10,26},{12,28},{14,30},{16,0},... | collective-permute-start | bytes 294920 | tf_op jit(solution)/shard_map/ppermute | solution.py:285
  31.9 0.0 collective-permute-start.6
  31.9 0.7 %collective-permute-done.4 = bf16[2,2,16,768]{3,2,1,0:T(8,128)(2,1)S(1)} collective-permute-done((bf16[2,2,16,768]{3,2,1,0:T(8,128)(2,1)S(1)}, bf16[2,2,16,768]{3,2,1,0:T(8,128)(2,1)S(1)}, u32[]{:S(2)}, u32[]{:S(2)}) %collective-permute-start.4) | collective-permute-done | bytes 98336 | tf_op jit(solution)/shard_map/ppermute | solution.py:285
  32.5 0.8 %collective-permute-start.10 = (f32[2,16,768]{2,1,0:T(8,128)S(1)}, f32[2,16,768]{2,1,0:T(8,128)S(1)}, u32[]{:S(2)}, u32[]{:S(2)}) collective-permute-start(f32[2,16,768]{2,1,0:T(8,128)S(1)} %copy-done.5), channel_id=1, source_target_pairs={{2,3},{3,2},{6,7},{7,6},{10,11},{11,10},{14,15},{15,14},{18,19},{1... | collective-permute-start | bytes 294920 | tf_op jit(solution)/shard_map/ppermute | solution.py:293
  33.4 6.6 %collective-permute-done.5 = bf16[2,2,16,768]{3,2,1,0:T(8,128)(2,1)S(1)} collective-permute-done((bf16[2,2,16,768]{3,2,1,0:T(8,128)(2,1)S(1)}, bf16[2,2,16,768]{3,2,1,0:T(8,128)(2,1)S(1)}, u32[]{:S(2)}, u32[]{:S(2)}) %collective-permute-start.5) | collective-permute-done | bytes 98336 | tf_op jit(solution)/shard_map/ppermute | solution.py:285
  40.0 0.0 collective-permute-done.6
  40.0 0.1 add_convert_fusion
  40.0 0.0 collective-permute-done.7.far_k
  40.1 1.7 %collective-permute-start.9 = (bf16[1,2,16,768]{3,2,1,0:T(8,128)(2,1)S(1)}, bf16[1,2,16,768]{3,2,1,0:T(8,128)(2,1)S(1)}, u32[]{:S(2)}, u32[]{:S(2)}) collective-permute-start(bf16[1,2,16,768]{3,2,1,0:T(8,128)(2,1)S(1)} %get-tuple-element.54), channel_id=1, source_target_pairs={{0,4},{2,6},{4,0},{6,2},{8,12},{10,14},{12,8},{14,10},{16,20},{18,... | collective-permute-start | bytes 147464 | tf_op jit(solution)/shard_map/ppermute | solution.py:285
  41.7 2.5 %collective-permute-done.9 = bf16[1,2,16,768]{3,2,1,0:T(8,128)(2,1)S(1)} collective-permute-done((bf16[1,2,16,768]{3,2,1,0:T(8,128)(2,1)S(1)}, bf16[1,2,16,768]{3,2,1,0:T(8,128)(2,1)S(1)}, u32[]{:S(2)}, u32[]{:S(2)}) %collective-permute-start.9) | collective-permute-done | bytes 49184 | tf_op jit(solution)/shard_map/ppermute | solution.py:285
  44.2 0.7 %shard_map.66 = bf16[2,16,768]{2,1,0:T(8,128)(2,1)S(1)} custom-call(s32[6]{0:T(128)S(1)} %copy-done.6, bf16[2,16,768]{2,1,0:T(8,128)(2,1)S(1)} %get-tuple-element.55.refs_0_, bf16[2,16,768]{2,1,0:T(8,128)(2,1)S(1)} %bitcast.13, f32[2,16,768]{2,1,0:T(8,128)S(1)} %copy-done.5, f32[2,16,768]{2,1,0:T(8,128)S(1)} %collective-permute-done.10.refs_3_), custom_call_target="tpu_custom_call" | custom-call | tf_op jit(solution)/shard_map/pallas_call | solution.py:130
  44.9 1.7 %collective-permute-start.11 = (bf16[1,2,16,768]{3,2,1,0:T(8,128)(2,1)S(1)}, bf16[1,2,16,768]{3,2,1,0:T(8,128)(2,1)S(1)}, u32[]{:S(2)}, u32[]{:S(2)}) collective-permute-start(bf16[1,2,16,768]{3,2,1,0:T(8,128)(2,1)S(1)} %bitcast.11), channel_id=1, source_target_pairs={{0,4},{2,6},{4,0},{6,2},{8,12},{10,14},{12,8},{14,10},{16,20},{18,... | collective-permute-start | bytes 147464 | tf_op jit(solution)/shard_map/ppermute | solution.py:285
  46.5 2.5 %collective-permute-done.11 = bf16[1,2,16,768]{3,2,1,0:T(8,128)(2,1)S(1)} collective-permute-done((bf16[1,2,16,768]{3,2,1,0:T(8,128)(2,1)S(1)}, bf16[1,2,16,768]{3,2,1,0:T(8,128)(2,1)S(1)}, u32[]{:S(2)}, u32[]{:S(2)}) %collective-permute-start.11) | collective-permute-done | bytes 49184 | tf_op jit(solution)/shard_map/ppermute | solution.py:285
  49.1 2.1 %collective-permute-start.12 = (bf16[2,2,16,768]{3,2,1,0:T(8,128)(2,1)S(1)}, bf16[2,2,16,768]{3,2,1,0:T(8,128)(2,1)S(1)}, u32[]{:S(2)}, u32[]{:S(2)}) collective-permute-start(bf16[2,2,16,768]{3,2,1,0:T(8,128)(2,1)S(1)} %pad_maximum_fusion), channel_id=1, source_target_pairs={{0,8},{2,10},{4,12},{6,14},{8,0},{10,2},{12,4},{14,6},{16,24},{18,... | collective-permute-start | bytes 294920 | tf_op jit(solution)/shard_map/ppermute | solution.py:285
  51.1 1.1 %collective-permute-start.13 = (bf16[2,2,16,768]{3,2,1,0:T(8,128)(2,1)S(1)}, bf16[2,2,16,768]{3,2,1,0:T(8,128)(2,1)S(1)}, u32[]{:S(2)}, u32[]{:S(2)}) collective-permute-start(bf16[2,2,16,768]{3,2,1,0:T(8,128)(2,1)S(1)} %pad_maximum_fusion), channel_id=1, source_target_pairs={{0,16},{2,18},{4,20},{6,22},{8,24},{10,26},{12,28},{14,30},{16,0},... | collective-permute-start | bytes 294920 | tf_op jit(solution)/shard_map/ppermute | solution.py:285
  52.2 1.4 %collective-permute-start.14 = (bf16[2,2,16,768]{3,2,1,0:T(8,128)(2,1)S(1)}, bf16[2,2,16,768]{3,2,1,0:T(8,128)(2,1)S(1)}, u32[]{:S(2)}, u32[]{:S(2)}) collective-permute-start(bf16[2,2,16,768]{3,2,1,0:T(8,128)(2,1)S(1)} %pad_maximum_fusion), channel_id=1, source_target_pairs={{0,24},{2,26},{4,28},{6,30},{8,16},{10,18},{12,20},{14,22},{16,8},... | collective-permute-start | bytes 294920 | tf_op jit(solution)/shard_map/ppermute | solution.py:285
  53.6 4.2 %shard_map.67.attended_ref = f32[512,512]{1,0:T(8,128)S(1)} custom-call(s32[6]{0:T(128)S(1)} %copy-done.6, s32[32,1]{1,0:T(8,128)S(1)} %copy.7.lengths, bf16[512,512]{1,0:T(8,128)(2,1)S(1)} %copy-done.2, bf16[512,512]{1,0:T(8,128)(2,1)S(1)} %collective-permute-done.7.far_k, bf16[512,512]{1,0:T(8,128)(2,1)S(1)} %collective-permute-done.8.far_v, ...), custom_call_target="tpu_custom_call" | custom-call | tf_op jit(solution)/shard_map/pallas_call | solution.py:225
  57.9 1.7 %collective-permute-done.13 = bf16[2,2,16,768]{3,2,1,0:T(8,128)(2,1)S(1)} collective-permute-done((bf16[2,2,16,768]{3,2,1,0:T(8,128)(2,1)S(1)}, bf16[2,2,16,768]{3,2,1,0:T(8,128)(2,1)S(1)}, u32[]{:S(2)}, u32[]{:S(2)}) %collective-permute-start.13) | collective-permute-done | bytes 98336 | tf_op jit(solution)/shard_map/ppermute | solution.py:285
  59.6 0.0 collective-permute-done.14
  59.6 0.1 collective-permute-start.15
  59.7 1.7 %collective-permute-done.15.mate_w = bf16[8,2,16,768]{3,2,1,0:T(8,128)(2,1)S(1)} collective-permute-done((bf16[8,2,16,768]{3,2,1,0:T(8,128)(2,1)S(1)}, bf16[8,2,16,768]{3,2,1,0:T(8,128)(2,1)S(1)}, u32[]{:S(2)}, u32[]{:S(2)}) %collective-permute-start.15) | collective-permute-done | bytes 393248 | tf_op jit(solution)/shard_map/ppermute | solution.py:276
  61.4 2.0 %shard_map.68 = bf16[512,512]{1,0:T(8,128)(2,1)} custom-call(bf16[512,512]{1,0:T(8,128)(2,1)S(1)} %copy-done.2, bf16[8,2,16,768]{3,2,1,0:T(8,128)(2,1)S(1)} %constant_dynamic-update-slice_fusion.own_w, bf16[8,2,16,768]{3,2,1,0:T(8,128)(2,1)S(1)} %collective-permute-done.15.mate_w, f32[512,512]{1,0:T(8,128)S(1)} %shard_map.67.attended_ref), custom_call_target="tpu_custom_call" | custom-call | tf_op jit(solution)/shard_map/pallas_call | solution.py:250
  (17 shorter events, 0.1 us)
Async XLA Ops:
  0.0 1.4 %copy-start = (f32[4,128,768]{2,1,0:T(8,128)S(1)}, f32[4,128,768]{2,1,0:T(8,128)}, u32[]{:S(2)}) copy-start(f32[4,128,768]{2,1,0:T(8,128)} %param.10) | copy-start | bytes 4718596
  1.5 10.5 %collective-permute-start = (bf16[512,512]{1,0:T(8,128)(2,1)}, bf16[512,512]{1,0:T(8,128)(2,1)S(1)}, u32[]{:S(2)}, u32[]{:S(2)}) collective-permute-start(bf16[512,512]{1,0:T(8,128)(2,1)} %own_k.1), channel_id=1, source_target_pairs={{0,2},{2,0},{4,6},{6,4},{8,10},{10,8},{12,14},{14,12},{16,18},{18,... | collective-permute-start | bytes 1572872 | tf_op jit(solution)/shard_map/ppermute | solution.py:276
  2.0 10.7 %collective-permute-start.1 = (bf16[512,512]{1,0:T(8,128)(2,1)}, bf16[512,512]{1,0:T(8,128)(2,1)S(1)}, u32[]{:S(2)}, u32[]{:S(2)}) collective-permute-start(bf16[512,512]{1,0:T(8,128)(2,1)} %own_v.1), channel_id=1, source_target_pairs={{0,2},{2,0},{4,6},{6,4},{8,10},{10,8},{12,14},{14,12},{16,18},{18,... | collective-permute-start | bytes 1572872 | tf_op jit(solution)/shard_map/ppermute | solution.py:276
  2.1 19.4 %collective-permute-start.2 = (bf16[2,128,768]{2,1,0:T(8,128)(2,1)S(1)}, bf16[2,128,768]{2,1,0:T(8,128)(2,1)}, u32[]{:S(2)}, u32[]{:S(2)}) collective-permute-start(bf16[2,128,768]{2,1,0:T(8,128)(2,1)S(1)} %dynamic-slice_convert_fusion.local_w), channel_id=1, source_target_pairs={{2,3},{3,2},{6,7},{7,6},{10,11},{11,10},{14,15},{15,14},{18,19},{1... | collective-permute-start | bytes 1179656 | tf_op jit(solution)/shard_map/ppermute | solution.py:293
  3.4 36.6 %collective-permute-start.7 = (bf16[512,512]{1,0:T(8,128)(2,1)}, bf16[512,512]{1,0:T(8,128)(2,1)S(1)}, u32[]{:S(2)}, u32[]{:S(2)}) collective-permute-start(bf16[512,512]{1,0:T(8,128)(2,1)} %own_k.1), channel_id=1, source_target_pairs={{2,4},{6,8},{10,12},{14,16},{18,20},{22,24},{26,28},{4,2},{8,6},{1... | collective-permute-start | bytes 1572872 | tf_op jit(solution)/shard_map/ppermute | solution.py:281
  5.5 16.0 %collective-permute-start.3 = (f32[8,512]{1,0:T(8,128)}, f32[8,512]{1,0:T(8,128)}, u32[]{:S(2)}, u32[]{:S(2)}) collective-permute-start(f32[8,512]{1,0:T(8,128)} %pad.4.own_rate), channel_id=1, source_target_pairs={{0,2},{2,0},{4,6},{6,4},{8,10},{10,8},{12,14},{14,12},{16,18},{18,... | collective-permute-start | bytes 49160 | tf_op jit(solution)/shard_map/ppermute | solution.py:276
  12.0 28.0 %collective-permute-start.8 = (bf16[512,512]{1,0:T(8,128)(2,1)}, bf16[512,512]{1,0:T(8,128)(2,1)S(1)}, u32[]{:S(2)}, u32[]{:S(2)}) collective-permute-start(bf16[512,512]{1,0:T(8,128)(2,1)} %own_v.1), channel_id=1, source_target_pairs={{2,4},{6,8},{10,12},{14,16},{18,20},{22,24},{26,28},{4,2},{8,6},{1... | collective-permute-start | bytes 1572872 | tf_op jit(solution)/shard_map/ppermute | solution.py:281
  12.7 1.0 %copy-start.1 = (bf16[512,512]{1,0:T(8,128)(2,1)S(1)}, bf16[512,512]{1,0:T(8,128)(2,1)}, u32[]{:S(2)}) copy-start(bf16[512,512]{1,0:T(8,128)(2,1)} %q_ref.5) | copy-start | bytes 1572868
  13.7 1.0 %copy-start.3 = (bf16[512,512]{1,0:T(8,128)(2,1)S(1)}, bf16[512,512]{1,0:T(8,128)(2,1)}, u32[]{:S(2)}) copy-start(bf16[512,512]{1,0:T(8,128)(2,1)} %own_k.1) | copy-start | bytes 1572868
  14.8 1.0 %copy-start.4 = (bf16[512,512]{1,0:T(8,128)(2,1)S(1)}, bf16[512,512]{1,0:T(8,128)(2,1)}, u32[]{:S(2)}) copy-start(bf16[512,512]{1,0:T(8,128)(2,1)} %own_v.1) | copy-start | bytes 1572868
  15.8 0.7 %copy-start.6 = (s32[6]{0:T(128)S(1)}, s32[6]{0:T(128)}, u32[]{:S(2)}) copy-start(s32[6]{0:T(128)} %stack.27.spots) | copy-start | bytes 76
  21.4 11.1 %copy-start.5 = (f32[2,16,768]{2,1,0:T(8,128)S(1)}, f32[2,16,768]{2,1,0:T(8,128)}, u32[]{:S(2)}) copy-start(f32[2,16,768]{2,1,0:T(8,128)} %constant_dynamic-slice_fusion.refs_2_) | copy-start | bytes 294916
  24.8 28.8 %copy-start.2 = (bf16[512,512]{1,0:T(8,128)(2,1)S(1)}, bf16[512,512]{1,0:T(8,128)(2,1)}, u32[]{:S(2)}) copy-start(bf16[512,512]{1,0:T(8,128)(2,1)} %q_ref.5) | copy-start | bytes 1572868
  24.8 7.7 %collective-permute-start.4 = (bf16[2,2,16,768]{3,2,1,0:T(8,128)(2,1)S(1)}, bf16[2,2,16,768]{3,2,1,0:T(8,128)(2,1)S(1)}, u32[]{:S(2)}, u32[]{:S(2)}) collective-permute-start(bf16[2,2,16,768]{3,2,1,0:T(8,128)(2,1)S(1)} %get-tuple-element.51), channel_id=1, source_target_pairs={{0,8},{2,10},{4,12},{6,14},{8,0},{10,2},{12,4},{14,6},{16,24},{18,... | collective-permute-start | bytes 294920 | tf_op jit(solution)/shard_map/ppermute | solution.py:285
  29.3 10.7 %collective-permute-start.5 = (bf16[2,2,16,768]{3,2,1,0:T(8,128)(2,1)S(1)}, bf16[2,2,16,768]{3,2,1,0:T(8,128)(2,1)S(1)}, u32[]{:S(2)}, u32[]{:S(2)}) collective-permute-start(bf16[2,2,16,768]{3,2,1,0:T(8,128)(2,1)S(1)} %get-tuple-element.53), channel_id=1, source_target_pairs={{0,16},{2,18},{4,20},{6,22},{8,24},{10,26},{12,28},{14,30},{16,0},... | collective-permute-start | bytes 294920 | tf_op jit(solution)/shard_map/ppermute | solution.py:285
  31.9 8.1 %collective-permute-start.6 = (bf16[2,2,16,768]{3,2,1,0:T(8,128)(2,1)S(1)}, bf16[2,2,16,768]{3,2,1,0:T(8,128)(2,1)S(1)}, u32[]{:S(2)}, u32[]{:S(2)}) collective-permute-start(bf16[2,2,16,768]{3,2,1,0:T(8,128)(2,1)S(1)} %get-tuple-element.52), channel_id=1, source_target_pairs={{0,24},{2,26},{4,28},{6,30},{8,16},{10,18},{12,20},{14,22},{16,8},... | collective-permute-start | bytes 294920 | tf_op jit(solution)/shard_map/ppermute | solution.py:285
  32.5 9.2 %collective-permute-start.10 = (f32[2,16,768]{2,1,0:T(8,128)S(1)}, f32[2,16,768]{2,1,0:T(8,128)S(1)}, u32[]{:S(2)}, u32[]{:S(2)}) collective-permute-start(f32[2,16,768]{2,1,0:T(8,128)S(1)} %copy-done.5), channel_id=1, source_target_pairs={{2,3},{3,2},{6,7},{7,6},{10,11},{11,10},{14,15},{15,14},{18,19},{1... | collective-permute-start | bytes 294920 | tf_op jit(solution)/shard_map/ppermute | solution.py:293
  40.1 4.2 %collective-permute-start.9 = (bf16[1,2,16,768]{3,2,1,0:T(8,128)(2,1)S(1)}, bf16[1,2,16,768]{3,2,1,0:T(8,128)(2,1)S(1)}, u32[]{:S(2)}, u32[]{:S(2)}) collective-permute-start(bf16[1,2,16,768]{3,2,1,0:T(8,128)(2,1)S(1)} %get-tuple-element.54), channel_id=1, source_target_pairs={{0,4},{2,6},{4,0},{6,2},{8,12},{10,14},{12,8},{14,10},{16,20},{18,... | collective-permute-start | bytes 147464 | tf_op jit(solution)/shard_map/ppermute | solution.py:285
  44.9 4.2 %collective-permute-start.11 = (bf16[1,2,16,768]{3,2,1,0:T(8,128)(2,1)S(1)}, bf16[1,2,16,768]{3,2,1,0:T(8,128)(2,1)S(1)}, u32[]{:S(2)}, u32[]{:S(2)}) collective-permute-start(bf16[1,2,16,768]{3,2,1,0:T(8,128)(2,1)S(1)} %bitcast.11), channel_id=1, source_target_pairs={{0,4},{2,6},{4,0},{6,2},{8,12},{10,14},{12,8},{14,10},{16,20},{18,... | collective-permute-start | bytes 147464 | tf_op jit(solution)/shard_map/ppermute | solution.py:285
  49.1 8.8 %collective-permute-start.12 = (bf16[2,2,16,768]{3,2,1,0:T(8,128)(2,1)S(1)}, bf16[2,2,16,768]{3,2,1,0:T(8,128)(2,1)S(1)}, u32[]{:S(2)}, u32[]{:S(2)}) collective-permute-start(bf16[2,2,16,768]{3,2,1,0:T(8,128)(2,1)S(1)} %pad_maximum_fusion), channel_id=1, source_target_pairs={{0,8},{2,10},{4,12},{6,14},{8,0},{10,2},{12,4},{14,6},{16,24},{18,... | collective-permute-start | bytes 294920 | tf_op jit(solution)/shard_map/ppermute | solution.py:285
  51.1 8.4 %collective-permute-start.13 = (bf16[2,2,16,768]{3,2,1,0:T(8,128)(2,1)S(1)}, bf16[2,2,16,768]{3,2,1,0:T(8,128)(2,1)S(1)}, u32[]{:S(2)}, u32[]{:S(2)}) collective-permute-start(bf16[2,2,16,768]{3,2,1,0:T(8,128)(2,1)S(1)} %pad_maximum_fusion), channel_id=1, source_target_pairs={{0,16},{2,18},{4,20},{6,22},{8,24},{10,26},{12,28},{14,30},{16,0},... | collective-permute-start | bytes 294920 | tf_op jit(solution)/shard_map/ppermute | solution.py:285
  52.2 7.4 %collective-permute-start.14 = (bf16[2,2,16,768]{3,2,1,0:T(8,128)(2,1)S(1)}, bf16[2,2,16,768]{3,2,1,0:T(8,128)(2,1)S(1)}, u32[]{:S(2)}, u32[]{:S(2)}) collective-permute-start(bf16[2,2,16,768]{3,2,1,0:T(8,128)(2,1)S(1)} %pad_maximum_fusion), channel_id=1, source_target_pairs={{0,24},{2,26},{4,28},{6,30},{8,16},{10,18},{12,20},{14,22},{16,8},... | collective-permute-start | bytes 294920 | tf_op jit(solution)/shard_map/ppermute | solution.py:285
  59.6 1.8 %collective-permute-start.15 = (bf16[8,2,16,768]{3,2,1,0:T(8,128)(2,1)S(1)}, bf16[8,2,16,768]{3,2,1,0:T(8,128)(2,1)S(1)}, u32[]{:S(2)}, u32[]{:S(2)}) collective-permute-start(bf16[8,2,16,768]{3,2,1,0:T(8,128)(2,1)S(1)} %constant_dynamic-update-slice_fusion.own_w), channel_id=1, source_target_pairs={{0,2},{2,0},{4,6},{6,4},{8,10},{10,8},{12,14},{14,12},{16,18},{18,... | collective-permute-start | bytes 1179656 | tf_op jit(solution)/shard_map/ppermute | solution.py:276

commit v4 on v3

v4 whole, which is shorter than its diff:
```python
import functools
import math

import jax
import jax.numpy as jnp
from jax import lax
from jax.experimental import pallas as pl
from jax.experimental.pallas import tpu as pltpu
from jax.sharding import PartitionSpec as P

DM = 256
HD = 128
CORES = 2
NORM_EPS = 1e-06
VMEM_BYTES = 40 * 2**20
MASKED = -1e30

BF16 = jnp.bfloat16
F32 = jnp.float32


def in_vmem(count):
    return [pl.BlockSpec(memory_space=pltpu.VMEM)] * count


def in_smem():
    return pl.BlockSpec(memory_space=pltpu.SMEM)


def params(limit=VMEM_BYTES):
    return pltpu.CompilerParams(vmem_limit_bytes=limit)


def dot_nt(a, b):
    return lax.dot_general(a, b, (((1,), (1,)), ((), ())), preferred_element_type=F32)


def dot_tn(a, b):
    return lax.dot_general(a, b, (((0,), (0,)), ((), ())), preferred_element_type=F32)


def dot_nn(a, b):
    return jnp.dot(a, b, preferred_element_type=F32)


def chip_digits(chips):
    digits = []
    while chips % 4 == 0:
        digits.append(4)
        chips //= 4
    if chips > 1:
        digits.append(chips)
    return digits[::-1]


def from_hbm(*arrays):
    return [pltpu.with_memory_space_constraint(array, pltpu.HBM) for array in arrays]


def stage_kernel(
    blocks, q_any, k_any, v_any, rates_any, weights_any,
    spots, q_ref, pack_ref, far_ref, last_ref, w_ref, give_ref, exact_ref,
    held, rates, sems,
):
    spot, plane = lax.axis_index("tok"), lax.axis_index("mem")
    devices, planes = lax.axis_size("tok"), lax.axis_size("mem")
    tokens, width = q_ref.shape
    memories, hidden, _ = exact_ref.shape
    core, chip = lax.rem(spot, CORES), lax.div(spot, CORES)
    copies = []

    def bring(source, goal):
        copies.append(pltpu.make_async_copy(source, goal, sems.at[len(copies)]))
        copies[-1].start()

    units = pl.ds(pl.multiple_of(core * hidden, hidden), hidden)
    other = planes - 1 - plane
    bring(weights_any.at[pl.ds(other * memories, memories), units], held)
    bring(weights_any.at[pl.ds(plane * memories, memories), units], exact_ref)
    bring(rates_any, rates)
    bring(v_any, pack_ref.at[pl.ds(tokens, tokens)])
    bring(k_any, pack_ref.at[pl.ds(0, tokens)])
    pieces = [part for m in range(memories) for part in ((k_any, m), (v_any, m))]
    for place, (part, m) in enumerate(pieces):
        goal = far_ref.at[pl.ds(place * tokens, tokens)] if place < len(pieces) - 1 else last_ref
        bring(part.at[:, pl.ds(m * DM, DM)], goal)
    bring(q_any, q_ref)
    spots[0] = spot * tokens
    spots[1] = (spot ^ 1) * tokens
    spots[2] = jnp.where(core == 0, spot - 1, spot + 1) * tokens
    spots[3] = lax.div(chip, devices // CORES // blocks)
    copies[0].wait()
    for memory in range(memories):
        give_ref[memory] = held[memory].astype(BF16)
    copies[1].wait()
    for memory in range(memories):
        w_ref[memory] = exact_ref[memory].astype(BF16)
    copies[2].wait()
    copies[3].wait()
    turned = jnp.transpose(rates[...])
    for memory in range(memories):
        rate = jnp.zeros((tokens, 1), F32)
        for here in range(planes):
            place = here * memories + memory
            rate = jnp.where(plane == here, turned[:, place : place + 1], rate)
        features = pl.ds(memory * DM, DM)
        value = pack_ref[pl.ds(tokens, tokens), features]
        pack_ref[pl.ds(2 * tokens, tokens), features] = (rate * value.astype(F32)).astype(BF16)
    for copy in copies[4:]:
        copy.wait()


def stage(queries, keys, values, step_sizes, fast_weights, memories, blocks):
    tokens, width = queries.shape
    half = (memories, fast_weights.shape[1] // CORES, 3 * DM)
    return pl.pallas_call(
        functools.partial(stage_kernel, blocks),
        out_shape=(
            jax.ShapeDtypeStruct((8,), jnp.int32),
            pltpu.VMEM((tokens, width), BF16),
            pltpu.VMEM((3 * tokens, width), BF16),
            pltpu.VMEM(((2 * memories - 1) * tokens, DM), BF16),
            pltpu.VMEM((tokens, DM), BF16),
            pltpu.VMEM(half, BF16),
            pltpu.VMEM(half, BF16),
            pltpu.VMEM(half, F32),
        ),
        in_specs=[pl.BlockSpec(memory_space=pltpu.HBM)] * 5,
        out_specs=(in_smem(),) + tuple(in_vmem(7)),
        scratch_shapes=[
            pltpu.VMEM(half, F32),
            pltpu.VMEM(step_sizes.shape, F32),
            pltpu.SemaphoreType.DMA((6 + 2 * memories,)),
        ],
        compiler_params=params(),
    )(*from_hbm(queries, keys, values, step_sizes, fast_weights))


def grads_kernel(spots, own, mate, own_w, sent_w, grad_ref):
    tokens = own.shape[0] // 3
    memories = own_w.shape[0]
    hidden = 2 * own_w.shape[1]
    for memory in range(memories):
        features = pl.ds(memory * DM, DM)
        weights = jnp.concatenate([own_w[memory], sent_w[memory]], axis=0)
        gate_up_w = jnp.concatenate([weights[:, :DM], weights[:, DM : 2 * DM]], axis=0)
        out_w = weights[:, 2 * DM :]
        grad_pair = jnp.zeros((2 * hidden, DM), F32)
        grad_out = jnp.zeros((hidden, DM), F32)
        for side in (own, mate):
            key = side[pl.ds(0, tokens), features]
            scaled = side[pl.ds(2 * tokens, tokens), features]
            gate_up = dot_nt(key, gate_up_w)
            gate, up = gate_up[:, :hidden], gate_up[:, hidden:]
            sigmoid = jax.nn.sigmoid(gate)
            swish = gate * sigmoid
            slope = sigmoid * (1.0 + gate * (1.0 - sigmoid))
            back = -dot_nt(scaled, out_w)
            pair = jnp.concatenate(
                [(back * up * slope).astype(BF16), (back * swish).astype(BF16)], axis=1
            )
            grad_pair += dot_tn(pair, key)
            grad_out -= dot_tn((swish * up).astype(BF16), scaled)
        found = (grad_pair[:hidden], grad_pair[hidden:], grad_out)
        for part, grad in enumerate(found):
            grad = grad.astype(BF16)
            columns = pl.ds(part * DM, DM)
            if grad_ref.ndim == 3:
                grad_ref[memory, :, columns] = grad
            else:
                blocks, _, rows, _ = grad_ref.shape
                for block in range(blocks):
                    piece = grad[block * rows : (block + 1) * rows]
                    grad_ref[spots[3] ^ block, memory, :, columns] = piece


def half_grads(spots, blocks, own, mate, own_w, sent_w):
    memories, quarter, width = own_w.shape
    hidden = 2 * quarter
    rows = hidden // blocks
    placed = rows % 16 == 0
    shape = (blocks, memories, rows, width) if placed else (memories, hidden, width)
    grads = pl.pallas_call(
        grads_kernel,
        out_shape=jax.ShapeDtypeStruct(shape, BF16),
        in_specs=[in_smem()] + in_vmem(4),
        out_specs=in_vmem(1)[0],
        compiler_params=params(),
    )(spots, own, mate, own_w, sent_w)
    if placed:
        return grads
    grads = grads.reshape(memories, blocks, rows, width).transpose(1, 0, 2, 3)
    return jnp.take(grads, jnp.arange(blocks, dtype=jnp.int32) ^ spots[3], axis=0)


def update_kernel(step_rate, parts, spots, *refs):
    *grads, exact, sent, new_ref = refs
    rows = new_ref.shape[1]
    total = grads[0][...].astype(F32)
    for part in grads[1:]:
        total += part[...].astype(F32)
    if sent is None:
        before = exact[...]
    else:
        held = exact.shape[1]
        first = spots[3] * rows
        near = pl.multiple_of(jnp.minimum(first, held - rows), rows)
        away = pl.multiple_of(jnp.maximum(first - held, 0), rows)
        before = jnp.where(
            first < held, exact[:, pl.ds(near, rows), :], sent[:, pl.ds(away, rows), :].astype(F32)
        )
    stepped = before - total * step_rate
    for block in range(3):
        columns = slice(block * DM, (block + 1) * DM)
        old, new = before[..., columns], stepped[..., columns]
        old_norm = jnp.sqrt(jnp.sum(old * old, axis=-1, keepdims=True))
        new_norm = jnp.sqrt(jnp.sum(new * new, axis=-1, keepdims=True) + NORM_EPS)
        new_ref[:, :, columns] = (new * (old_norm / new_norm)).astype(BF16)


def update_rows(spots, step_rate, grads, exact, sent):
    rows = grads[0].shape[1]
    body = functools.partial(update_kernel, step_rate, len(grads))
    given = list(grads) + [exact, sent]
    if rows % 16:
        whole = jnp.concatenate([exact, sent.astype(F32)], axis=1)
        given[-2:] = [lax.dynamic_slice_in_dim(whole, spots[3] * rows, rows, 1)]

        def body(spots, *refs):
            update_kernel(step_rate, len(grads), spots, *refs[:-1], None, refs[-1])

    return pl.pallas_call(
        body,
        out_shape=jax.ShapeDtypeStruct(grads[0].shape, BF16),
        in_specs=[in_smem()] + in_vmem(len(given)),
        out_specs=in_vmem(1)[0],
        compiler_params=params(),
    )(spots, *given)


def view_bounds(lengths, own, tokens):
    views = lengths.shape[1]
    down = lax.broadcasted_iota(jnp.int32, (views, views), 0)
    across = lax.broadcasted_iota(jnp.int32, (views, views), 1)
    column = jnp.sum(jnp.where(down == across, lengths[...], 0), axis=1, keepdims=True)
    ends = jnp.sum(jnp.where(down <= across, column, 0), axis=0, keepdims=True)
    spot = own + lax.broadcasted_iota(jnp.int32, (tokens, 1), 0)
    stop = jnp.min(jnp.where(ends > spot, ends, jnp.int32(2**30)), axis=1, keepdims=True)
    start = jnp.max(jnp.where(ends <= spot, ends, 0), axis=1, keepdims=True)
    return start, stop


def inside(base, count, start, stop):
    place = base + lax.broadcasted_iota(jnp.int32, (1, count), 1)
    return (place >= start) & (place < stop)


SCORE_SCALE = math.log2(math.e) / math.sqrt(HD)


def near_kernel(spots, lengths, q_ref, own, mate, mixed_ref, peak_ref, sum_ref):
    tokens, width = q_ref.shape
    start, stop = view_bounds(lengths, spots[0], tokens)
    block_rows = tokens // 2
    for block in range(2):
        rows = slice(block * block_rows, (block + 1) * block_rows)
        masks = [inside(spots[i], tokens, start[rows], stop[rows]) for i in range(2)]
        for head in range(width // HD):
            lanes = pl.ds(head * HD, HD)
            query = q_ref[rows, lanes]
            scores = [
                jnp.where(mask, dot_nt(query, side[:tokens, lanes]) * SCORE_SCALE, MASKED)
                for mask, side in zip(masks, (own, mate))
            ]
            peak = functools.reduce(
                jnp.maximum, [jnp.max(s, axis=1, keepdims=True) for s in scores]
            )
            weights = [jnp.exp2(s - peak) for s in scores]
            peak_ref[rows, head : head + 1] = peak
            sum_ref[rows, head : head + 1] = sum(
                jnp.sum(w, axis=1, keepdims=True) for w in weights
            )
            mixed_ref[rows, lanes] = sum(
                dot_nn(w.astype(BF16), side[pl.ds(tokens, tokens), lanes])
                for w, side in zip(weights, (own, mate))
            )


def far_kernel(
    memory, spots, lengths, q_ref, far, last, mixed_ref, peak_ref, sum_ref, out_ref
):
    tokens, _ = q_ref.shape
    start, stop = view_bounds(lengths, spots[0], tokens)
    far_k = far.at[pl.ds(2 * memory * tokens, tokens)]
    far_v = last if last is not None else far.at[pl.ds((2 * memory + 1) * tokens, tokens)]
    block_rows = tokens // 2
    for block in range(2):
        rows = slice(block * block_rows, (block + 1) * block_rows)
        mask = inside(spots[2], tokens, start[rows], stop[rows])
        for step in range(DM // HD):
            lanes = pl.ds(step * HD, HD)
            head = memory * (DM // HD) + step
            across = pl.ds(head * HD, HD)
            scores = dot_nt(q_ref[rows, across], far_k[:, lanes]) * SCORE_SCALE
            scores = jnp.where(mask, scores, MASKED)
            before = peak_ref[rows, head : head + 1]
            peak = jnp.maximum(before, jnp.max(scores, axis=1, keepdims=True))
            weights = jnp.exp2(scores - peak)
            shrink = jnp.exp2(before - peak)
            total = sum_ref[rows, head : head + 1] * shrink + jnp.sum(
                weights, axis=1, keepdims=True
            )
            mixed = mixed_ref[rows, across] * shrink + dot_nn(
                weights.astype(BF16), far_v[:, lanes]
            )
            out_ref[rows, lanes] = mixed / total


def attend_near(spots, lengths, queries, own, mate):
    tokens, width = queries.shape
    stats = jax.ShapeDtypeStruct((tokens, width // HD), F32)
    return pl.pallas_call(
        near_kernel,
        out_shape=(jax.ShapeDtypeStruct(queries.shape, F32), stats, stats),
        in_specs=[in_smem()] + in_vmem(4),
        out_specs=tuple(in_vmem(3)),
        compiler_params=params(),
    )(spots, lengths, queries, own, mate)


def attend_far(memory, spots, lengths, queries, far, last, near):
    if last is None:

        def body(spots, lengths, q_ref, far, *rest):
            far_kernel(memory, spots, lengths, q_ref, far, None, *rest)
    else:
        body = functools.partial(far_kernel, memory)
    given = (lengths, queries, far) + (() if last is None else (last,)) + tuple(near)
    return pl.pallas_call(
        body,
        out_shape=jax.ShapeDtypeStruct((queries.shape[0], DM), F32),
        in_specs=[in_smem()] + in_vmem(len(given)),
        out_specs=in_vmem(1)[0],
        compiler_params=params(),
    )(spots, *given)


def read_kernel(parts, q_ref, w_ref, *refs):
    before, out_ref = refs[:parts], refs[parts]
    blocks, memories, rows, _ = w_ref.shape
    for memory in range(memories):
        features = pl.ds(memory * DM, DM)
        query = q_ref[:, features]
        weights = w_ref[:, memory].reshape(blocks * rows, 3 * DM)
        gate = dot_nt(query, weights[:, :DM])
        up = dot_nt(query, weights[:, DM : 2 * DM])
        hidden = (gate * jax.nn.sigmoid(gate) * up).astype(BF16)
        total = dot_nn(hidden, weights[:, 2 * DM :])
        if parts > 0:
            total += before[0][:, features] + before[1 + memory][...]
        out_ref[:, features] = total.astype(out_ref.dtype)


def read_half(queries, weights, before, kind):
    return pl.pallas_call(
        functools.partial(read_kernel, len(before)),
        out_shape=jax.ShapeDtypeStruct(queries.shape, kind),
        in_specs=in_vmem(2 + len(before)),
        out_specs=in_vmem(1)[0],
        compiler_params=params(),
    )(queries, weights, *before)


def on_device(queries, keys, values, step_sizes, fast_weights, view_lengths):
    tokens = queries.shape[0]
    memories = queries.shape[1] // DM
    devices = lax.axis_size("tok")
    planes = lax.axis_size("mem")
    chips = devices // CORES
    digits = chip_digits(chips)
    blocks = chips // digits[0]

    def to_core(x):
        return lax.ppermute(x, "tok", [(i, i ^ 1) for i in range(devices)])

    def to_far(x):
        return lax.ppermute(x, "tok", [(i, (i + i % 2 * 2 - 1) % devices) for i in range(devices)])

    def to_chip(x, flip):
        pairs = [(i, (((i // CORES) ^ flip) * CORES) + i % CORES) for i in range(devices)]
        return lax.ppermute(x, "tok", pairs)

    def to_plane(x):
        return lax.ppermute(x, "mem", [(p, planes - 1 - p) for p in range(planes)])

    spots, q, own, far, last, own_w, give_w, exact = stage(
        queries, keys, values, step_sizes, fast_weights, memories, blocks
    )
    sent_w = to_plane(give_w)
    mate = to_core(own)
    far = to_far(far)
    lengths = view_lengths.reshape(1, -1)

    held = half_grads(spots, blocks, own, mate, own_w, sent_w)
    held, q = lax.optimization_barrier((held, q))
    near = attend_near(spots, lengths, q, own, mate)
    stride = chips
    for place, radix in enumerate(digits[:0:-1]):
        stride //= radix
        held = held.reshape((radix, stride // digits[0]) + held.shape[1:])
        came = [to_chip(held[step], step * stride) for step in range(1, radix)]
        if place == 0:
            came, near, far = lax.optimization_barrier((came, near, far))
        held = sum([part.astype(F32) for part in came], held[0].astype(F32)).astype(BF16)
    held = held[0]
    came = [to_chip(held, step) for step in range(1, digits[0])]
    came, last = lax.optimization_barrier((came, last))
    last = to_far(last)
    all_tokens = tokens * devices
    fresh = update_rows(
        spots, 1.0 / math.sqrt(all_tokens), [held] + came, exact, sent_w
    )

    gathered = fresh[None]
    stride = digits[0]
    for radix in digits[1:]:
        came = [to_chip(gathered, step * stride) for step in range(1, radix)]
        if stride == digits[0]:
            gathered, near = lax.optimization_barrier((gathered, near))
            attended = [
                attend_far(m, spots, lengths, q, far, last if m == memories - 1 else None, near)
                for m in range(memories)
            ]
            came, attended = lax.optimization_barrier((came, attended))
        stride *= radix
        gathered = jnp.concatenate([gathered] + came, axis=0)
    mate_w = to_core(gathered)
    partial = read_half(q, gathered, [], F32)
    return read_half(q, mate_w, [partial] + attended, BF16)


def solution(mesh):
    placed = (
        P("tok", "mem"),
        P("tok", "mem"),
        P("tok", "mem"),
        P(None, "tok"),
        P(None, "mem", None),
        P(),
    )
    return jax.shard_map(
        on_device, mesh=mesh, in_specs=placed, out_specs=P("tok", "mem"), check_vma=False
    )
```

time: 63.9 us -> 49.6 us (0.78)
  local copies, waits for them, and re-layouts: 8.66 us -> 0.06 us
  waiting for transfers between devices: 15.7 us -> 9.14 us
  Pallas kernels: 15.2 us -> 18.2 us
  starting transfers between devices: 23.7 us -> 21.9 us
    ppermute x8 -> x7, waiting for transfers between devices: 13.9 us -> 3.97 us  [to_chip(): return lax.ppermute(x, 'tok', pairs)]
    ppermute x4 -> x3, starting transfers between devices: 3.6 us -> 10.4 us  [the longest x2 8.87 us: to_far(): lax.ppermute(x, 'tok', [(i, (i + i % 2 * 2 - 1) % devices) for i in range...]
    unnamed x17 -> x5, local copies, waits for them, and re-layouts: 5.23 us -> 0.03 us
    ppermute x4 -> x2, starting transfers between devices: 5.16 us -> 0.59 us  [to_core(): return lax.ppermute(x, 'tok', [(i, i ^ 1) for i in range(devices)])]
    ppermute x4 -> x3, waiting for transfers between devices: 0.01 us -> 4.16 us  [the longest x1 4.15 us: to_plane(): return lax.ppermute(x, 'mem', [(p, planes - 1 - p) for p in range(planes)])]
    ppermute x8 -> x7, starting transfers between devices: 14.9 us -> 10.9 us  [to_chip(): return lax.ppermute(x, 'tok', pairs)]
    pallas_call x3 -> x6, Pallas kernels: 6.95 us -> 11 us  [the longest x2 5.46 us: attend_far(): pl.pallas_call(body, out_shape=jax.ShapeDtypeStruct((queries.shape[0], DM...]
    dynamic_slice x2 -> x0, local copies, waits for them, and re-layouts: 1.35 us -> none  [the longest x1 0.71 us: on_device(): rates = lax.dynamic_slice_in_dim(step_sizes, plane * memories, memories, 0)]
  transfers between devices with their start and end apart: 16 -> 12, of which waited for: 6 -> 5; matrix products, arithmetic and copies ran while one was open for 5% -> 0% of each run, Pallas kernels for 20% -> 29%
where the time goes in v4:
time: 49.6 us; the launch traced here: 49.4 us
  starting transfers between devices  21.9 us (44%)
  Pallas kernels  18.2 us (37%)
  waiting for transfers between devices  9.14 us (18%)
    ppermute x7, starting transfers between devices, to_chip(): return lax.ppermute(x, 'tok', pairs)  10.9 us
    ppermute x2, starting transfers between devices, to_far(): lax.ppermute(x, 'tok', [(i, (i + i % 2 * 2 - 1) % devices) for i in range...  8.87 us
    pallas_call x2, Pallas kernels, attend_far(): pl.pallas_call(body, out_shape=jax.ShapeDtypeStruct((queries.shape[0], DM...  5.46 us
    pallas_call x1, Pallas kernels, attend_near(): pl.pallas_call(near_kernel, out_shape=(jax.ShapeDtypeStruct(queries.shape...  4.95 us
    ppermute x1, waiting for transfers between devices, to_plane(): return lax.ppermute(x, 'mem', [(p, planes - 1 - p) for p in range(planes)])  4.15 us
    ppermute x7, waiting for transfers between devices, to_chip(): return lax.ppermute(x, 'tok', pairs)  3.97 us
    pallas_call x1, Pallas kernels, stage(): pl.pallas_call(functools.partial(stage_kernel, blocks), out_shape=(jax.Sh...  2.6 us
    pallas_call x1, Pallas kernels, half_grads(): pl.pallas_call(grads_kernel, out_shape=jax.ShapeDtypeStruct(shape, BF16),...  2.27 us
  transfers between devices with their start and end apart: 12, of which 5 were waited for; matrix products, arithmetic and copies ran while one was open for 0% of the time, Pallas kernels for 29%

profile of v4, /device:TPU:0, one launch (start us, length us, event | category | flops | bytes accessed | tf_op | source)
XLA Modules:
  0.0 49.4 jit_solution(3955680788804555976)
XLA Ops:
  0.0 2.6 %shard_map.64 = (s32[8]{0:T(128)S(1)}, bf16[512,512]{1,0:T(8,128)(2,1)S(1)}, bf16[1536,512]{1,0:T(8,128)(2,1)S(1)}, bf16[1536,256]{1,0:T(8,128)(2,1)S(1)}, bf16[...) custom-call(bf16[512,512]{1,0:T(8,128)(2,1)} %q_any.1, ...), custom_call_target="tpu_custom_call" | custom-call | tf_op jit(solution)/shard_map/pallas_call | solution.py:116
  2.6 0.5 %collective-permute-start = (bf16[1536,512]{1,0:T(8,128)(2,1)S(1)}, bf16[1536,512]{1,0:T(8,128)(2,1)S(1)}, u32[]{:S(2)}, u32[]{:S(2)}) collective-permute-start(bf16[1536,512]{1,0:T(8,128)(2,1)S(1)} %get-tuple-element.37.own), channel_id=1, source_target_pairs={{0,2},{2,0},{4,6},{6,4},{8,10},{10,8},{12,14},{14,12},{16,18},{18,... | collective-permute-start | bytes 4718600 | tf_op jit(solution)/shard_map/ppermute | solution.py:384
  3.1 5.6 %collective-permute-start.5 = (bf16[1536,256]{1,0:T(8,128)(2,1)S(1)}, bf16[1536,256]{1,0:T(8,128)(2,1)S(1)}, u32[]{:S(2)}, u32[]{:S(2)}) collective-permute-start(bf16[1536,256]{1,0:T(8,128)(2,1)S(1)} %get-tuple-element.46), channel_id=1, source_target_pairs={{0,30},{2,4},{4,2},{6,8},{8,6},{10,12},{12,10},{14,16},{16,14},{18... | collective-permute-start | bytes 2359304 | tf_op jit(solution)/shard_map/ppermute | solution.py:387
  8.8 1.5 %collective-permute-start.1 = (bf16[2,64,768]{2,1,0:T(8,128)(2,1)S(1)}, bf16[2,64,768]{2,1,0:T(8,128)(2,1)S(1)}, u32[]{:S(2)}, u32[]{:S(2)}) collective-permute-start(bf16[2,64,768]{2,1,0:T(8,128)(2,1)S(1)} %get-tuple-element.39), channel_id=1, source_target_pairs={{0,1},{1,0},{2,3},{3,2},{4,5},{5,4},{6,7},{7,6},{8,9},{9,8},{10,11... | collective-permute-start | bytes 589832 | tf_op jit(solution)/shard_map/ppermute | solution.py:394
  10.3 4.2 %collective-permute-done.1.sent_w.refs_3_ = bf16[2,64,768]{2,1,0:T(8,128)(2,1)S(1)} collective-permute-done((bf16[2,64,768]{2,1,0:T(8,128)(2,1)S(1)}, bf16[2,64,768]{2,1,0:T(8,128)(2,1)S(1)}, u32[]{:S(2)}, u32[]{:S(2)}) %collective-permute-start.1) | collective-permute-done | bytes 196640 | tf_op jit(solution)/shard_map/ppermute | solution.py:394
  14.4 0.0 collective-permute-done.mate
  14.4 0.0 copy-start
  14.4 2.3 %shard_map.65 = bf16[4,2,32,768]{3,2,1,0:T(8,128)(2,1)S(1)} custom-call(s32[8]{0:T(128)S(1)} %get-tuple-element.36.spots, bf16[1536,512]{1,0:T(8,128)(2,1)S(1)} %get-tuple-element.37.own, bf16[1536,512]{1,0:T(8,128)(2,1)S(1)} %collective-permute-done.mate, bf16[2,64,768]{2,1,0:T(8,128)(2,1)S(1)} %get-tuple-element.38.own_w, ...), custom_call_target="tpu_custom_call" | custom-call | tf_op jit(solution)/shard_map/pallas_call | solution.py:183
  16.7 1.8 %collective-permute-start.4 = (bf16[1,2,32,768]{3,2,1,0:T(8,128)(2,1)S(1)}, bf16[1,2,32,768]{3,2,1,0:T(8,128)(2,1)S(1)}, u32[]{:S(2)}, u32[]{:S(2)}) collective-permute-start(bf16[1,2,32,768]{3,2,1,0:T(8,128)(2,1)S(1)} %get-tuple-element.67), channel_id=1, source_target_pairs={{0,24},{2,26},{4,28},{6,30},{8,16},{10,18},{12,20},{14,22},{16,8},... | collective-permute-start | bytes 294920 | tf_op jit(solution)/shard_map/ppermute | solution.py:391
  18.6 0.0 collective-permute-start.3
  18.6 2.6 %collective-permute-start.2 = (bf16[1,2,32,768]{3,2,1,0:T(8,128)(2,1)S(1)}, bf16[1,2,32,768]{3,2,1,0:T(8,128)(2,1)S(1)}, u32[]{:S(2)}, u32[]{:S(2)}) collective-permute-start(bf16[1,2,32,768]{3,2,1,0:T(8,128)(2,1)S(1)} %get-tuple-element.69), channel_id=1, source_target_pairs={{0,8},{2,10},{4,12},{6,14},{8,0},{10,2},{12,4},{14,6},{16,24},{18,... | collective-permute-start | bytes 294920 | tf_op jit(solution)/shard_map/ppermute | solution.py:391
  21.2 0.0 copy-done
  21.2 5.0 %shard_map.66 = (f32[512,512]{1,0:T(8,128)S(1)}, f32[512,4]{1,0:T(8,128)S(1)}, f32[512,4]{1,0:T(8,128)S(1)}) custom-call(s32[8]{0:T(128)S(1)} %get-tuple-element.36.spots, s32[1,32]{1,0:T(1,128)S(1)} %bitcast.8, bf16[512,512]{1,0:T(8,128)(2,1)S(1)} %get-tuple-element.41.q_ref, bf16[1536,512]{1,0:T(8,128)(2,1)S(1)} %get-tuple-element.37.own, ...), custom_call_target="tpu_custom_call" | custom-call | tf_op jit(solution)/shard_map/pallas_call | solution.py:322
  26.2 0.0 collective-permute-done.5.far
  26.2 0.0 collective-permute-done.4
  26.2 0.5 collective-permute-done.3
  26.6 0.0 collective-permute-done.2
  26.6 0.1 fusion.refs_0_
  26.7 2.0 %collective-permute-start.6 = (bf16[2,32,768]{2,1,0:T(8,128)(2,1)S(1)}, bf16[2,32,768]{2,1,0:T(8,128)(2,1)S(1)}, u32[]{:S(2)}, u32[]{:S(2)}) collective-permute-start(bf16[2,32,768]{2,1,0:T(8,128)(2,1)S(1)} %fusion.refs_0_), channel_id=1, source_target_pairs={{0,4},{2,6},{4,0},{6,2},{8,12},{10,14},{12,8},{14,10},{16,20},{18,... | collective-permute-start | bytes 294920 | tf_op jit(solution)/shard_map/ppermute | solution.py:391
  28.7 2.7 %collective-permute-done.6.refs_1_ = bf16[2,32,768]{2,1,0:T(8,128)(2,1)S(1)} collective-permute-done((bf16[2,32,768]{2,1,0:T(8,128)(2,1)S(1)}, bf16[2,32,768]{2,1,0:T(8,128)(2,1)S(1)}, u32[]{:S(2)}, u32[]{:S(2)}) %collective-permute-start.6) | collective-permute-done | bytes 98336 | tf_op jit(solution)/shard_map/ppermute | solution.py:391
  31.4 3.2 %collective-permute-start.10 = (bf16[512,256]{1,0:T(8,128)(2,1)S(1)}, bf16[512,256]{1,0:T(8,128)(2,1)S(1)}, u32[]{:S(2)}, u32[]{:S(2)}) collective-permute-start(bf16[512,256]{1,0:T(8,128)(2,1)S(1)} %get-tuple-element.61), channel_id=1, source_target_pairs={{0,30},{2,4},{4,2},{6,8},{8,6},{10,12},{12,10},{14,16},{16,14},{18... | collective-permute-start | bytes 786440 | tf_op jit(solution)/shard_map/ppermute | solution.py:387
  34.6 0.7 %shard_map.67 = bf16[2,32,768]{2,1,0:T(8,128)(2,1)S(1)} custom-call(s32[8]{0:T(128)S(1)} %get-tuple-element.36.spots, bf16[2,32,768]{2,1,0:T(8,128)(2,1)S(1)} %fusion.refs_0_, bf16[2,32,768]{2,1,0:T(8,128)(2,1)S(1)} %collective-permute-done.6.refs_1_, f32[2,64,768]{2,1,0:T(8,128)S(1)} %get-tuple-element.52.refs_2_, ...), custom_call_target="tpu_custom_call" | custom-call | tf_op jit(solution)/shard_map/pallas_call | solution.py:232
  35.4 1.3 %collective-permute-start.9 = (bf16[1,2,32,768]{3,2,1,0:T(8,128)(2,1)S(1)}, bf16[1,2,32,768]{3,2,1,0:T(8,128)(2,1)S(1)}, u32[]{:S(2)}, u32[]{:S(2)}) collective-permute-start(bf16[1,2,32,768]{3,2,1,0:T(8,128)(2,1)S(1)} %bitcast.4), channel_id=1, source_target_pairs={{0,24},{2,26},{4,28},{6,30},{8,16},{10,18},{12,20},{14,22},{16,8},... | collective-permute-start | bytes 294920 | tf_op jit(solution)/shard_map/ppermute | solution.py:391
  36.6 0.0 collective-permute-start.8
  36.6 3.2 %collective-permute-start.7 = (bf16[1,2,32,768]{3,2,1,0:T(8,128)(2,1)S(1)}, bf16[1,2,32,768]{3,2,1,0:T(8,128)(2,1)S(1)}, u32[]{:S(2)}, u32[]{:S(2)}) collective-permute-start(bf16[1,2,32,768]{3,2,1,0:T(8,128)(2,1)S(1)} %bitcast.6), channel_id=1, source_target_pairs={{0,8},{2,10},{4,12},{6,14},{8,0},{10,2},{12,4},{14,6},{16,24},{18,... | collective-permute-start | bytes 294920 | tf_op jit(solution)/shard_map/ppermute | solution.py:391
  39.8 2.7 %shard_map.68.refs_1_ = f32[512,256]{1,0:T(8,128)S(1)} custom-call(s32[8]{0:T(128)S(1)} %get-tuple-element.36.spots, s32[1,32]{1,0:T(1,128)S(1)} %bitcast.9, bf16[512,512]{1,0:T(8,128)(2,1)S(1)} %get-tuple-element.41.q_ref, bf16[1536,256]{1,0:T(8,128)(2,1)S(1)} %collective-permute-done.5.far, f32[512,512]{1,0:T(8,128)S(1)} %get-tuple-element.58.rest_0_.mixed_ref, ...), custom_call_target="tpu_custom_call" | custom-call | tf_op jit(solution)/shard_map/pallas_call | solution.py:339
  42.6 0.0 collective-permute-done.10.last
  42.6 2.7 %shard_map.69.refs_2_ = f32[512,256]{1,0:T(8,128)S(1)} custom-call(s32[8]{0:T(128)S(1)} %get-tuple-element.36.spots, s32[1,32]{1,0:T(1,128)S(1)} %bitcast.10, bf16[512,512]{1,0:T(8,128)(2,1)S(1)} %get-tuple-element.41.q_ref, bf16[1536,256]{1,0:T(8,128)(2,1)S(1)} %collective-permute-done.5.far, bf16[512,256]{1,0:T(8,128)(2,1)S(1)} %collective-permute-done.10.last, ...), custom_call_target="tpu_custom_call" | custom-call | tf_op jit(solution)/shard_map/pallas_call | solution.py:339
  45.3 0.0 collective-permute-done.9
  45.3 0.8 %collective-permute-done.8 = bf16[1,2,32,768]{3,2,1,0:T(8,128)(2,1)S(1)} collective-permute-done((bf16[1,2,32,768]{3,2,1,0:T(8,128)(2,1)S(1)}, bf16[1,2,32,768]{3,2,1,0:T(8,128)(2,1)S(1)}, u32[]{:S(2)}, u32[]{:S(2)}) %collective-permute-start.8) | collective-permute-done | bytes 98336 | tf_op jit(solution)/shard_map/ppermute | solution.py:391
  46.1 0.0 collective-permute-done.7
  46.2 0.1 collective-permute-start.11
  46.2 0.7 %shard_map.70.refs_0_ = f32[512,512]{1,0:T(8,128)S(1)} custom-call(bf16[512,512]{1,0:T(8,128)(2,1)S(1)} %get-tuple-element.41.q_ref, bf16[4,2,32,768]{3,2,1,0:T(8,128)(2,1)S(1)} %constant_dynamic-update-slice_fusion.w_ref), custom_call_target="tpu_custom_call" | custom-call | tf_op jit(solution)/shard_map/pallas_call | solution.py:365
  46.9 1.0 %collective-permute-done.11.w_ref = bf16[4,2,32,768]{3,2,1,0:T(8,128)(2,1)S(1)} collective-permute-done((bf16[4,2,32,768]{3,2,1,0:T(8,128)(2,1)S(1)}, bf16[4,2,32,768]{3,2,1,0:T(8,128)(2,1)S(1)}, u32[]{:S(2)}, u32[]{:S(2)}) %collective-permute-start.11) | collective-permute-done | bytes 393248 | tf_op jit(solution)/shard_map/ppermute | solution.py:384
  47.9 1.5 %shard_map.71 = bf16[512,512]{1,0:T(8,128)(2,1)} custom-call(bf16[512,512]{1,0:T(8,128)(2,1)S(1)} %get-tuple-element.41.q_ref, bf16[4,2,32,768]{3,2,1,0:T(8,128)(2,1)S(1)} %collective-permute-done.11.w_ref, f32[512,512]{1,0:T(8,128)S(1)} %shard_map.70.refs_0_, f32[512,256]{1,0:T(8,128)S(1)} %shard_map.68.refs_1_, f32[512,256]{1,0:T(8,128)S(1)} %shard_map.69.refs_2_), custom_call_target="tpu_custom_call" | custom-call | tf_op jit(solution)/shard_map/pallas_call | solution.py:365
  (5 shorter events, 0.1 us)
Async XLA Ops:
  2.6 11.8 %collective-permute-start = (bf16[1536,512]{1,0:T(8,128)(2,1)S(1)}, bf16[1536,512]{1,0:T(8,128)(2,1)S(1)}, u32[]{:S(2)}, u32[]{:S(2)}) collective-permute-start(bf16[1536,512]{1,0:T(8,128)(2,1)S(1)} %get-tuple-element.37.own), channel_id=1, source_target_pairs={{0,2},{2,0},{4,6},{6,4},{8,10},{10,8},{12,14},{14,12},{16,18},{18,... | collective-permute-start | bytes 4718600 | tf_op jit(solution)/shard_map/ppermute | solution.py:384
  3.1 23.0 %collective-permute-start.5 = (bf16[1536,256]{1,0:T(8,128)(2,1)S(1)}, bf16[1536,256]{1,0:T(8,128)(2,1)S(1)}, u32[]{:S(2)}, u32[]{:S(2)}) collective-permute-start(bf16[1536,256]{1,0:T(8,128)(2,1)S(1)} %get-tuple-element.46), channel_id=1, source_target_pairs={{0,30},{2,4},{4,2},{6,8},{8,6},{10,12},{12,10},{14,16},{16,14},{18... | collective-permute-start | bytes 2359304 | tf_op jit(solution)/shard_map/ppermute | solution.py:387
  8.8 5.7 %collective-permute-start.1 = (bf16[2,64,768]{2,1,0:T(8,128)(2,1)S(1)}, bf16[2,64,768]{2,1,0:T(8,128)(2,1)S(1)}, u32[]{:S(2)}, u32[]{:S(2)}) collective-permute-start(bf16[2,64,768]{2,1,0:T(8,128)(2,1)S(1)} %get-tuple-element.39), channel_id=1, source_target_pairs={{0,1},{1,0},{2,3},{3,2},{4,5},{5,4},{6,7},{7,6},{8,9},{9,8},{10,11... | collective-permute-start | bytes 589832 | tf_op jit(solution)/shard_map/ppermute | solution.py:394
  14.4 6.8 %copy-start = (s32[32]{0:T(128)S(1)}, s32[32]{0:T(128)}, u32[]{:S(2)}) copy-start(s32[32]{0:T(128)} %param.11) | copy-start | bytes 388
  16.7 9.4 %collective-permute-start.4 = (bf16[1,2,32,768]{3,2,1,0:T(8,128)(2,1)S(1)}, bf16[1,2,32,768]{3,2,1,0:T(8,128)(2,1)S(1)}, u32[]{:S(2)}, u32[]{:S(2)}) collective-permute-start(bf16[1,2,32,768]{3,2,1,0:T(8,128)(2,1)S(1)} %get-tuple-element.67), channel_id=1, source_target_pairs={{0,24},{2,26},{4,28},{6,30},{8,16},{10,18},{12,20},{14,22},{16,8},... | collective-permute-start | bytes 294920 | tf_op jit(solution)/shard_map/ppermute | solution.py:391
  18.6 8.1 %collective-permute-start.3 = (bf16[1,2,32,768]{3,2,1,0:T(8,128)(2,1)S(1)}, bf16[1,2,32,768]{3,2,1,0:T(8,128)(2,1)S(1)}, u32[]{:S(2)}, u32[]{:S(2)}) collective-permute-start(bf16[1,2,32,768]{3,2,1,0:T(8,128)(2,1)S(1)} %get-tuple-element.68), channel_id=1, source_target_pairs={{0,16},{2,18},{4,20},{6,22},{8,24},{10,26},{12,28},{14,30},{16,0},... | collective-permute-start | bytes 294920 | tf_op jit(solution)/shard_map/ppermute | solution.py:391
  18.6 8.1 %collective-permute-start.2 = (bf16[1,2,32,768]{3,2,1,0:T(8,128)(2,1)S(1)}, bf16[1,2,32,768]{3,2,1,0:T(8,128)(2,1)S(1)}, u32[]{:S(2)}, u32[]{:S(2)}) collective-permute-start(bf16[1,2,32,768]{3,2,1,0:T(8,128)(2,1)S(1)} %get-tuple-element.69), channel_id=1, source_target_pairs={{0,8},{2,10},{4,12},{6,14},{8,0},{10,2},{12,4},{14,6},{16,24},{18,... | collective-permute-start | bytes 294920 | tf_op jit(solution)/shard_map/ppermute | solution.py:391
  26.7 4.7 %collective-permute-start.6 = (bf16[2,32,768]{2,1,0:T(8,128)(2,1)S(1)}, bf16[2,32,768]{2,1,0:T(8,128)(2,1)S(1)}, u32[]{:S(2)}, u32[]{:S(2)}) collective-permute-start(bf16[2,32,768]{2,1,0:T(8,128)(2,1)S(1)} %fusion.refs_0_), channel_id=1, source_target_pairs={{0,4},{2,6},{4,0},{6,2},{8,12},{10,14},{12,8},{14,10},{16,20},{18,... | collective-permute-start | bytes 294920 | tf_op jit(solution)/shard_map/ppermute | solution.py:391
  31.4 11.2 %collective-permute-start.10 = (bf16[512,256]{1,0:T(8,128)(2,1)S(1)}, bf16[512,256]{1,0:T(8,128)(2,1)S(1)}, u32[]{:S(2)}, u32[]{:S(2)}) collective-permute-start(bf16[512,256]{1,0:T(8,128)(2,1)S(1)} %get-tuple-element.61), channel_id=1, source_target_pairs={{0,30},{2,4},{4,2},{6,8},{8,6},{10,12},{12,10},{14,16},{16,14},{18... | collective-permute-start | bytes 786440 | tf_op jit(solution)/shard_map/ppermute | solution.py:387
  35.4 10.0 %collective-permute-start.9 = (bf16[1,2,32,768]{3,2,1,0:T(8,128)(2,1)S(1)}, bf16[1,2,32,768]{3,2,1,0:T(8,128)(2,1)S(1)}, u32[]{:S(2)}, u32[]{:S(2)}) collective-permute-start(bf16[1,2,32,768]{3,2,1,0:T(8,128)(2,1)S(1)} %bitcast.4), channel_id=1, source_target_pairs={{0,24},{2,26},{4,28},{6,30},{8,16},{10,18},{12,20},{14,22},{16,8},... | collective-permute-start | bytes 294920 | tf_op jit(solution)/shard_map/ppermute | solution.py:391
  36.6 9.5 %collective-permute-start.8 = (bf16[1,2,32,768]{3,2,1,0:T(8,128)(2,1)S(1)}, bf16[1,2,32,768]{3,2,1,0:T(8,128)(2,1)S(1)}, u32[]{:S(2)}, u32[]{:S(2)}) collective-permute-start(bf16[1,2,32,768]{3,2,1,0:T(8,128)(2,1)S(1)} %bitcast.5), channel_id=1, source_target_pairs={{0,16},{2,18},{4,20},{6,22},{8,24},{10,26},{12,28},{14,30},{16,0},... | collective-permute-start | bytes 294920 | tf_op jit(solution)/shard_map/ppermute | solution.py:391
  36.6 9.5 %collective-permute-start.7 = (bf16[1,2,32,768]{3,2,1,0:T(8,128)(2,1)S(1)}, bf16[1,2,32,768]{3,2,1,0:T(8,128)(2,1)S(1)}, u32[]{:S(2)}, u32[]{:S(2)}) collective-permute-start(bf16[1,2,32,768]{3,2,1,0:T(8,128)(2,1)S(1)} %bitcast.6), channel_id=1, source_target_pairs={{0,8},{2,10},{4,12},{6,14},{8,0},{10,2},{12,4},{14,6},{16,24},{18,... | collective-permute-start | bytes 294920 | tf_op jit(solution)/shard_map/ppermute | solution.py:391
  46.2 1.8 %collective-permute-start.11 = (bf16[4,2,32,768]{3,2,1,0:T(8,128)(2,1)S(1)}, bf16[4,2,32,768]{3,2,1,0:T(8,128)(2,1)S(1)}, u32[]{:S(2)}, u32[]{:S(2)}) collective-permute-start(bf16[4,2,32,768]{3,2,1,0:T(8,128)(2,1)S(1)} %constant_dynamic-update-slice_fusion.w_ref), channel_id=1, source_target_pairs={{0,2},{2,0},{4,6},{6,4},{8,10},{10,8},{12,14},{14,12},{16,18},{18,... | collective-permute-start | bytes 1179656 | tf_op jit(solution)/shard_map/ppermute | solution.py:384

commit v5 on v4

--- a/solution.py
+++ b/solution.py
@@ -138,8 +138,8 @@
 
 def grads_kernel(spots, own, mate, own_w, sent_w, grad_ref):
     tokens = own.shape[0] // 3
-    memories = own_w.shape[0]
-    hidden = 2 * own_w.shape[1]
+    memories, quarter, _ = own_w.shape
+    hidden = 2 * quarter
     for memory in range(memories):
         features = pl.ds(memory * DM, DM)
         weights = jnp.concatenate([own_w[memory], sent_w[memory]], axis=0)
@@ -150,17 +150,17 @@
         for side in (own, mate):
             key = side[pl.ds(0, tokens), features]
             scaled = side[pl.ds(2 * tokens, tokens), features]
-            gate_up = dot_nt(key, gate_up_w)
-            gate, up = gate_up[:, :hidden], gate_up[:, hidden:]
+            gate_up = dot_nt(gate_up_w, key)
+            gate, up = gate_up[:hidden], gate_up[hidden:]
             sigmoid = jax.nn.sigmoid(gate)
             swish = gate * sigmoid
             slope = sigmoid * (1.0 + gate * (1.0 - sigmoid))
-            back = -dot_nt(scaled, out_w)
+            back = -dot_nt(out_w, scaled)
             pair = jnp.concatenate(
-                [(back * up * slope).astype(BF16), (back * swish).astype(BF16)], axis=1
+                [(back * up * slope).astype(BF16), (back * swish).astype(BF16)], axis=0
             )
-            grad_pair += dot_tn(pair, key)
-            grad_out -= dot_tn((swish * up).astype(BF16), scaled)
+            grad_pair += dot_nn(pair, key)
+            grad_out -= dot_nn((swish * up).astype(BF16), scaled)
         found = (grad_pair[:hidden], grad_pair[hidden:], grad_out)
         for part, grad in enumerate(found):
             grad = grad.astype(BF16)
@@ -169,17 +169,20 @@
                 grad_ref[memory, :, columns] = grad
             else:
                 blocks, _, rows, _ = grad_ref.shape
+                rows //= 2
                 for block in range(blocks):
-                    piece = grad[block * rows : (block + 1) * rows]
-                    grad_ref[spots[3] ^ block, memory, :, columns] = piece
+                    for half in range(2):
+                        first = half * quarter + block * rows
+                        piece = grad[first : first + rows]
+                        owned = pl.ds(half * rows, rows)
+                        grad_ref[spots[3] ^ block, memory, owned, columns] = piece
 
 
 def half_grads(spots, blocks, own, mate, own_w, sent_w):
     memories, quarter, width = own_w.shape
-    hidden = 2 * quarter
-    rows = hidden // blocks
+    rows = quarter // blocks
     placed = rows % 16 == 0
-    shape = (blocks, memories, rows, width) if placed else (memories, hidden, width)
+    shape = (blocks, memories, 2 * rows, width) if placed else (memories, 2 * quarter, width)
     grads = pl.pallas_call(
         grads_kernel,
         out_shape=jax.ShapeDtypeStruct(shape, BF16),
@@ -189,48 +192,42 @@
     )(spots, own, mate, own_w, sent_w)
     if placed:
         return grads
-    grads = grads.reshape(memories, blocks, rows, width).transpose(1, 0, 2, 3)
+    grads = grads.reshape(memories, 2, blocks, rows, width).transpose(2, 0, 1, 3, 4)
+    grads = grads.reshape(blocks, memories, 2 * rows, width)
     return jnp.take(grads, jnp.arange(blocks, dtype=jnp.int32) ^ spots[3], axis=0)
 
 
 def update_kernel(step_rate, parts, spots, *refs):
     *grads, exact, sent, new_ref = refs
-    rows = new_ref.shape[1]
-    total = grads[0][...].astype(F32)
-    for part in grads[1:]:
-        total += part[...].astype(F32)
-    if sent is None:
-        before = exact[...]
+    rows = new_ref.shape[1] // 2
+    if exact.shape[1] == rows:
+        here = pl.ds(0, rows)
     else:
-        held = exact.shape[1]
-        first = spots[3] * rows
-        near = pl.multiple_of(jnp.minimum(first, held - rows), rows)
-        away = pl.multiple_of(jnp.maximum(first - held, 0), rows)
-        before = jnp.where(
-            first < held, exact[:, pl.ds(near, rows), :], sent[:, pl.ds(away, rows), :].astype(F32)
+        here = pl.ds(pl.multiple_of(spots[3] * rows, rows), rows)
+    for half, held in enumerate((exact, sent)):
+        owned = pl.ds(half * rows, rows)
+        total = grads[0][:, owned, :].astype(F32)
+        for part in grads[1:]:
+            total += part[:, owned, :].astype(F32)
+        before = held[:, here, :].astype(F32)
+        stepped = before - total * step_rate
+        for block in range(3):
+            columns = slice(block * DM, (block + 1) * DM)
+            old, new = before[..., columns], stepped[..., columns]
+            old_norm = jnp.sqrt(jnp.sum(old * old, axis=-1, keepdims=True))
+            new_norm = jnp.sqrt(jnp.sum(new * new, axis=-1, keepdims=True) + NORM_EPS)
+            new_ref[:, owned, columns] = (new * (old_norm / new_norm)).astype(BF16)
+
+
+def update_rows(spots, step_rate, grads, exact, sent):
+    rows = grads[0].shape[1] // 2
+    if rows % 16:
+        exact, sent = (
+            lax.dynamic_slice_in_dim(held, spots[3] * rows, rows, 1) for held in (exact, sent)
         )
-    stepped = before - total * step_rate
-    for block in range(3):
-        columns = slice(block * DM, (block + 1) * DM)
-        old, new = before[..., columns], stepped[..., columns]
-        old_norm = jnp.sqrt(jnp.sum(old * old, axis=-1, keepdims=True))
-        new_norm = jnp.sqrt(jnp.sum(new * new, axis=-1, keepdims=True) + NORM_EPS)
-        new_ref[:, :, columns] = (new * (old_norm / new_norm)).astype(BF16)
-
-
-def update_rows(spots, step_rate, grads, exact, sent):
-    rows = grads[0].shape[1]
-    body = functools.partial(update_kernel, step_rate, len(grads))
     given = list(grads) + [exact, sent]
-    if rows % 16:
-        whole = jnp.concatenate([exact, sent.astype(F32)], axis=1)
-        given[-2:] = [lax.dynamic_slice_in_dim(whole, spots[3] * rows, rows, 1)]
-
-        def body(spots, *refs):
-            update_kernel(step_rate, len(grads), spots, *refs[:-1], None, refs[-1])
-
     return pl.pallas_call(
-        body,
+        functools.partial(update_kernel, step_rate, len(grads)),
         out_shape=jax.ShapeDtypeStruct(grads[0].shape, BF16),
         in_specs=[in_smem()] + in_vmem(len(given)),
         out_specs=in_vmem(1)[0],
@@ -250,92 +247,97 @@
     return start, stop
 
 
-def inside(base, count, start, stop):
-    place = base + lax.broadcasted_iota(jnp.int32, (1, count), 1)
-    return (place >= start) & (place < stop)
+def inside(base, start, stop):
+    place = base + lax.broadcasted_iota(jnp.int32, start.shape, 1)
+    return jnp.where((place >= start) & (place < stop), 0.0, MASKED)
 
 
 SCORE_SCALE = math.log2(math.e) / math.sqrt(HD)
 
 
-def near_kernel(spots, lengths, q_ref, own, mate, mixed_ref, peak_ref, sum_ref):
+def lanes_wide(column, count):
+    return jnp.concatenate([column] * (count // HD), axis=1) if count > HD else column
+
+
+def summing(values):
+    return jnp.concatenate([values, jnp.ones_like(values)], axis=1)
+
+
+def near_kernel(spots, lengths, q_ref, own, mate, mixed_ref, peak_ref, sum_ref, bound_ref):
     tokens, width = q_ref.shape
-    start, stop = view_bounds(lengths, spots[0], tokens)
-    block_rows = tokens // 2
-    for block in range(2):
+    bounds = [
+        jnp.broadcast_to(bound, (tokens, HD)) for bound in view_bounds(lengths, spots[0], tokens)
+    ]
+    bound_ref[0], bound_ref[1] = bounds
+    block_rows = tokens // 4
+    for block in range(4):
         rows = slice(block * block_rows, (block + 1) * block_rows)
-        masks = [inside(spots[i], tokens, start[rows], stop[rows]) for i in range(2)]
+        start, stop = (lanes_wide(bound[rows], tokens) for bound in bounds)
+        shifts = [inside(spots[i], start, stop) for i in range(2)]
         for head in range(width // HD):
             lanes = pl.ds(head * HD, HD)
             query = q_ref[rows, lanes]
             scores = [
-                jnp.where(mask, dot_nt(query, side[:tokens, lanes]) * SCORE_SCALE, MASKED)
-                for mask, side in zip(masks, (own, mate))
+                dot_nt(query, side[:tokens, lanes]) + shift
+                for shift, side in zip(shifts, (own, mate))
             ]
-            peak = functools.reduce(
-                jnp.maximum, [jnp.max(s, axis=1, keepdims=True) for s in scores]
+            peak = jnp.max(jnp.maximum(*scores), axis=1, keepdims=True)
+            mixed = sum(
+                dot_nn(
+                    jnp.exp2((score - peak) * SCORE_SCALE).astype(BF16),
+                    summing(side[pl.ds(tokens, tokens), lanes]),
+                )
+                for score, side in zip(scores, (own, mate))
             )
-            weights = [jnp.exp2(s - peak) for s in scores]
-            peak_ref[rows, head : head + 1] = peak
-            sum_ref[rows, head : head + 1] = sum(
-                jnp.sum(w, axis=1, keepdims=True) for w in weights
-            )
-            mixed_ref[rows, lanes] = sum(
-                dot_nn(w.astype(BF16), side[pl.ds(tokens, tokens), lanes])
-                for w, side in zip(weights, (own, mate))
-            )
-
-
-def far_kernel(
-    memory, spots, lengths, q_ref, far, last, mixed_ref, peak_ref, sum_ref, out_ref
-):
+            mixed_ref[rows, lanes] = mixed[:, :HD]
+            peak_ref[head, rows] = jnp.broadcast_to(peak, (block_rows, HD))
+            sum_ref[head, rows] = mixed[:, HD:]
+
+
+def far_kernel(memory, spots, q_ref, far, last, mixed_ref, peak_ref, sum_ref, bound_ref, out_ref):
     tokens, _ = q_ref.shape
-    start, stop = view_bounds(lengths, spots[0], tokens)
     far_k = far.at[pl.ds(2 * memory * tokens, tokens)]
     far_v = last if last is not None else far.at[pl.ds((2 * memory + 1) * tokens, tokens)]
-    block_rows = tokens // 2
-    for block in range(2):
+    block_rows = tokens // 4
+    for block in range(4):
         rows = slice(block * block_rows, (block + 1) * block_rows)
-        mask = inside(spots[2], tokens, start[rows], stop[rows])
+        start, stop = (lanes_wide(bound_ref[i, rows], tokens) for i in range(2))
+        shift = inside(spots[2], start, stop)
         for step in range(DM // HD):
             lanes = pl.ds(step * HD, HD)
             head = memory * (DM // HD) + step
             across = pl.ds(head * HD, HD)
-            scores = dot_nt(q_ref[rows, across], far_k[:, lanes]) * SCORE_SCALE
-            scores = jnp.where(mask, scores, MASKED)
-            before = peak_ref[rows, head : head + 1]
+            scores = dot_nt(q_ref[rows, across], far_k[:, lanes]) + shift
+            before = peak_ref[head, rows]
             peak = jnp.maximum(before, jnp.max(scores, axis=1, keepdims=True))
-            weights = jnp.exp2(scores - peak)
-            shrink = jnp.exp2(before - peak)
-            total = sum_ref[rows, head : head + 1] * shrink + jnp.sum(
-                weights, axis=1, keepdims=True
-            )
-            mixed = mixed_ref[rows, across] * shrink + dot_nn(
-                weights.astype(BF16), far_v[:, lanes]
-            )
-            out_ref[rows, lanes] = mixed / total
+            weights = jnp.exp2((scores - lanes_wide(peak, tokens)) * SCORE_SCALE)
+            shrink = jnp.exp2((before - peak) * SCORE_SCALE)
+            mixed = dot_nn(weights.astype(BF16), summing(far_v[:, lanes]))
+            total = sum_ref[head, rows] * shrink + mixed[:, HD:]
+            out_ref[rows, lanes] = (mixed_ref[rows, across] * shrink + mixed[:, :HD]) / total
 
 
 def attend_near(spots, lengths, queries, own, mate):
     tokens, width = queries.shape
-    stats = jax.ShapeDtypeStruct((tokens, width // HD), F32)
+    stats = jax.ShapeDtypeStruct((width // HD, tokens, HD), F32)
+    bounds = jax.ShapeDtypeStruct((2, tokens, HD), jnp.int32)
     return pl.pallas_call(
         near_kernel,
-        out_shape=(jax.ShapeDtypeStruct(queries.shape, F32), stats, stats),
+        out_shape=(jax.ShapeDtypeStruct(queries.shape, F32), stats, stats, bounds),
         in_specs=[in_smem()] + in_vmem(4),
-        out_specs=tuple(in_vmem(3)),
+        out_specs=tuple(in_vmem(4)),
         compiler_params=params(),
     )(spots, lengths, queries, own, mate)
 
 
-def attend_far(memory, spots, lengths, queries, far, last, near):
+def attend_far(memory, spots, queries, far, last, near):
     if last is None:
 
-        def body(spots, lengths, q_ref, far, *rest):
-            far_kernel(memory, spots, lengths, q_ref, far, None, *rest)
+        def body(spots, q_ref, far, *rest):
+            far_kernel(memory, spots, q_ref, far, None, *rest)
     else:
         body = functools.partial(far_kernel, memory)
-    given = (lengths, queries, far) + (() if last is None else (last,)) + tuple(near)
+    given = (queries, far) + (() if last is None else (last,)) + tuple(near)
     return pl.pallas_call(
         body,
         out_shape=jax.ShapeDtypeStruct((queries.shape[0], DM), F32),
@@ -384,7 +386,14 @@
         return lax.ppermute(x, "tok", [(i, i ^ 1) for i in range(devices)])
 
     def to_far(x):
-        return lax.ppermute(x, "tok", [(i, (i + i % 2 * 2 - 1) % devices) for i in range(devices)])
+        pairs = [
+            (i * planes + p, (i + i % 2 * 2 - 1) * planes + p)
+            for i in range(1, devices - 1)
+            for p in range(planes)
+        ]
+        for i in (0, devices - 1):
+            pairs += [(i * planes + p, i * planes + planes - 1 - p) for p in range(planes)]
+        return lax.ppermute(x, ("tok", "mem"), pairs)
 
     def to_chip(x, flip):
         pairs = [(i, (((i // CORES) ^ flip) * CORES) + i % CORES) for i in range(devices)]
@@ -410,11 +419,11 @@
         held = held.reshape((radix, stride // digits[0]) + held.shape[1:])
         came = [to_chip(held[step], step * stride) for step in range(1, radix)]
         if place == 0:
-            came, near, far = lax.optimization_barrier((came, near, far))
+            came, near = lax.optimization_barrier((came, near))
         held = sum([part.astype(F32) for part in came], held[0].astype(F32)).astype(BF16)
     held = held[0]
     came = [to_chip(held, step) for step in range(1, digits[0])]
-    came, last = lax.optimization_barrier((came, last))
+    came, last, far = lax.optimization_barrier((came, last, far))
     last = to_far(last)
     all_tokens = tokens * devices
     fresh = update_rows(
@@ -428,7 +437,7 @@
         if stride == digits[0]:
             gathered, near = lax.optimization_barrier((gathered, near))
             attended = [
-                attend_far(m, spots, lengths, q, far, last if m == memories - 1 else None, near)
+                attend_far(m, spots, q, far, last if m == memories - 1 else None, near)
                 for m in range(memories)
             ]
             came, attended = lax.optimization_barrier((came, attended))

time: 49.6 us -> 48.1 us (0.970)
  waiting for transfers between devices: 9.14 us -> 19.6 us
  starting transfers between devices: 21.9 us -> 12.8 us
  Pallas kernels: 18.2 us -> 15.2 us
    ppermute x7, waiting for transfers between devices: 3.97 us -> 13.2 us  [to_chip(): return lax.ppermute(x, 'tok', pairs)]
    ppermute x2, starting transfers between devices: 8.87 us -> 0.58 us  [to_far(): return lax.ppermute(x, ('tok', 'mem'), pairs)]
    pallas_call x2, Pallas kernels: 5.46 us -> 3.44 us  [attend_far(): pl.pallas_call(body, out_shape=jax.ShapeDtypeStruct((queries.shape[0], DM...]
    ppermute x7, starting transfers between devices: 10.9 us -> 9.07 us  [to_chip(): return lax.ppermute(x, 'tok', pairs)]
    ppermute x1, waiting for transfers between devices: 4.15 us -> 5.42 us  [to_plane(): return lax.ppermute(x, 'mem', [(p, planes - 1 - p) for p in range(planes)])]
    ppermute x1, starting transfers between devices: 1.52 us -> 2.59 us  [to_plane(): return lax.ppermute(x, 'mem', [(p, planes - 1 - p) for p in range(planes)])]
    pallas_call x1, Pallas kernels: 4.95 us -> 4.19 us  [attend_near(): pl.pallas_call(near_kernel, out_shape=(jax.ShapeDtypeStruct(queries.shape...]
  transfers between devices with their start and end apart: 12 -> 12, of which waited for: 5 -> 7; matrix products, arithmetic and copies ran while one was open for 0% -> 0% of each run, Pallas kernels for 29% -> 23%
where the time goes in v5:
time: 48.1 us; the launch traced here: 47.9 us
  waiting for transfers between devices  19.6 us (41%)
  Pallas kernels  15.2 us (32%)
  starting transfers between devices  12.8 us (27%)
    ppermute x7, waiting for transfers between devices, to_chip(): return lax.ppermute(x, 'tok', pairs)  13.2 us
    ppermute x7, starting transfers between devices, to_chip(): return lax.ppermute(x, 'tok', pairs)  9.07 us
    ppermute x1, waiting for transfers between devices, to_plane(): return lax.ppermute(x, 'mem', [(p, planes - 1 - p) for p in range(planes)])  5.42 us
    pallas_call x1, Pallas kernels, attend_near(): pl.pallas_call(near_kernel, out_shape=(jax.ShapeDtypeStruct(queries.shape...  4.19 us
    pallas_call x2, Pallas kernels, attend_far(): pl.pallas_call(body, out_shape=jax.ShapeDtypeStruct((queries.shape[0], DM...  3.44 us
    pallas_call x1, Pallas kernels, stage(): pl.pallas_call(functools.partial(stage_kernel, blocks), out_shape=(jax.Sh...  2.6 us
    ppermute x1, starting transfers between devices, to_plane(): return lax.ppermute(x, 'mem', [(p, planes - 1 - p) for p in range(planes)])  2.59 us
    pallas_call x2, Pallas kernels, read_half(): pl.pallas_call(functools.partial(read_kernel, len(before)), out_shape=jax...  2.2 us
  transfers between devices with their start and end apart: 12, of which 7 were waited for; matrix products, arithmetic and copies ran while one was open for 0% of the time, Pallas kernels for 23%

profile of v5, /device:TPU:0, one launch (start us, length us, event | category | flops | bytes accessed | tf_op | source)
XLA Modules:
  0.0 47.9 jit_solution(5921606299920843960)
XLA Ops:
  0.0 2.6 %shard_map.64 = (s32[8]{0:T(128)S(1)}, bf16[512,512]{1,0:T(8,128)(2,1)S(1)}, bf16[1536,512]{1,0:T(8,128)(2,1)S(1)}, bf16[1536,256]{1,0:T(8,128)(2,1)S(1)}, bf16[...) custom-call(bf16[512,512]{1,0:T(8,128)(2,1)} %q_any.1, ...), custom_call_target="tpu_custom_call" | custom-call | tf_op jit(solution)/shard_map/pallas_call | solution.py:116
  2.6 0.5 %collective-permute-start = (bf16[1536,512]{1,0:T(8,128)(2,1)S(1)}, bf16[1536,512]{1,0:T(8,128)(2,1)S(1)}, u32[]{:S(2)}, u32[]{:S(2)}) collective-permute-start(bf16[1536,512]{1,0:T(8,128)(2,1)S(1)} %get-tuple-element.40.own), channel_id=1, source_target_pairs={{0,2},{2,0},{4,6},{6,4},{8,10},{10,8},{12,14},{14,12},{16,18},{18,... | collective-permute-start | bytes 4718600 | tf_op jit(solution)/shard_map/ppermute | solution.py:386
  3.1 2.6 %collective-permute-start.1 = (bf16[2,64,768]{2,1,0:T(8,128)(2,1)S(1)}, bf16[2,64,768]{2,1,0:T(8,128)(2,1)S(1)}, u32[]{:S(2)}, u32[]{:S(2)}) collective-permute-start(bf16[2,64,768]{2,1,0:T(8,128)(2,1)S(1)} %get-tuple-element.42), channel_id=1, source_target_pairs={{0,1},{1,0},{2,3},{3,2},{4,5},{5,4},{6,7},{7,6},{8,9},{9,8},{10,11... | collective-permute-start | bytes 589832 | tf_op jit(solution)/shard_map/ppermute | solution.py:403
  5.7 0.1 collective-permute-start.6
  5.8 5.4 %collective-permute-done.1.sent_w.refs_3_ = bf16[2,64,768]{2,1,0:T(8,128)(2,1)S(1)} collective-permute-done((bf16[2,64,768]{2,1,0:T(8,128)(2,1)S(1)}, bf16[2,64,768]{2,1,0:T(8,128)(2,1)S(1)}, u32[]{:S(2)}, u32[]{:S(2)}) %collective-permute-start.1) | collective-permute-done | bytes 196640 | tf_op jit(solution)/shard_map/ppermute | solution.py:403
  11.2 0.0 collective-permute-done.mate
  11.2 0.0 copy-start
  11.2 2.1 %shard_map.65 = bf16[4,2,32,768]{3,2,1,0:T(8,128)(2,1)S(1)} custom-call(s32[8]{0:T(128)S(1)} %get-tuple-element.39.spots, bf16[1536,512]{1,0:T(8,128)(2,1)S(1)} %get-tuple-element.40.own, bf16[1536,512]{1,0:T(8,128)(2,1)S(1)} %collective-permute-done.mate, bf16[2,64,768]{2,1,0:T(8,128)(2,1)S(1)} %get-tuple-element.41.own_w, ...), custom_call_target="tpu_custom_call" | custom-call | tf_op jit(solution)/shard_map/pallas_call | solution.py:186
  13.4 1.9 %collective-permute-start.2 = (bf16[1,2,32,768]{3,2,1,0:T(8,128)(2,1)S(1)}, bf16[1,2,32,768]{3,2,1,0:T(8,128)(2,1)S(1)}, u32[]{:S(2)}, u32[]{:S(2)}) collective-permute-start(bf16[1,2,32,768]{3,2,1,0:T(8,128)(2,1)S(1)} %get-tuple-element.75), channel_id=1, source_target_pairs={{0,8},{2,10},{4,12},{6,14},{8,0},{10,2},{12,4},{14,6},{16,24},{18,... | collective-permute-start | bytes 294920 | tf_op jit(solution)/shard_map/ppermute | solution.py:400
  15.2 2.6 %collective-permute-start.3 = (bf16[1,2,32,768]{3,2,1,0:T(8,128)(2,1)S(1)}, bf16[1,2,32,768]{3,2,1,0:T(8,128)(2,1)S(1)}, u32[]{:S(2)}, u32[]{:S(2)}) collective-permute-start(bf16[1,2,32,768]{3,2,1,0:T(8,128)(2,1)S(1)} %get-tuple-element.74), channel_id=1, source_target_pairs={{0,16},{2,18},{4,20},{6,22},{8,24},{10,26},{12,28},{14,30},{16,0},... | collective-permute-start | bytes 294920 | tf_op jit(solution)/shard_map/ppermute | solution.py:400
  17.8 0.0 collective-permute-start.4
  17.8 0.0 copy-done
  17.8 4.2 %shard_map.66 = (f32[512,512]{1,0:T(8,128)S(1)}, f32[4,512,128]{2,1,0:T(8,128)S(1)}, f32[4,512,128]{2,1,0:T(8,128)S(1)}, s32[2,512,128]{2,1,0:T(8,128)S(1)}) custom-call(s32[8]{0:T(128)S(1)} %get-tuple-element.39.spots, s32[1,32]{1,0:T(1,128)S(1)} %bitcast.8, bf16[512,512]{1,0:T(8,128)(2,1)S(1)} %get-tuple-element.44.q_ref, ...), custom_call_target="tpu_custom_call" | custom-call | tf_op jit(solution)/shard_map/pallas_call | solution.py:324
  22.0 0.0 collective-permute-done.2
  22.0 2.7 %collective-permute-done.3 = bf16[1,2,32,768]{3,2,1,0:T(8,128)(2,1)S(1)} collective-permute-done((bf16[1,2,32,768]{3,2,1,0:T(8,128)(2,1)S(1)}, bf16[1,2,32,768]{3,2,1,0:T(8,128)(2,1)S(1)}, u32[]{:S(2)}, u32[]{:S(2)}) %collective-permute-start.3) | collective-permute-done | bytes 98336 | tf_op jit(solution)/shard_map/ppermute | solution.py:400
  24.7 2.2 %collective-permute-done.4 = bf16[1,2,32,768]{3,2,1,0:T(8,128)(2,1)S(1)} collective-permute-done((bf16[1,2,32,768]{3,2,1,0:T(8,128)(2,1)S(1)}, bf16[1,2,32,768]{3,2,1,0:T(8,128)(2,1)S(1)}, u32[]{:S(2)}, u32[]{:S(2)}) %collective-permute-start.4) | collective-permute-done | bytes 98336 | tf_op jit(solution)/shard_map/ppermute | solution.py:400
  26.9 0.1 fusion.refs_0_
  27.0 0.1 collective-permute-start.5
  27.1 0.0 collective-permute-done.6.far
  27.1 4.5 %collective-permute-done.5.refs_1_ = bf16[2,32,768]{2,1,0:T(8,128)(2,1)S(1)} collective-permute-done((bf16[2,32,768]{2,1,0:T(8,128)(2,1)S(1)}, bf16[2,32,768]{2,1,0:T(8,128)(2,1)S(1)}, u32[]{:S(2)}, u32[]{:S(2)}) %collective-permute-start.5) | collective-permute-done | bytes 98336 | tf_op jit(solution)/shard_map/ppermute | solution.py:400
  31.6 0.5 %collective-permute-start.10 = (bf16[512,256]{1,0:T(8,128)(2,1)S(1)}, bf16[512,256]{1,0:T(8,128)(2,1)S(1)}, u32[]{:S(2)}, u32[]{:S(2)}) collective-permute-start(bf16[512,256]{1,0:T(8,128)(2,1)S(1)} %get-tuple-element.67), channel_id=1, source_target_pairs={{2,4},{3,5},{4,2},{5,3},{6,8},{7,9},{8,6},{9,7},{10,12},{11,13},{1... | collective-permute-start | bytes 786440 | tf_op jit(solution)/shard_map/ppermute | solution.py:396
  32.2 0.7 %shard_map.67 = bf16[2,32,768]{2,1,0:T(8,128)(2,1)S(1)} custom-call(s32[8]{0:T(128)S(1)} %get-tuple-element.39.spots, bf16[2,32,768]{2,1,0:T(8,128)(2,1)S(1)} %fusion.refs_0_, bf16[2,32,768]{2,1,0:T(8,128)(2,1)S(1)} %collective-permute-done.5.refs_1_, f32[2,64,768]{2,1,0:T(8,128)S(1)} %get-tuple-element.56.refs_2_, ...), custom_call_target="tpu_custom_call" | custom-call | tf_op jit(solution)/shard_map/pallas_call | solution.py:229
  32.9 1.1 %collective-permute-start.7 = (bf16[1,2,32,768]{3,2,1,0:T(8,128)(2,1)S(1)}, bf16[1,2,32,768]{3,2,1,0:T(8,128)(2,1)S(1)}, u32[]{:S(2)}, u32[]{:S(2)}) collective-permute-start(bf16[1,2,32,768]{3,2,1,0:T(8,128)(2,1)S(1)} %bitcast.4), channel_id=1, source_target_pairs={{0,8},{2,10},{4,12},{6,14},{8,0},{10,2},{12,4},{14,6},{16,24},{18,... | collective-permute-start | bytes 294920 | tf_op jit(solution)/shard_map/ppermute | solution.py:400
  34.0 0.1 collective-permute-start.8
  34.1 3.3 %collective-permute-start.9 = (bf16[1,2,32,768]{3,2,1,0:T(8,128)(2,1)S(1)}, bf16[1,2,32,768]{3,2,1,0:T(8,128)(2,1)S(1)}, u32[]{:S(2)}, u32[]{:S(2)}) collective-permute-start(bf16[1,2,32,768]{3,2,1,0:T(8,128)(2,1)S(1)} %bitcast.6), channel_id=1, source_target_pairs={{0,24},{2,26},{4,28},{6,30},{8,16},{10,18},{12,20},{14,22},{16,8},... | collective-permute-start | bytes 294920 | tf_op jit(solution)/shard_map/ppermute | solution.py:400
  37.3 1.7 %shard_map.68.refs_1_ = f32[512,256]{1,0:T(8,128)S(1)} custom-call(s32[8]{0:T(128)S(1)} %get-tuple-element.39.spots, bf16[512,512]{1,0:T(8,128)(2,1)S(1)} %get-tuple-element.44.q_ref, bf16[1536,256]{1,0:T(8,128)(2,1)S(1)} %collective-permute-done.6.far, f32[512,512]{1,0:T(8,128)S(1)} %get-tuple-element.63.rest_0_.mixed_ref, ...), custom_call_target="tpu_custom_call" | custom-call | tf_op jit(solution)/shard_map/pallas_call | solution.py:341
  39.1 0.0 collective-permute-done.10.last
  39.1 1.7 %shard_map.69.refs_2_ = f32[512,256]{1,0:T(8,128)S(1)} custom-call(s32[8]{0:T(128)S(1)} %get-tuple-element.39.spots, bf16[512,512]{1,0:T(8,128)(2,1)S(1)} %get-tuple-element.44.q_ref, bf16[1536,256]{1,0:T(8,128)(2,1)S(1)} %collective-permute-done.6.far, bf16[512,256]{1,0:T(8,128)(2,1)S(1)} %collective-permute-done.10.last, ...), custom_call_target="tpu_custom_call" | custom-call | tf_op jit(solution)/shard_map/pallas_call | solution.py:341
  40.8 0.5 %collective-permute-done.7 = bf16[1,2,32,768]{3,2,1,0:T(8,128)(2,1)S(1)} collective-permute-done((bf16[1,2,32,768]{3,2,1,0:T(8,128)(2,1)S(1)}, bf16[1,2,32,768]{3,2,1,0:T(8,128)(2,1)S(1)}, u32[]{:S(2)}, u32[]{:S(2)}) %collective-permute-start.7) | collective-permute-done | bytes 98336 | tf_op jit(solution)/shard_map/ppermute | solution.py:400
  41.3 3.3 %collective-permute-done.8 = bf16[1,2,32,768]{3,2,1,0:T(8,128)(2,1)S(1)} collective-permute-done((bf16[1,2,32,768]{3,2,1,0:T(8,128)(2,1)S(1)}, bf16[1,2,32,768]{3,2,1,0:T(8,128)(2,1)S(1)}, u32[]{:S(2)}, u32[]{:S(2)}) %collective-permute-start.8) | collective-permute-done | bytes 98336 | tf_op jit(solution)/shard_map/ppermute | solution.py:400
  44.6 0.0 collective-permute-done.9
  44.6 0.1 collective-permute-start.11
  44.7 0.7 %shard_map.70.refs_0_ = f32[512,512]{1,0:T(8,128)S(1)} custom-call(bf16[512,512]{1,0:T(8,128)(2,1)S(1)} %get-tuple-element.44.q_ref, bf16[4,2,32,768]{3,2,1,0:T(8,128)(2,1)S(1)} %constant_dynamic-update-slice_fusion.w_ref), custom_call_target="tpu_custom_call" | custom-call | tf_op jit(solution)/shard_map/pallas_call | solution.py:367
  45.4 1.0 %collective-permute-done.11.w_ref = bf16[4,2,32,768]{3,2,1,0:T(8,128)(2,1)S(1)} collective-permute-done((bf16[4,2,32,768]{3,2,1,0:T(8,128)(2,1)S(1)}, bf16[4,2,32,768]{3,2,1,0:T(8,128)(2,1)S(1)}, u32[]{:S(2)}, u32[]{:S(2)}) %collective-permute-start.11) | collective-permute-done | bytes 393248 | tf_op jit(solution)/shard_map/ppermute | solution.py:386
  46.4 1.5 %shard_map.71 = bf16[512,512]{1,0:T(8,128)(2,1)} custom-call(bf16[512,512]{1,0:T(8,128)(2,1)S(1)} %get-tuple-element.44.q_ref, bf16[4,2,32,768]{3,2,1,0:T(8,128)(2,1)S(1)} %collective-permute-done.11.w_ref, f32[512,512]{1,0:T(8,128)S(1)} %shard_map.70.refs_0_, f32[512,256]{1,0:T(8,128)S(1)} %shard_map.68.refs_1_, f32[512,256]{1,0:T(8,128)S(1)} %shard_map.69.refs_2_), custom_call_target="tpu_custom_call" | custom-call | tf_op jit(solution)/shard_map/pallas_call | solution.py:367
  (5 shorter events, 0.1 us)
Async XLA Ops:
  2.6 8.6 %collective-permute-start = (bf16[1536,512]{1,0:T(8,128)(2,1)S(1)}, bf16[1536,512]{1,0:T(8,128)(2,1)S(1)}, u32[]{:S(2)}, u32[]{:S(2)}) collective-permute-start(bf16[1536,512]{1,0:T(8,128)(2,1)S(1)} %get-tuple-element.40.own), channel_id=1, source_target_pairs={{0,2},{2,0},{4,6},{6,4},{8,10},{10,8},{12,14},{14,12},{16,18},{18,... | collective-permute-start | bytes 4718600 | tf_op jit(solution)/shard_map/ppermute | solution.py:386
  3.1 8.1 %collective-permute-start.1 = (bf16[2,64,768]{2,1,0:T(8,128)(2,1)S(1)}, bf16[2,64,768]{2,1,0:T(8,128)(2,1)S(1)}, u32[]{:S(2)}, u32[]{:S(2)}) collective-permute-start(bf16[2,64,768]{2,1,0:T(8,128)(2,1)S(1)} %get-tuple-element.42), channel_id=1, source_target_pairs={{0,1},{1,0},{2,3},{3,2},{4,5},{5,4},{6,7},{7,6},{8,9},{9,8},{10,11... | collective-permute-start | bytes 589832 | tf_op jit(solution)/shard_map/ppermute | solution.py:403
  5.7 21.4 %collective-permute-start.6 = (bf16[1536,256]{1,0:T(8,128)(2,1)S(1)}, bf16[1536,256]{1,0:T(8,128)(2,1)S(1)}, u32[]{:S(2)}, u32[]{:S(2)}) collective-permute-start(bf16[1536,256]{1,0:T(8,128)(2,1)S(1)} %get-tuple-element.54), channel_id=1, source_target_pairs={{2,4},{3,5},{4,2},{5,3},{6,8},{7,9},{8,6},{9,7},{10,12},{11,13},{1... | collective-permute-start | bytes 2359304 | tf_op jit(solution)/shard_map/ppermute | solution.py:396
  11.2 6.6 %copy-start = (s32[32]{0:T(128)S(1)}, s32[32]{0:T(128)}, u32[]{:S(2)}) copy-start(s32[32]{0:T(128)} %param.11) | copy-start | bytes 388
  13.4 8.7 %collective-permute-start.2 = (bf16[1,2,32,768]{3,2,1,0:T(8,128)(2,1)S(1)}, bf16[1,2,32,768]{3,2,1,0:T(8,128)(2,1)S(1)}, u32[]{:S(2)}, u32[]{:S(2)}) collective-permute-start(bf16[1,2,32,768]{3,2,1,0:T(8,128)(2,1)S(1)} %get-tuple-element.75), channel_id=1, source_target_pairs={{0,8},{2,10},{4,12},{6,14},{8,0},{10,2},{12,4},{14,6},{16,24},{18,... | collective-permute-start | bytes 294920 | tf_op jit(solution)/shard_map/ppermute | solution.py:400
  15.2 9.5 %collective-permute-start.3 = (bf16[1,2,32,768]{3,2,1,0:T(8,128)(2,1)S(1)}, bf16[1,2,32,768]{3,2,1,0:T(8,128)(2,1)S(1)}, u32[]{:S(2)}, u32[]{:S(2)}) collective-permute-start(bf16[1,2,32,768]{3,2,1,0:T(8,128)(2,1)S(1)} %get-tuple-element.74), channel_id=1, source_target_pairs={{0,16},{2,18},{4,20},{6,22},{8,24},{10,26},{12,28},{14,30},{16,0},... | collective-permute-start | bytes 294920 | tf_op jit(solution)/shard_map/ppermute | solution.py:400
  17.8 9.1 %collective-permute-start.4 = (bf16[1,2,32,768]{3,2,1,0:T(8,128)(2,1)S(1)}, bf16[1,2,32,768]{3,2,1,0:T(8,128)(2,1)S(1)}, u32[]{:S(2)}, u32[]{:S(2)}) collective-permute-start(bf16[1,2,32,768]{3,2,1,0:T(8,128)(2,1)S(1)} %get-tuple-element.73), channel_id=1, source_target_pairs={{0,24},{2,26},{4,28},{6,30},{8,16},{10,18},{12,20},{14,22},{16,8},... | collective-permute-start | bytes 294920 | tf_op jit(solution)/shard_map/ppermute | solution.py:400
  27.0 4.7 %collective-permute-start.5 = (bf16[2,32,768]{2,1,0:T(8,128)(2,1)S(1)}, bf16[2,32,768]{2,1,0:T(8,128)(2,1)S(1)}, u32[]{:S(2)}, u32[]{:S(2)}) collective-permute-start(bf16[2,32,768]{2,1,0:T(8,128)(2,1)S(1)} %fusion.refs_0_), channel_id=1, source_target_pairs={{0,4},{2,6},{4,0},{6,2},{8,12},{10,14},{12,8},{14,10},{16,20},{18,... | collective-permute-start | bytes 294920 | tf_op jit(solution)/shard_map/ppermute | solution.py:400
  31.6 7.4 %collective-permute-start.10 = (bf16[512,256]{1,0:T(8,128)(2,1)S(1)}, bf16[512,256]{1,0:T(8,128)(2,1)S(1)}, u32[]{:S(2)}, u32[]{:S(2)}) collective-permute-start(bf16[512,256]{1,0:T(8,128)(2,1)S(1)} %get-tuple-element.67), channel_id=1, source_target_pairs={{2,4},{3,5},{4,2},{5,3},{6,8},{7,9},{8,6},{9,7},{10,12},{11,13},{1... | collective-permute-start | bytes 786440 | tf_op jit(solution)/shard_map/ppermute | solution.py:396
  32.9 8.4 %collective-permute-start.7 = (bf16[1,2,32,768]{3,2,1,0:T(8,128)(2,1)S(1)}, bf16[1,2,32,768]{3,2,1,0:T(8,128)(2,1)S(1)}, u32[]{:S(2)}, u32[]{:S(2)}) collective-permute-start(bf16[1,2,32,768]{3,2,1,0:T(8,128)(2,1)S(1)} %bitcast.4), channel_id=1, source_target_pairs={{0,8},{2,10},{4,12},{6,14},{8,0},{10,2},{12,4},{14,6},{16,24},{18,... | collective-permute-start | bytes 294920 | tf_op jit(solution)/shard_map/ppermute | solution.py:400
  34.0 10.6 %collective-permute-start.8 = (bf16[1,2,32,768]{3,2,1,0:T(8,128)(2,1)S(1)}, bf16[1,2,32,768]{3,2,1,0:T(8,128)(2,1)S(1)}, u32[]{:S(2)}, u32[]{:S(2)}) collective-permute-start(bf16[1,2,32,768]{3,2,1,0:T(8,128)(2,1)S(1)} %bitcast.5), channel_id=1, source_target_pairs={{0,16},{2,18},{4,20},{6,22},{8,24},{10,26},{12,28},{14,30},{16,0},... | collective-permute-start | bytes 294920 | tf_op jit(solution)/shard_map/ppermute | solution.py:400
  34.1 10.5 %collective-permute-start.9 = (bf16[1,2,32,768]{3,2,1,0:T(8,128)(2,1)S(1)}, bf16[1,2,32,768]{3,2,1,0:T(8,128)(2,1)S(1)}, u32[]{:S(2)}, u32[]{:S(2)}) collective-permute-start(bf16[1,2,32,768]{3,2,1,0:T(8,128)(2,1)S(1)} %bitcast.6), channel_id=1, source_target_pairs={{0,24},{2,26},{4,28},{6,30},{8,16},{10,18},{12,20},{14,22},{16,8},... | collective-permute-start | bytes 294920 | tf_op jit(solution)/shard_map/ppermute | solution.py:400
  44.6 1.8 %collective-permute-start.11 = (bf16[4,2,32,768]{3,2,1,0:T(8,128)(2,1)S(1)}, bf16[4,2,32,768]{3,2,1,0:T(8,128)(2,1)S(1)}, u32[]{:S(2)}, u32[]{:S(2)}) collective-permute-start(bf16[4,2,32,768]{3,2,1,0:T(8,128)(2,1)S(1)} %constant_dynamic-update-slice_fusion.w_ref), channel_id=1, source_target_pairs={{0,2},{2,0},{4,6},{6,4},{8,10},{10,8},{12,14},{14,12},{16,18},{18,... | collective-permute-start | bytes 1179656 | tf_op jit(solution)/shard_map/ppermute | solution.py:386

commit v6 on v5

--- a/solution.py
+++ b/solution.py
@@ -58,13 +58,13 @@
 
 
 def stage_kernel(
-    blocks, q_any, k_any, v_any, rates_any, weights_any,
-    spots, q_ref, pack_ref, far_ref, last_ref, w_ref, give_ref, exact_ref,
+    blocks, k_any, v_any, rates_any, weights_any,
+    spots, pack_ref, far_ref, w_ref, give_ref, exact_ref,
     held, rates, sems,
 ):
     spot, plane = lax.axis_index("tok"), lax.axis_index("mem")
     devices, planes = lax.axis_size("tok"), lax.axis_size("mem")
-    tokens, width = q_ref.shape
+    tokens = pack_ref.shape[0] // 3
     memories, hidden, _ = exact_ref.shape
     core, chip = lax.rem(spot, CORES), lax.div(spot, CORES)
     copies = []
@@ -81,10 +81,8 @@
     bring(v_any, pack_ref.at[pl.ds(tokens, tokens)])
     bring(k_any, pack_ref.at[pl.ds(0, tokens)])
     pieces = [part for m in range(memories) for part in ((k_any, m), (v_any, m))]
-    for place, (part, m) in enumerate(pieces):
-        goal = far_ref.at[pl.ds(place * tokens, tokens)] if place < len(pieces) - 1 else last_ref
-        bring(part.at[:, pl.ds(m * DM, DM)], goal)
-    bring(q_any, q_ref)
+    for place, (part, m) in enumerate(pieces[:-1]):
+        bring(part.at[:, pl.ds(m * DM, DM)], far_ref.at[pl.ds(place * tokens, tokens)])
     spots[0] = spot * tokens
     spots[1] = (spot ^ 1) * tokens
     spots[2] = jnp.where(core == 0, spot - 1, spot + 1) * tokens
@@ -110,30 +108,28 @@
         copy.wait()
 
 
-def stage(queries, keys, values, step_sizes, fast_weights, memories, blocks):
-    tokens, width = queries.shape
+def stage(keys, values, step_sizes, fast_weights, memories, blocks):
+    tokens, width = keys.shape
     half = (memories, fast_weights.shape[1] // CORES, 3 * DM)
     return pl.pallas_call(
         functools.partial(stage_kernel, blocks),
         out_shape=(
             jax.ShapeDtypeStruct((8,), jnp.int32),
-            pltpu.VMEM((tokens, width), BF16),
             pltpu.VMEM((3 * tokens, width), BF16),
             pltpu.VMEM(((2 * memories - 1) * tokens, DM), BF16),
-            pltpu.VMEM((tokens, DM), BF16),
             pltpu.VMEM(half, BF16),
             pltpu.VMEM(half, BF16),
             pltpu.VMEM(half, F32),
         ),
-        in_specs=[pl.BlockSpec(memory_space=pltpu.HBM)] * 5,
-        out_specs=(in_smem(),) + tuple(in_vmem(7)),
+        in_specs=[pl.BlockSpec(memory_space=pltpu.HBM)] * 4,
+        out_specs=(in_smem(),) + tuple(in_vmem(5)),
         scratch_shapes=[
             pltpu.VMEM(half, F32),
             pltpu.VMEM(step_sizes.shape, F32),
-            pltpu.SemaphoreType.DMA((6 + 2 * memories,)),
+            pltpu.SemaphoreType.DMA((4 + 2 * memories,)),
         ],
         compiler_params=params(),
-    )(*from_hbm(queries, keys, values, step_sizes, fast_weights))
+    )(*from_hbm(keys, values, step_sizes, fast_weights))
 
 
 def grads_kernel(spots, own, mate, own_w, sent_w, grad_ref):
@@ -263,12 +259,19 @@
     return jnp.concatenate([values, jnp.ones_like(values)], axis=1)
 
 
-def near_kernel(spots, lengths, q_ref, own, mate, mixed_ref, peak_ref, sum_ref, bound_ref):
+def near_kernel(
+    spots, lengths, q_any, own, mate,
+    q_ref, last_ref, mixed_ref, peak_ref, sum_ref, bound_ref, sem,
+):
     tokens, width = q_ref.shape
+    copy = pltpu.make_async_copy(q_any, q_ref, sem)
+    copy.start()
+    last_ref[...] = own[pl.ds(tokens, tokens), width - DM :]
     bounds = [
         jnp.broadcast_to(bound, (tokens, HD)) for bound in view_bounds(lengths, spots[0], tokens)
     ]
     bound_ref[0], bound_ref[1] = bounds
+    copy.wait()
     block_rows = tokens // 4
     for block in range(4):
         rows = slice(block * block_rows, (block + 1) * block_rows)
@@ -323,11 +326,19 @@
     bounds = jax.ShapeDtypeStruct((2, tokens, HD), jnp.int32)
     return pl.pallas_call(
         near_kernel,
-        out_shape=(jax.ShapeDtypeStruct(queries.shape, F32), stats, stats, bounds),
-        in_specs=[in_smem()] + in_vmem(4),
-        out_specs=tuple(in_vmem(4)),
-        compiler_params=params(),
-    )(spots, lengths, queries, own, mate)
+        out_shape=(
+            pltpu.VMEM(queries.shape, BF16),
+            pltpu.VMEM((tokens, DM), BF16),
+            jax.ShapeDtypeStruct(queries.shape, F32),
+            stats,
+            stats,
+            bounds,
+        ),
+        in_specs=[in_smem()] + in_vmem(1) + [pl.BlockSpec(memory_space=pltpu.HBM)] + in_vmem(2),
+        out_specs=tuple(in_vmem(6)),
+        scratch_shapes=[pltpu.SemaphoreType.DMA],
+        compiler_params=params(),
+    )(spots, lengths, *from_hbm(queries), own, mate)
 
 
 def attend_far(memory, spots, queries, far, last, near):
@@ -402,8 +413,8 @@
     def to_plane(x):
         return lax.ppermute(x, "mem", [(p, planes - 1 - p) for p in range(planes)])
 
-    spots, q, own, far, last, own_w, give_w, exact = stage(
-        queries, keys, values, step_sizes, fast_weights, memories, blocks
+    spots, own, far, own_w, give_w, exact = stage(
+        keys, values, step_sizes, fast_weights, memories, blocks
     )
     sent_w = to_plane(give_w)
     mate = to_core(own)
@@ -411,8 +422,8 @@
     lengths = view_lengths.reshape(1, -1)
 
     held = half_grads(spots, blocks, own, mate, own_w, sent_w)
-    held, q = lax.optimization_barrier((held, q))
-    near = attend_near(spots, lengths, q, own, mate)
+    held, lengths = lax.optimization_barrier((held, lengths))
+    q, last, *near = attend_near(spots, lengths, queries, own, mate)
     stride = chips
     for place, radix in enumerate(digits[:0:-1]):
         stride //= radix

time: 48.1 us -> 47.9 us (level)
  waiting for transfers between devices: 19.6 us -> 18.8 us
  Pallas kernels: 15.2 us -> 15.8 us
    ppermute x7, waiting for transfers between devices: 13.2 us -> 12.4 us  [to_chip(): return lax.ppermute(x, 'tok', pairs)]
    pallas_call x1, Pallas kernels: 4.19 us -> 4.95 us  [attend_near(): pl.pallas_call(near_kernel, out_shape=(pltpu.VMEM(queries.shape, BF16), p...]
  transfers between devices with their start and end apart: 12 -> 12, of which waited for: 7 -> 7; matrix products, arithmetic and copies ran while one was open for 0% -> 0% of each run, Pallas kernels for 23% -> 25%
where the time goes in v6:
time: 47.9 us; the launch traced here: 47.7 us
  waiting for transfers between devices  18.8 us (39%)
  Pallas kernels  15.8 us (33%)
  starting transfers between devices  12.8 us (27%)
    ppermute x7, waiting for transfers between devices, to_chip(): return lax.ppermute(x, 'tok', pairs)  12.4 us
    ppermute x7, starting transfers between devices, to_chip(): return lax.ppermute(x, 'tok', pairs)  9.07 us
    ppermute x1, waiting for transfers between devices, to_plane(): return lax.ppermute(x, 'mem', [(p, planes - 1 - p) for p in range(planes)])  5.42 us
    pallas_call x1, Pallas kernels, attend_near(): pl.pallas_call(near_kernel, out_shape=(pltpu.VMEM(queries.shape, BF16), p...  4.95 us
    pallas_call x2, Pallas kernels, attend_far(): pl.pallas_call(body, out_shape=jax.ShapeDtypeStruct((queries.shape[0], DM...  3.44 us
    ppermute x1, starting transfers between devices, to_plane(): return lax.ppermute(x, 'mem', [(p, planes - 1 - p) for p in range(planes)])  2.58 us
    pallas_call x1, Pallas kernels, stage(): pl.pallas_call(functools.partial(stage_kernel, blocks), out_shape=(jax.Sh...  2.36 us
    pallas_call x2, Pallas kernels, read_half(): pl.pallas_call(functools.partial(read_kernel, len(before)), out_shape=jax...  2.21 us
  transfers between devices with their start and end apart: 12, of which 7 were waited for; matrix products, arithmetic and copies ran while one was open for 0% of the time, Pallas kernels for 25%

profile of v6, /device:TPU:0, one launch (start us, length us, event | category | flops | bytes accessed | tf_op | source)
XLA Modules:
  0.0 47.7 jit_solution(243480065536972628)
XLA Ops:
  0.0 2.4 %shard_map.64 = (s32[8]{0:T(128)S(1)}, bf16[1536,512]{1,0:T(8,128)(2,1)S(1)}, bf16[1536,256]{1,0:T(8,128)(2,1)S(1)}, bf16[2,64,768]{2,1,0:T(8,128)(2,1)S(1)}, bf...) custom-call(bf16[512,512]{1,0:T(8,128)(2,1)} %k_any.1, bf16[512,512]{1,0:T(8,128)(2,1)} %v_any.1, ...), custom_call_target="tpu_custom_call" | custom-call | tf_op jit(solution)/shard_map/pallas_call | solution.py:114
  2.4 0.5 %collective-permute-start = (bf16[1536,512]{1,0:T(8,128)(2,1)S(1)}, bf16[1536,512]{1,0:T(8,128)(2,1)S(1)}, u32[]{:S(2)}, u32[]{:S(2)}) collective-permute-start(bf16[1536,512]{1,0:T(8,128)(2,1)S(1)} %get-tuple-element.40.own), channel_id=1, source_target_pairs={{0,2},{2,0},{4,6},{6,4},{8,10},{10,8},{12,14},{14,12},{16,18},{18,... | collective-permute-start | bytes 4718600 | tf_op jit(solution)/shard_map/ppermute | solution.py:397
  2.9 2.6 %collective-permute-start.1 = (bf16[2,64,768]{2,1,0:T(8,128)(2,1)S(1)}, bf16[2,64,768]{2,1,0:T(8,128)(2,1)S(1)}, u32[]{:S(2)}, u32[]{:S(2)}) collective-permute-start(bf16[2,64,768]{2,1,0:T(8,128)(2,1)S(1)} %get-tuple-element.42), channel_id=1, source_target_pairs={{0,1},{1,0},{2,3},{3,2},{4,5},{5,4},{6,7},{7,6},{8,9},{9,8},{10,11... | collective-permute-start | bytes 589832 | tf_op jit(solution)/shard_map/ppermute | solution.py:414
  5.5 0.1 collective-permute-start.6
  5.6 5.4 %collective-permute-done.1.sent_w.refs_3_ = bf16[2,64,768]{2,1,0:T(8,128)(2,1)S(1)} collective-permute-done((bf16[2,64,768]{2,1,0:T(8,128)(2,1)S(1)}, bf16[2,64,768]{2,1,0:T(8,128)(2,1)S(1)}, u32[]{:S(2)}, u32[]{:S(2)}) %collective-permute-start.1) | collective-permute-done | bytes 196640 | tf_op jit(solution)/shard_map/ppermute | solution.py:414
  11.0 0.0 collective-permute-done.mate
  11.0 0.0 copy-start
  11.0 2.1 %shard_map.65 = bf16[4,2,32,768]{3,2,1,0:T(8,128)(2,1)S(1)} custom-call(s32[8]{0:T(128)S(1)} %get-tuple-element.39.spots, bf16[1536,512]{1,0:T(8,128)(2,1)S(1)} %get-tuple-element.40.own, bf16[1536,512]{1,0:T(8,128)(2,1)S(1)} %collective-permute-done.mate, bf16[2,64,768]{2,1,0:T(8,128)(2,1)S(1)} %get-tuple-element.41.own_w, ...), custom_call_target="tpu_custom_call" | custom-call | tf_op jit(solution)/shard_map/pallas_call | solution.py:182
  13.1 1.9 %collective-permute-start.2 = (bf16[1,2,32,768]{3,2,1,0:T(8,128)(2,1)S(1)}, bf16[1,2,32,768]{3,2,1,0:T(8,128)(2,1)S(1)}, u32[]{:S(2)}, u32[]{:S(2)}) collective-permute-start(bf16[1,2,32,768]{3,2,1,0:T(8,128)(2,1)S(1)} %get-tuple-element.75), channel_id=1, source_target_pairs={{0,8},{2,10},{4,12},{6,14},{8,0},{10,2},{12,4},{14,6},{16,24},{18,... | collective-permute-start | bytes 294920 | tf_op jit(solution)/shard_map/ppermute | solution.py:411
  15.0 2.6 %collective-permute-start.3 = (bf16[1,2,32,768]{3,2,1,0:T(8,128)(2,1)S(1)}, bf16[1,2,32,768]{3,2,1,0:T(8,128)(2,1)S(1)}, u32[]{:S(2)}, u32[]{:S(2)}) collective-permute-start(bf16[1,2,32,768]{3,2,1,0:T(8,128)(2,1)S(1)} %get-tuple-element.74), channel_id=1, source_target_pairs={{0,16},{2,18},{4,20},{6,22},{8,24},{10,26},{12,28},{14,30},{16,0},... | collective-permute-start | bytes 294920 | tf_op jit(solution)/shard_map/ppermute | solution.py:411
  17.6 0.0 collective-permute-start.4
  17.6 0.0 copy-done
  17.6 5.0 %shard_map.66 = (bf16[512,512]{1,0:T(8,128)(2,1)S(1)}, bf16[512,256]{1,0:T(8,128)(2,1)S(1)}, f32[512,512]{1,0:T(8,128)S(1)}, f32[4,512,128]{2,1,0:T(8,128)S(1)},...) custom-call(s32[8]{0:T(128)S(1)} %get-tuple-element.39.spots, s32[1,32]{1,0:T(1,128)S(1)} %bitcast.8, ...), custom_call_target="tpu_custom_call" | custom-call | tf_op jit(solution)/shard_map/pallas_call | solution.py:327
  22.6 0.0 collective-permute-done.2
  22.6 1.9 %collective-permute-done.3 = bf16[1,2,32,768]{3,2,1,0:T(8,128)(2,1)S(1)} collective-permute-done((bf16[1,2,32,768]{3,2,1,0:T(8,128)(2,1)S(1)}, bf16[1,2,32,768]{3,2,1,0:T(8,128)(2,1)S(1)}, u32[]{:S(2)}, u32[]{:S(2)}) %collective-permute-start.3) | collective-permute-done | bytes 98336 | tf_op jit(solution)/shard_map/ppermute | solution.py:411
  24.5 2.2 %collective-permute-done.4 = bf16[1,2,32,768]{3,2,1,0:T(8,128)(2,1)S(1)} collective-permute-done((bf16[1,2,32,768]{3,2,1,0:T(8,128)(2,1)S(1)}, bf16[1,2,32,768]{3,2,1,0:T(8,128)(2,1)S(1)}, u32[]{:S(2)}, u32[]{:S(2)}) %collective-permute-start.4) | collective-permute-done | bytes 98336 | tf_op jit(solution)/shard_map/ppermute | solution.py:411
  26.7 0.1 fusion.refs_0_
  26.7 0.2 collective-permute-start.5
  26.9 0.0 collective-permute-done.6.far
  26.9 4.5 %collective-permute-done.5.refs_1_ = bf16[2,32,768]{2,1,0:T(8,128)(2,1)S(1)} collective-permute-done((bf16[2,32,768]{2,1,0:T(8,128)(2,1)S(1)}, bf16[2,32,768]{2,1,0:T(8,128)(2,1)S(1)}, u32[]{:S(2)}, u32[]{:S(2)}) %collective-permute-start.5) | collective-permute-done | bytes 98336 | tf_op jit(solution)/shard_map/ppermute | solution.py:411
  31.4 0.5 %collective-permute-start.10 = (bf16[512,256]{1,0:T(8,128)(2,1)S(1)}, bf16[512,256]{1,0:T(8,128)(2,1)S(1)}, u32[]{:S(2)}, u32[]{:S(2)}) collective-permute-start(bf16[512,256]{1,0:T(8,128)(2,1)S(1)} %get-tuple-element.67), channel_id=1, source_target_pairs={{2,4},{3,5},{4,2},{5,3},{6,8},{7,9},{8,6},{9,7},{10,12},{11,13},{1... | collective-permute-start | bytes 786440 | tf_op jit(solution)/shard_map/ppermute | solution.py:407
  31.9 0.7 %shard_map.67 = bf16[2,32,768]{2,1,0:T(8,128)(2,1)S(1)} custom-call(s32[8]{0:T(128)S(1)} %get-tuple-element.39.spots, bf16[2,32,768]{2,1,0:T(8,128)(2,1)S(1)} %fusion.refs_0_, bf16[2,32,768]{2,1,0:T(8,128)(2,1)S(1)} %collective-permute-done.5.refs_1_, f32[2,64,768]{2,1,0:T(8,128)S(1)} %get-tuple-element.56.refs_2_, ...), custom_call_target="tpu_custom_call" | custom-call | tf_op jit(solution)/shard_map/pallas_call | solution.py:225
  32.6 1.1 %collective-permute-start.7 = (bf16[1,2,32,768]{3,2,1,0:T(8,128)(2,1)S(1)}, bf16[1,2,32,768]{3,2,1,0:T(8,128)(2,1)S(1)}, u32[]{:S(2)}, u32[]{:S(2)}) collective-permute-start(bf16[1,2,32,768]{3,2,1,0:T(8,128)(2,1)S(1)} %bitcast.4), channel_id=1, source_target_pairs={{0,8},{2,10},{4,12},{6,14},{8,0},{10,2},{12,4},{14,6},{16,24},{18,... | collective-permute-start | bytes 294920 | tf_op jit(solution)/shard_map/ppermute | solution.py:411
  33.7 0.1 collective-permute-start.8
  33.8 3.3 %collective-permute-start.9 = (bf16[1,2,32,768]{3,2,1,0:T(8,128)(2,1)S(1)}, bf16[1,2,32,768]{3,2,1,0:T(8,128)(2,1)S(1)}, u32[]{:S(2)}, u32[]{:S(2)}) collective-permute-start(bf16[1,2,32,768]{3,2,1,0:T(8,128)(2,1)S(1)} %bitcast.6), channel_id=1, source_target_pairs={{0,24},{2,26},{4,28},{6,30},{8,16},{10,18},{12,20},{14,22},{16,8},... | collective-permute-start | bytes 294920 | tf_op jit(solution)/shard_map/ppermute | solution.py:411
  37.1 1.7 %shard_map.68.refs_1_ = f32[512,256]{1,0:T(8,128)S(1)} custom-call(s32[8]{0:T(128)S(1)} %get-tuple-element.39.spots, bf16[512,512]{1,0:T(8,128)(2,1)S(1)} %get-tuple-element.44.q_ref, bf16[1536,256]{1,0:T(8,128)(2,1)S(1)} %collective-permute-done.6.far, f32[512,512]{1,0:T(8,128)S(1)} %get-tuple-element.63.rest_0_.mixed_ref, ...), custom_call_target="tpu_custom_call" | custom-call | tf_op jit(solution)/shard_map/pallas_call | solution.py:352
  38.8 0.0 collective-permute-done.10.last
  38.8 1.7 %shard_map.69.refs_2_ = f32[512,256]{1,0:T(8,128)S(1)} custom-call(s32[8]{0:T(128)S(1)} %get-tuple-element.39.spots, bf16[512,512]{1,0:T(8,128)(2,1)S(1)} %get-tuple-element.44.q_ref, bf16[1536,256]{1,0:T(8,128)(2,1)S(1)} %collective-permute-done.6.far, bf16[512,256]{1,0:T(8,128)(2,1)S(1)} %collective-permute-done.10.last, ...), custom_call_target="tpu_custom_call" | custom-call | tf_op jit(solution)/shard_map/pallas_call | solution.py:352
  40.5 0.5 %collective-permute-done.7 = bf16[1,2,32,768]{3,2,1,0:T(8,128)(2,1)S(1)} collective-permute-done((bf16[1,2,32,768]{3,2,1,0:T(8,128)(2,1)S(1)}, bf16[1,2,32,768]{3,2,1,0:T(8,128)(2,1)S(1)}, u32[]{:S(2)}, u32[]{:S(2)}) %collective-permute-start.7) | collective-permute-done | bytes 98336 | tf_op jit(solution)/shard_map/ppermute | solution.py:411
  41.1 3.3 %collective-permute-done.8 = bf16[1,2,32,768]{3,2,1,0:T(8,128)(2,1)S(1)} collective-permute-done((bf16[1,2,32,768]{3,2,1,0:T(8,128)(2,1)S(1)}, bf16[1,2,32,768]{3,2,1,0:T(8,128)(2,1)S(1)}, u32[]{:S(2)}, u32[]{:S(2)}) %collective-permute-start.8) | collective-permute-done | bytes 98336 | tf_op jit(solution)/shard_map/ppermute | solution.py:411
  44.3 0.0 collective-permute-done.9
  44.4 0.1 collective-permute-start.11
  44.5 0.7 %shard_map.70.refs_0_ = f32[512,512]{1,0:T(8,128)S(1)} custom-call(bf16[512,512]{1,0:T(8,128)(2,1)S(1)} %get-tuple-element.44.q_ref, bf16[4,2,32,768]{3,2,1,0:T(8,128)(2,1)S(1)} %constant_dynamic-update-slice_fusion.w_ref), custom_call_target="tpu_custom_call" | custom-call | tf_op jit(solution)/shard_map/pallas_call | solution.py:378
  45.2 1.0 %collective-permute-done.11.w_ref = bf16[4,2,32,768]{3,2,1,0:T(8,128)(2,1)S(1)} collective-permute-done((bf16[4,2,32,768]{3,2,1,0:T(8,128)(2,1)S(1)}, bf16[4,2,32,768]{3,2,1,0:T(8,128)(2,1)S(1)}, u32[]{:S(2)}, u32[]{:S(2)}) %collective-permute-start.11) | collective-permute-done | bytes 393248 | tf_op jit(solution)/shard_map/ppermute | solution.py:397
  46.2 1.5 %shard_map.71 = bf16[512,512]{1,0:T(8,128)(2,1)} custom-call(bf16[512,512]{1,0:T(8,128)(2,1)S(1)} %get-tuple-element.44.q_ref, bf16[4,2,32,768]{3,2,1,0:T(8,128)(2,1)S(1)} %collective-permute-done.11.w_ref, f32[512,512]{1,0:T(8,128)S(1)} %shard_map.70.refs_0_, f32[512,256]{1,0:T(8,128)S(1)} %shard_map.68.refs_1_, f32[512,256]{1,0:T(8,128)S(1)} %shard_map.69.refs_2_), custom_call_target="tpu_custom_call" | custom-call | tf_op jit(solution)/shard_map/pallas_call | solution.py:378
  (5 shorter events, 0.1 us)
Async XLA Ops:
  2.4 8.6 %collective-permute-start = (bf16[1536,512]{1,0:T(8,128)(2,1)S(1)}, bf16[1536,512]{1,0:T(8,128)(2,1)S(1)}, u32[]{:S(2)}, u32[]{:S(2)}) collective-permute-start(bf16[1536,512]{1,0:T(8,128)(2,1)S(1)} %get-tuple-element.40.own), channel_id=1, source_target_pairs={{0,2},{2,0},{4,6},{6,4},{8,10},{10,8},{12,14},{14,12},{16,18},{18,... | collective-permute-start | bytes 4718600 | tf_op jit(solution)/shard_map/ppermute | solution.py:397
  2.9 8.1 %collective-permute-start.1 = (bf16[2,64,768]{2,1,0:T(8,128)(2,1)S(1)}, bf16[2,64,768]{2,1,0:T(8,128)(2,1)S(1)}, u32[]{:S(2)}, u32[]{:S(2)}) collective-permute-start(bf16[2,64,768]{2,1,0:T(8,128)(2,1)S(1)} %get-tuple-element.42), channel_id=1, source_target_pairs={{0,1},{1,0},{2,3},{3,2},{4,5},{5,4},{6,7},{7,6},{8,9},{9,8},{10,11... | collective-permute-start | bytes 589832 | tf_op jit(solution)/shard_map/ppermute | solution.py:414
  5.5 21.4 %collective-permute-start.6 = (bf16[1536,256]{1,0:T(8,128)(2,1)S(1)}, bf16[1536,256]{1,0:T(8,128)(2,1)S(1)}, u32[]{:S(2)}, u32[]{:S(2)}) collective-permute-start(bf16[1536,256]{1,0:T(8,128)(2,1)S(1)} %get-tuple-element.54), channel_id=1, source_target_pairs={{2,4},{3,5},{4,2},{5,3},{6,8},{7,9},{8,6},{9,7},{10,12},{11,13},{1... | collective-permute-start | bytes 2359304 | tf_op jit(solution)/shard_map/ppermute | solution.py:407
  11.0 6.6 %copy-start = (s32[32]{0:T(128)S(1)}, s32[32]{0:T(128)}, u32[]{:S(2)}) copy-start(s32[32]{0:T(128)} %param.11) | copy-start | bytes 388
  13.1 9.4 %collective-permute-start.2 = (bf16[1,2,32,768]{3,2,1,0:T(8,128)(2,1)S(1)}, bf16[1,2,32,768]{3,2,1,0:T(8,128)(2,1)S(1)}, u32[]{:S(2)}, u32[]{:S(2)}) collective-permute-start(bf16[1,2,32,768]{3,2,1,0:T(8,128)(2,1)S(1)} %get-tuple-element.75), channel_id=1, source_target_pairs={{0,8},{2,10},{4,12},{6,14},{8,0},{10,2},{12,4},{14,6},{16,24},{18,... | collective-permute-start | bytes 294920 | tf_op jit(solution)/shard_map/ppermute | solution.py:411
  15.0 9.5 %collective-permute-start.3 = (bf16[1,2,32,768]{3,2,1,0:T(8,128)(2,1)S(1)}, bf16[1,2,32,768]{3,2,1,0:T(8,128)(2,1)S(1)}, u32[]{:S(2)}, u32[]{:S(2)}) collective-permute-start(bf16[1,2,32,768]{3,2,1,0:T(8,128)(2,1)S(1)} %get-tuple-element.74), channel_id=1, source_target_pairs={{0,16},{2,18},{4,20},{6,22},{8,24},{10,26},{12,28},{14,30},{16,0},... | collective-permute-start | bytes 294920 | tf_op jit(solution)/shard_map/ppermute | solution.py:411
  17.6 9.1 %collective-permute-start.4 = (bf16[1,2,32,768]{3,2,1,0:T(8,128)(2,1)S(1)}, bf16[1,2,32,768]{3,2,1,0:T(8,128)(2,1)S(1)}, u32[]{:S(2)}, u32[]{:S(2)}) collective-permute-start(bf16[1,2,32,768]{3,2,1,0:T(8,128)(2,1)S(1)} %get-tuple-element.73), channel_id=1, source_target_pairs={{0,24},{2,26},{4,28},{6,30},{8,16},{10,18},{12,20},{14,22},{16,8},... | collective-permute-start | bytes 294920 | tf_op jit(solution)/shard_map/ppermute | solution.py:411
  26.7 4.7 %collective-permute-start.5 = (bf16[2,32,768]{2,1,0:T(8,128)(2,1)S(1)}, bf16[2,32,768]{2,1,0:T(8,128)(2,1)S(1)}, u32[]{:S(2)}, u32[]{:S(2)}) collective-permute-start(bf16[2,32,768]{2,1,0:T(8,128)(2,1)S(1)} %fusion.refs_0_), channel_id=1, source_target_pairs={{0,4},{2,6},{4,0},{6,2},{8,12},{10,14},{12,8},{14,10},{16,20},{18,... | collective-permute-start | bytes 294920 | tf_op jit(solution)/shard_map/ppermute | solution.py:411
  31.4 7.4 %collective-permute-start.10 = (bf16[512,256]{1,0:T(8,128)(2,1)S(1)}, bf16[512,256]{1,0:T(8,128)(2,1)S(1)}, u32[]{:S(2)}, u32[]{:S(2)}) collective-permute-start(bf16[512,256]{1,0:T(8,128)(2,1)S(1)} %get-tuple-element.67), channel_id=1, source_target_pairs={{2,4},{3,5},{4,2},{5,3},{6,8},{7,9},{8,6},{9,7},{10,12},{11,13},{1... | collective-permute-start | bytes 786440 | tf_op jit(solution)/shard_map/ppermute | solution.py:407
  32.6 8.4 %collective-permute-start.7 = (bf16[1,2,32,768]{3,2,1,0:T(8,128)(2,1)S(1)}, bf16[1,2,32,768]{3,2,1,0:T(8,128)(2,1)S(1)}, u32[]{:S(2)}, u32[]{:S(2)}) collective-permute-start(bf16[1,2,32,768]{3,2,1,0:T(8,128)(2,1)S(1)} %bitcast.4), channel_id=1, source_target_pairs={{0,8},{2,10},{4,12},{6,14},{8,0},{10,2},{12,4},{14,6},{16,24},{18,... | collective-permute-start | bytes 294920 | tf_op jit(solution)/shard_map/ppermute | solution.py:411
  33.7 10.6 %collective-permute-start.8 = (bf16[1,2,32,768]{3,2,1,0:T(8,128)(2,1)S(1)}, bf16[1,2,32,768]{3,2,1,0:T(8,128)(2,1)S(1)}, u32[]{:S(2)}, u32[]{:S(2)}) collective-permute-start(bf16[1,2,32,768]{3,2,1,0:T(8,128)(2,1)S(1)} %bitcast.5), channel_id=1, source_target_pairs={{0,16},{2,18},{4,20},{6,22},{8,24},{10,26},{12,28},{14,30},{16,0},... | collective-permute-start | bytes 294920 | tf_op jit(solution)/shard_map/ppermute | solution.py:411
  33.8 10.5 %collective-permute-start.9 = (bf16[1,2,32,768]{3,2,1,0:T(8,128)(2,1)S(1)}, bf16[1,2,32,768]{3,2,1,0:T(8,128)(2,1)S(1)}, u32[]{:S(2)}, u32[]{:S(2)}) collective-permute-start(bf16[1,2,32,768]{3,2,1,0:T(8,128)(2,1)S(1)} %bitcast.6), channel_id=1, source_target_pairs={{0,24},{2,26},{4,28},{6,30},{8,16},{10,18},{12,20},{14,22},{16,8},... | collective-permute-start | bytes 294920 | tf_op jit(solution)/shard_map/ppermute | solution.py:411
  44.4 1.8 %collective-permute-start.11 = (bf16[4,2,32,768]{3,2,1,0:T(8,128)(2,1)S(1)}, bf16[4,2,32,768]{3,2,1,0:T(8,128)(2,1)S(1)}, u32[]{:S(2)}, u32[]{:S(2)}) collective-permute-start(bf16[4,2,32,768]{3,2,1,0:T(8,128)(2,1)S(1)} %constant_dynamic-update-slice_fusion.w_ref), channel_id=1, source_target_pairs={{0,2},{2,0},{4,6},{6,4},{8,10},{10,8},{12,14},{14,12},{16,18},{18,... | collective-permute-start | bytes 1179656 | tf_op jit(solution)/shard_map/ppermute | solution.py:397

commit v7 on v6

--- a/solution.py
+++ b/solution.py
@@ -358,30 +358,56 @@
     )(spots, *given)
 
 
-def read_kernel(parts, q_ref, w_ref, *refs):
-    before, out_ref = refs[:parts], refs[parts]
-    blocks, memories, rows, _ = w_ref.shape
+def read_kernel(q_ref, w_ref, out_ref):
+    blocks, memories, rows, width = w_ref.shape
     for memory in range(memories):
         features = pl.ds(memory * DM, DM)
-        query = q_ref[:, features]
-        weights = w_ref[:, memory].reshape(blocks * rows, 3 * DM)
-        gate = dot_nt(query, weights[:, :DM])
-        up = dot_nt(query, weights[:, DM : 2 * DM])
-        hidden = (gate * jax.nn.sigmoid(gate) * up).astype(BF16)
-        total = dot_nn(hidden, weights[:, 2 * DM :])
-        if parts > 0:
-            total += before[0][:, features] + before[1 + memory][...]
-        out_ref[:, features] = total.astype(out_ref.dtype)
-
-
-def read_half(queries, weights, before, kind):
-    return pl.pallas_call(
-        functools.partial(read_kernel, len(before)),
-        out_shape=jax.ShapeDtypeStruct(queries.shape, kind),
-        in_specs=in_vmem(2 + len(before)),
+        out_ref[:, features] = read_rows(q_ref[:, features], w_ref[:, memory])
+
+
+def read_rows(query, weights):
+    held = weights.reshape(weights.shape[0] * weights.shape[1], weights.shape[2])
+    units = held.shape[0]
+    gate_up = dot_nt(query, jnp.concatenate([held[:, :DM], held[:, DM : 2 * DM]], axis=0))
+    gate, up = gate_up[:, :units], gate_up[:, units:]
+    hidden = (gate * jax.nn.sigmoid(gate) * up).astype(BF16)
+    return dot_nn(hidden, held[:, 2 * DM :])
+
+
+def last_kernel(q_ref, w_ref, before, *refs):
+    *attended, out_any, result, sems = refs
+    copies = []
+    for memory in range(w_ref.shape[1]):
+        features = pl.ds(memory * DM, DM)
+        total = read_rows(q_ref[:, features], w_ref[:, memory])
+        total += before[:, features] + attended[memory][...]
+        result[:, features] = total.astype(BF16)
+        done, goal = result.at[:, features], out_any.at[:, features]
+        copies.append(pltpu.make_async_copy(done, goal, sems.at[memory]))
+        copies[-1].start()
+    for copy in copies:
+        copy.wait()
+
+
+def read_first(queries, weights):
+    return pl.pallas_call(
+        read_kernel,
+        out_shape=jax.ShapeDtypeStruct(queries.shape, F32),
+        in_specs=in_vmem(2),
         out_specs=in_vmem(1)[0],
         compiler_params=params(),
-    )(queries, weights, *before)
+    )(queries, weights)
+
+
+def read_last(queries, weights, before, attended):
+    return pl.pallas_call(
+        last_kernel,
+        out_shape=jax.ShapeDtypeStruct(queries.shape, BF16),
+        in_specs=in_vmem(3 + len(attended)),
+        out_specs=pl.BlockSpec(memory_space=pltpu.HBM),
+        scratch_shapes=[pltpu.VMEM(queries.shape, BF16), pltpu.SemaphoreType.DMA((len(attended),))],
+        compiler_params=params(),
+    )(queries, weights, before, *attended)
 
 
 def on_device(queries, keys, values, step_sizes, fast_weights, view_lengths):
@@ -455,8 +481,8 @@
         stride *= radix
         gathered = jnp.concatenate([gathered] + came, axis=0)
     mate_w = to_core(gathered)
-    partial = read_half(q, gathered, [], F32)
-    return read_half(q, mate_w, [partial] + attended, BF16)
+    partial = read_first(q, gathered)
+    return read_last(q, mate_w, partial, attended)
 
 
 def solution(mesh):

time: 47.9 us -> 47.8 us (level)
  no operation moved by 1% of the time
where the time goes in v7:
time: 47.8 us; the launch traced here: 47.6 us
  waiting for transfers between devices  18.8 us (39%)
  Pallas kernels  15.7 us (33%)
  starting transfers between devices  12.8 us (27%)
    ppermute x7, waiting for transfers between devices, to_chip(): return lax.ppermute(x, 'tok', pairs)  12.4 us
    ppermute x7, starting transfers between devices, to_chip(): return lax.ppermute(x, 'tok', pairs)  9.07 us
    ppermute x1, waiting for transfers between devices, to_plane(): return lax.ppermute(x, 'mem', [(p, planes - 1 - p) for p in range(planes)])  5.42 us
    pallas_call x1, Pallas kernels, attend_near(): pl.pallas_call(near_kernel, out_shape=(pltpu.VMEM(queries.shape, BF16), p...  4.95 us
    pallas_call x2, Pallas kernels, attend_far(): pl.pallas_call(body, out_shape=jax.ShapeDtypeStruct((queries.shape[0], DM...  3.44 us
    ppermute x1, starting transfers between devices, to_plane(): return lax.ppermute(x, 'mem', [(p, planes - 1 - p) for p in range(planes)])  2.58 us
    pallas_call x1, Pallas kernels, stage(): pl.pallas_call(functools.partial(stage_kernel, blocks), out_shape=(jax.Sh...  2.36 us
    pallas_call x1, Pallas kernels, half_grads(): pl.pallas_call(grads_kernel, out_shape=jax.ShapeDtypeStruct(shape, BF16),...  2.11 us
  transfers between devices with their start and end apart: 12, of which 7 were waited for; matrix products, arithmetic and copies ran while one was open for 0% of the time, Pallas kernels for 25%

profile of v7, /device:TPU:0, one launch (start us, length us, event | category | flops | bytes accessed | tf_op | source)
XLA Modules:
  0.0 47.6 jit_solution(17846967634263789794)
XLA Ops:
  0.0 2.4 %shard_map.64 = (s32[8]{0:T(128)S(1)}, bf16[1536,512]{1,0:T(8,128)(2,1)S(1)}, bf16[1536,256]{1,0:T(8,128)(2,1)S(1)}, bf16[2,64,768]{2,1,0:T(8,128)(2,1)S(1)}, bf...) custom-call(bf16[512,512]{1,0:T(8,128)(2,1)} %k_any.1, bf16[512,512]{1,0:T(8,128)(2,1)} %v_any.1, ...), custom_call_target="tpu_custom_call" | custom-call | tf_op jit(solution)/shard_map/pallas_call | solution.py:114
  2.4 0.5 %collective-permute-start = (bf16[1536,512]{1,0:T(8,128)(2,1)S(1)}, bf16[1536,512]{1,0:T(8,128)(2,1)S(1)}, u32[]{:S(2)}, u32[]{:S(2)}) collective-permute-start(bf16[1536,512]{1,0:T(8,128)(2,1)S(1)} %get-tuple-element.40.own), channel_id=1, source_target_pairs={{0,2},{2,0},{4,6},{6,4},{8,10},{10,8},{12,14},{14,12},{16,18},{18,... | collective-permute-start | bytes 4718600 | tf_op jit(solution)/shard_map/ppermute | solution.py:423
  2.9 2.6 %collective-permute-start.1 = (bf16[2,64,768]{2,1,0:T(8,128)(2,1)S(1)}, bf16[2,64,768]{2,1,0:T(8,128)(2,1)S(1)}, u32[]{:S(2)}, u32[]{:S(2)}) collective-permute-start(bf16[2,64,768]{2,1,0:T(8,128)(2,1)S(1)} %get-tuple-element.42), channel_id=1, source_target_pairs={{0,1},{1,0},{2,3},{3,2},{4,5},{5,4},{6,7},{7,6},{8,9},{9,8},{10,11... | collective-permute-start | bytes 589832 | tf_op jit(solution)/shard_map/ppermute | solution.py:440
  5.5 0.1 collective-permute-start.6
  5.6 5.4 %collective-permute-done.1.sent_w.refs_3_ = bf16[2,64,768]{2,1,0:T(8,128)(2,1)S(1)} collective-permute-done((bf16[2,64,768]{2,1,0:T(8,128)(2,1)S(1)}, bf16[2,64,768]{2,1,0:T(8,128)(2,1)S(1)}, u32[]{:S(2)}, u32[]{:S(2)}) %collective-permute-start.1) | collective-permute-done | bytes 196640 | tf_op jit(solution)/shard_map/ppermute | solution.py:440
  11.0 0.0 collective-permute-done.mate
  11.0 0.0 copy-start
  11.0 2.1 %shard_map.65 = bf16[4,2,32,768]{3,2,1,0:T(8,128)(2,1)S(1)} custom-call(s32[8]{0:T(128)S(1)} %get-tuple-element.39.spots, bf16[1536,512]{1,0:T(8,128)(2,1)S(1)} %get-tuple-element.40.own, bf16[1536,512]{1,0:T(8,128)(2,1)S(1)} %collective-permute-done.mate, bf16[2,64,768]{2,1,0:T(8,128)(2,1)S(1)} %get-tuple-element.41.own_w, ...), custom_call_target="tpu_custom_call" | custom-call | tf_op jit(solution)/shard_map/pallas_call | solution.py:182
  13.1 1.9 %collective-permute-start.2 = (bf16[1,2,32,768]{3,2,1,0:T(8,128)(2,1)S(1)}, bf16[1,2,32,768]{3,2,1,0:T(8,128)(2,1)S(1)}, u32[]{:S(2)}, u32[]{:S(2)}) collective-permute-start(bf16[1,2,32,768]{3,2,1,0:T(8,128)(2,1)S(1)} %get-tuple-element.75), channel_id=1, source_target_pairs={{0,8},{2,10},{4,12},{6,14},{8,0},{10,2},{12,4},{14,6},{16,24},{18,... | collective-permute-start | bytes 294920 | tf_op jit(solution)/shard_map/ppermute | solution.py:437
  15.0 2.6 %collective-permute-start.3 = (bf16[1,2,32,768]{3,2,1,0:T(8,128)(2,1)S(1)}, bf16[1,2,32,768]{3,2,1,0:T(8,128)(2,1)S(1)}, u32[]{:S(2)}, u32[]{:S(2)}) collective-permute-start(bf16[1,2,32,768]{3,2,1,0:T(8,128)(2,1)S(1)} %get-tuple-element.74), channel_id=1, source_target_pairs={{0,16},{2,18},{4,20},{6,22},{8,24},{10,26},{12,28},{14,30},{16,0},... | collective-permute-start | bytes 294920 | tf_op jit(solution)/shard_map/ppermute | solution.py:437
  17.6 0.0 collective-permute-start.4
  17.6 0.0 copy-done
  17.6 5.0 %shard_map.66 = (bf16[512,512]{1,0:T(8,128)(2,1)S(1)}, bf16[512,256]{1,0:T(8,128)(2,1)S(1)}, f32[512,512]{1,0:T(8,128)S(1)}, f32[4,512,128]{2,1,0:T(8,128)S(1)},...) custom-call(s32[8]{0:T(128)S(1)} %get-tuple-element.39.spots, s32[1,32]{1,0:T(1,128)S(1)} %bitcast.8, ...), custom_call_target="tpu_custom_call" | custom-call | tf_op jit(solution)/shard_map/pallas_call | solution.py:327
  22.6 0.0 collective-permute-done.2
  22.6 1.9 %collective-permute-done.3 = bf16[1,2,32,768]{3,2,1,0:T(8,128)(2,1)S(1)} collective-permute-done((bf16[1,2,32,768]{3,2,1,0:T(8,128)(2,1)S(1)}, bf16[1,2,32,768]{3,2,1,0:T(8,128)(2,1)S(1)}, u32[]{:S(2)}, u32[]{:S(2)}) %collective-permute-start.3) | collective-permute-done | bytes 98336 | tf_op jit(solution)/shard_map/ppermute | solution.py:437
  24.5 2.2 %collective-permute-done.4 = bf16[1,2,32,768]{3,2,1,0:T(8,128)(2,1)S(1)} collective-permute-done((bf16[1,2,32,768]{3,2,1,0:T(8,128)(2,1)S(1)}, bf16[1,2,32,768]{3,2,1,0:T(8,128)(2,1)S(1)}, u32[]{:S(2)}, u32[]{:S(2)}) %collective-permute-start.4) | collective-permute-done | bytes 98336 | tf_op jit(solution)/shard_map/ppermute | solution.py:437
  26.7 0.1 fusion.refs_0_
  26.7 0.2 collective-permute-start.5
  26.9 0.0 collective-permute-done.6.far
  26.9 4.5 %collective-permute-done.5.refs_1_ = bf16[2,32,768]{2,1,0:T(8,128)(2,1)S(1)} collective-permute-done((bf16[2,32,768]{2,1,0:T(8,128)(2,1)S(1)}, bf16[2,32,768]{2,1,0:T(8,128)(2,1)S(1)}, u32[]{:S(2)}, u32[]{:S(2)}) %collective-permute-start.5) | collective-permute-done | bytes 98336 | tf_op jit(solution)/shard_map/ppermute | solution.py:437
  31.4 0.5 %collective-permute-start.10 = (bf16[512,256]{1,0:T(8,128)(2,1)S(1)}, bf16[512,256]{1,0:T(8,128)(2,1)S(1)}, u32[]{:S(2)}, u32[]{:S(2)}) collective-permute-start(bf16[512,256]{1,0:T(8,128)(2,1)S(1)} %get-tuple-element.67), channel_id=1, source_target_pairs={{2,4},{3,5},{4,2},{5,3},{6,8},{7,9},{8,6},{9,7},{10,12},{11,13},{1... | collective-permute-start | bytes 786440 | tf_op jit(solution)/shard_map/ppermute | solution.py:433
  31.9 0.7 %shard_map.67 = bf16[2,32,768]{2,1,0:T(8,128)(2,1)S(1)} custom-call(s32[8]{0:T(128)S(1)} %get-tuple-element.39.spots, bf16[2,32,768]{2,1,0:T(8,128)(2,1)S(1)} %fusion.refs_0_, bf16[2,32,768]{2,1,0:T(8,128)(2,1)S(1)} %collective-permute-done.5.refs_1_, f32[2,64,768]{2,1,0:T(8,128)S(1)} %get-tuple-element.56.refs_2_, ...), custom_call_target="tpu_custom_call" | custom-call | tf_op jit(solution)/shard_map/pallas_call | solution.py:225
  32.6 1.1 %collective-permute-start.7 = (bf16[1,2,32,768]{3,2,1,0:T(8,128)(2,1)S(1)}, bf16[1,2,32,768]{3,2,1,0:T(8,128)(2,1)S(1)}, u32[]{:S(2)}, u32[]{:S(2)}) collective-permute-start(bf16[1,2,32,768]{3,2,1,0:T(8,128)(2,1)S(1)} %bitcast.4), channel_id=1, source_target_pairs={{0,8},{2,10},{4,12},{6,14},{8,0},{10,2},{12,4},{14,6},{16,24},{18,... | collective-permute-start | bytes 294920 | tf_op jit(solution)/shard_map/ppermute | solution.py:437
  33.7 0.1 collective-permute-start.8
  33.8 3.3 %collective-permute-start.9 = (bf16[1,2,32,768]{3,2,1,0:T(8,128)(2,1)S(1)}, bf16[1,2,32,768]{3,2,1,0:T(8,128)(2,1)S(1)}, u32[]{:S(2)}, u32[]{:S(2)}) collective-permute-start(bf16[1,2,32,768]{3,2,1,0:T(8,128)(2,1)S(1)} %bitcast.6), channel_id=1, source_target_pairs={{0,24},{2,26},{4,28},{6,30},{8,16},{10,18},{12,20},{14,22},{16,8},... | collective-permute-start | bytes 294920 | tf_op jit(solution)/shard_map/ppermute | solution.py:437
  37.1 1.7 %shard_map.68.refs_0_ = f32[512,256]{1,0:T(8,128)S(1)} custom-call(s32[8]{0:T(128)S(1)} %get-tuple-element.39.spots, bf16[512,512]{1,0:T(8,128)(2,1)S(1)} %get-tuple-element.44.q_ref, bf16[1536,256]{1,0:T(8,128)(2,1)S(1)} %collective-permute-done.6.far, f32[512,512]{1,0:T(8,128)S(1)} %get-tuple-element.63.rest_0_.mixed_ref, ...), custom_call_target="tpu_custom_call" | custom-call | tf_op jit(solution)/shard_map/pallas_call | solution.py:352
  38.8 0.0 collective-permute-done.10.last
  38.8 1.7 %shard_map.69.refs_1_ = f32[512,256]{1,0:T(8,128)S(1)} custom-call(s32[8]{0:T(128)S(1)} %get-tuple-element.39.spots, bf16[512,512]{1,0:T(8,128)(2,1)S(1)} %get-tuple-element.44.q_ref, bf16[1536,256]{1,0:T(8,128)(2,1)S(1)} %collective-permute-done.6.far, bf16[512,256]{1,0:T(8,128)(2,1)S(1)} %collective-permute-done.10.last, ...), custom_call_target="tpu_custom_call" | custom-call | tf_op jit(solution)/shard_map/pallas_call | solution.py:352
  40.5 0.5 %collective-permute-done.7 = bf16[1,2,32,768]{3,2,1,0:T(8,128)(2,1)S(1)} collective-permute-done((bf16[1,2,32,768]{3,2,1,0:T(8,128)(2,1)S(1)}, bf16[1,2,32,768]{3,2,1,0:T(8,128)(2,1)S(1)}, u32[]{:S(2)}, u32[]{:S(2)}) %collective-permute-start.7) | collective-permute-done | bytes 98336 | tf_op jit(solution)/shard_map/ppermute | solution.py:437
  41.1 3.3 %collective-permute-done.8 = bf16[1,2,32,768]{3,2,1,0:T(8,128)(2,1)S(1)} collective-permute-done((bf16[1,2,32,768]{3,2,1,0:T(8,128)(2,1)S(1)}, bf16[1,2,32,768]{3,2,1,0:T(8,128)(2,1)S(1)}, u32[]{:S(2)}, u32[]{:S(2)}) %collective-permute-start.8) | collective-permute-done | bytes 98336 | tf_op jit(solution)/shard_map/ppermute | solution.py:437
  44.3 0.0 collective-permute-done.9
  44.4 0.1 collective-permute-start.11
  44.5 0.7 %shard_map.70.before = f32[512,512]{1,0:T(8,128)S(1)} custom-call(bf16[512,512]{1,0:T(8,128)(2,1)S(1)} %get-tuple-element.44.q_ref, bf16[4,2,32,768]{3,2,1,0:T(8,128)(2,1)S(1)} %constant_dynamic-update-slice_fusion.w_ref), custom_call_target="tpu_custom_call" | custom-call | tf_op jit(solution)/shard_map/pallas_call | solution.py:393
  45.2 1.0 %collective-permute-done.11.w_ref = bf16[4,2,32,768]{3,2,1,0:T(8,128)(2,1)S(1)} collective-permute-done((bf16[4,2,32,768]{3,2,1,0:T(8,128)(2,1)S(1)}, bf16[4,2,32,768]{3,2,1,0:T(8,128)(2,1)S(1)}, u32[]{:S(2)}, u32[]{:S(2)}) %collective-permute-start.11) | collective-permute-done | bytes 393248 | tf_op jit(solution)/shard_map/ppermute | solution.py:423
  46.2 1.4 %shard_map.71 = bf16[512,512]{1,0:T(8,128)(2,1)} custom-call(bf16[512,512]{1,0:T(8,128)(2,1)S(1)} %get-tuple-element.44.q_ref, bf16[4,2,32,768]{3,2,1,0:T(8,128)(2,1)S(1)} %collective-permute-done.11.w_ref, f32[512,512]{1,0:T(8,128)S(1)} %shard_map.70.before, f32[512,256]{1,0:T(8,128)S(1)} %shard_map.68.refs_0_, f32[512,256]{1,0:T(8,128)S(1)} %shard_map.69.refs_1_), custom_call_target="tpu_custom_call" | custom-call | tf_op jit(solution)/shard_map/pallas_call | solution.py:403
  (5 shorter events, 0.1 us)
Async XLA Ops:
  2.4 8.6 %collective-permute-start = (bf16[1536,512]{1,0:T(8,128)(2,1)S(1)}, bf16[1536,512]{1,0:T(8,128)(2,1)S(1)}, u32[]{:S(2)}, u32[]{:S(2)}) collective-permute-start(bf16[1536,512]{1,0:T(8,128)(2,1)S(1)} %get-tuple-element.40.own), channel_id=1, source_target_pairs={{0,2},{2,0},{4,6},{6,4},{8,10},{10,8},{12,14},{14,12},{16,18},{18,... | collective-permute-start | bytes 4718600 | tf_op jit(solution)/shard_map/ppermute | solution.py:423
  2.9 8.1 %collective-permute-start.1 = (bf16[2,64,768]{2,1,0:T(8,128)(2,1)S(1)}, bf16[2,64,768]{2,1,0:T(8,128)(2,1)S(1)}, u32[]{:S(2)}, u32[]{:S(2)}) collective-permute-start(bf16[2,64,768]{2,1,0:T(8,128)(2,1)S(1)} %get-tuple-element.42), channel_id=1, source_target_pairs={{0,1},{1,0},{2,3},{3,2},{4,5},{5,4},{6,7},{7,6},{8,9},{9,8},{10,11... | collective-permute-start | bytes 589832 | tf_op jit(solution)/shard_map/ppermute | solution.py:440
  5.5 21.4 %collective-permute-start.6 = (bf16[1536,256]{1,0:T(8,128)(2,1)S(1)}, bf16[1536,256]{1,0:T(8,128)(2,1)S(1)}, u32[]{:S(2)}, u32[]{:S(2)}) collective-permute-start(bf16[1536,256]{1,0:T(8,128)(2,1)S(1)} %get-tuple-element.54), channel_id=1, source_target_pairs={{2,4},{3,5},{4,2},{5,3},{6,8},{7,9},{8,6},{9,7},{10,12},{11,13},{1... | collective-permute-start | bytes 2359304 | tf_op jit(solution)/shard_map/ppermute | solution.py:433
  11.0 6.6 %copy-start = (s32[32]{0:T(128)S(1)}, s32[32]{0:T(128)}, u32[]{:S(2)}) copy-start(s32[32]{0:T(128)} %param.11) | copy-start | bytes 388
  13.1 9.4 %collective-permute-start.2 = (bf16[1,2,32,768]{3,2,1,0:T(8,128)(2,1)S(1)}, bf16[1,2,32,768]{3,2,1,0:T(8,128)(2,1)S(1)}, u32[]{:S(2)}, u32[]{:S(2)}) collective-permute-start(bf16[1,2,32,768]{3,2,1,0:T(8,128)(2,1)S(1)} %get-tuple-element.75), channel_id=1, source_target_pairs={{0,8},{2,10},{4,12},{6,14},{8,0},{10,2},{12,4},{14,6},{16,24},{18,... | collective-permute-start | bytes 294920 | tf_op jit(solution)/shard_map/ppermute | solution.py:437
  15.0 9.5 %collective-permute-start.3 = (bf16[1,2,32,768]{3,2,1,0:T(8,128)(2,1)S(1)}, bf16[1,2,32,768]{3,2,1,0:T(8,128)(2,1)S(1)}, u32[]{:S(2)}, u32[]{:S(2)}) collective-permute-start(bf16[1,2,32,768]{3,2,1,0:T(8,128)(2,1)S(1)} %get-tuple-element.74), channel_id=1, source_target_pairs={{0,16},{2,18},{4,20},{6,22},{8,24},{10,26},{12,28},{14,30},{16,0},... | collective-permute-start | bytes 294920 | tf_op jit(solution)/shard_map/ppermute | solution.py:437
  17.6 9.1 %collective-permute-start.4 = (bf16[1,2,32,768]{3,2,1,0:T(8,128)(2,1)S(1)}, bf16[1,2,32,768]{3,2,1,0:T(8,128)(2,1)S(1)}, u32[]{:S(2)}, u32[]{:S(2)}) collective-permute-start(bf16[1,2,32,768]{3,2,1,0:T(8,128)(2,1)S(1)} %get-tuple-element.73), channel_id=1, source_target_pairs={{0,24},{2,26},{4,28},{6,30},{8,16},{10,18},{12,20},{14,22},{16,8},... | collective-permute-start | bytes 294920 | tf_op jit(solution)/shard_map/ppermute | solution.py:437
  26.7 4.7 %collective-permute-start.5 = (bf16[2,32,768]{2,1,0:T(8,128)(2,1)S(1)}, bf16[2,32,768]{2,1,0:T(8,128)(2,1)S(1)}, u32[]{:S(2)}, u32[]{:S(2)}) collective-permute-start(bf16[2,32,768]{2,1,0:T(8,128)(2,1)S(1)} %fusion.refs_0_), channel_id=1, source_target_pairs={{0,4},{2,6},{4,0},{6,2},{8,12},{10,14},{12,8},{14,10},{16,20},{18,... | collective-permute-start | bytes 294920 | tf_op jit(solution)/shard_map/ppermute | solution.py:437
  31.4 7.4 %collective-permute-start.10 = (bf16[512,256]{1,0:T(8,128)(2,1)S(1)}, bf16[512,256]{1,0:T(8,128)(2,1)S(1)}, u32[]{:S(2)}, u32[]{:S(2)}) collective-permute-start(bf16[512,256]{1,0:T(8,128)(2,1)S(1)} %get-tuple-element.67), channel_id=1, source_target_pairs={{2,4},{3,5},{4,2},{5,3},{6,8},{7,9},{8,6},{9,7},{10,12},{11,13},{1... | collective-permute-start | bytes 786440 | tf_op jit(solution)/shard_map/ppermute | solution.py:433
  32.6 8.4 %collective-permute-start.7 = (bf16[1,2,32,768]{3,2,1,0:T(8,128)(2,1)S(1)}, bf16[1,2,32,768]{3,2,1,0:T(8,128)(2,1)S(1)}, u32[]{:S(2)}, u32[]{:S(2)}) collective-permute-start(bf16[1,2,32,768]{3,2,1,0:T(8,128)(2,1)S(1)} %bitcast.4), channel_id=1, source_target_pairs={{0,8},{2,10},{4,12},{6,14},{8,0},{10,2},{12,4},{14,6},{16,24},{18,... | collective-permute-start | bytes 294920 | tf_op jit(solution)/shard_map/ppermute | solution.py:437
  33.7 10.6 %collective-permute-start.8 = (bf16[1,2,32,768]{3,2,1,0:T(8,128)(2,1)S(1)}, bf16[1,2,32,768]{3,2,1,0:T(8,128)(2,1)S(1)}, u32[]{:S(2)}, u32[]{:S(2)}) collective-permute-start(bf16[1,2,32,768]{3,2,1,0:T(8,128)(2,1)S(1)} %bitcast.5), channel_id=1, source_target_pairs={{0,16},{2,18},{4,20},{6,22},{8,24},{10,26},{12,28},{14,30},{16,0},... | collective-permute-start | bytes 294920 | tf_op jit(solution)/shard_map/ppermute | solution.py:437
  33.8 10.5 %collective-permute-start.9 = (bf16[1,2,32,768]{3,2,1,0:T(8,128)(2,1)S(1)}, bf16[1,2,32,768]{3,2,1,0:T(8,128)(2,1)S(1)}, u32[]{:S(2)}, u32[]{:S(2)}) collective-permute-start(bf16[1,2,32,768]{3,2,1,0:T(8,128)(2,1)S(1)} %bitcast.6), channel_id=1, source_target_pairs={{0,24},{2,26},{4,28},{6,30},{8,16},{10,18},{12,20},{14,22},{16,8},... | collective-permute-start | bytes 294920 | tf_op jit(solution)/shard_map/ppermute | solution.py:437
  44.4 1.8 %collective-permute-start.11 = (bf16[4,2,32,768]{3,2,1,0:T(8,128)(2,1)S(1)}, bf16[4,2,32,768]{3,2,1,0:T(8,128)(2,1)S(1)}, u32[]{:S(2)}, u32[]{:S(2)}) collective-permute-start(bf16[4,2,32,768]{3,2,1,0:T(8,128)(2,1)S(1)} %constant_dynamic-update-slice_fusion.w_ref), channel_id=1, source_target_pairs={{0,2},{2,0},{4,6},{6,4},{8,10},{10,8},{12,14},{14,12},{16,18},{18,... | collective-permute-start | bytes 1179656 | tf_op jit(solution)/shard_map/ppermute | solution.py:423

commit v8 on v7

--- a/solution.py
+++ b/solution.py
@@ -454,7 +454,7 @@
     for place, radix in enumerate(digits[:0:-1]):
         stride //= radix
         held = held.reshape((radix, stride // digits[0]) + held.shape[1:])
-        came = [to_chip(held[step], step * stride) for step in range(1, radix)]
+        came = [to_chip(held[step], step * stride) for step in sorted(range(1, radix), key=lambda step: (step % 2, step))]
         if place == 0:
             came, near = lax.optimization_barrier((came, near))
         held = sum([part.astype(F32) for part in came], held[0].astype(F32)).astype(BF16)
@@ -470,7 +470,7 @@
     gathered = fresh[None]
     stride = digits[0]
     for radix in digits[1:]:
-        came = [to_chip(gathered, step * stride) for step in range(1, radix)]
+        came = [to_chip(gathered, step * stride) for step in sorted(range(1, radix), key=lambda step: (step % 2, step))]
         if stride == digits[0]:
             gathered, near = lax.optimization_barrier((gathered, near))
             attended = [

time: 47.8 us -> 47.6 us (level)
  no operation moved by 1% of the time
where the time goes in v8:
time: 47.6 us; the launch traced here: 47.4 us
  waiting for transfers between devices  18.7 us (39%)
  Pallas kernels  15.7 us (33%)
  starting transfers between devices  12.8 us (27%)
    ppermute x7, waiting for transfers between devices, to_chip(): return lax.ppermute(x, 'tok', pairs)  12.3 us
    ppermute x7, starting transfers between devices, to_chip(): return lax.ppermute(x, 'tok', pairs)  8.99 us
    ppermute x1, waiting for transfers between devices, to_plane(): return lax.ppermute(x, 'mem', [(p, planes - 1 - p) for p in range(planes)])  5.42 us
    pallas_call x1, Pallas kernels, attend_near(): pl.pallas_call(near_kernel, out_shape=(pltpu.VMEM(queries.shape, BF16), p...  4.95 us
    pallas_call x2, Pallas kernels, attend_far(): pl.pallas_call(body, out_shape=jax.ShapeDtypeStruct((queries.shape[0], DM...  3.44 us
    ppermute x1, starting transfers between devices, to_plane(): return lax.ppermute(x, 'mem', [(p, planes - 1 - p) for p in range(planes)])  2.58 us
    pallas_call x1, Pallas kernels, stage(): pl.pallas_call(functools.partial(stage_kernel, blocks), out_shape=(jax.Sh...  2.36 us
    pallas_call x1, Pallas kernels, half_grads(): pl.pallas_call(grads_kernel, out_shape=jax.ShapeDtypeStruct(shape, BF16),...  2.11 us
  transfers between devices with their start and end apart: 12, of which 7 were waited for; matrix products, arithmetic and copies ran while one was open for 0% of the time, Pallas kernels for 25%

profile of v8, /device:TPU:0, one launch (start us, length us, event | category | flops | bytes accessed | tf_op | source)
XLA Modules:
  0.0 47.4 jit_solution(90850327513841328)
XLA Ops:
  0.0 2.4 %shard_map.64 = (s32[8]{0:T(128)S(1)}, bf16[1536,512]{1,0:T(8,128)(2,1)S(1)}, bf16[1536,256]{1,0:T(8,128)(2,1)S(1)}, bf16[2,64,768]{2,1,0:T(8,128)(2,1)S(1)}, bf...) custom-call(bf16[512,512]{1,0:T(8,128)(2,1)} %k_any.1, bf16[512,512]{1,0:T(8,128)(2,1)} %v_any.1, ...), custom_call_target="tpu_custom_call" | custom-call | tf_op jit(solution)/shard_map/pallas_call | solution.py:114
  2.4 0.5 %collective-permute-start = (bf16[1536,512]{1,0:T(8,128)(2,1)S(1)}, bf16[1536,512]{1,0:T(8,128)(2,1)S(1)}, u32[]{:S(2)}, u32[]{:S(2)}) collective-permute-start(bf16[1536,512]{1,0:T(8,128)(2,1)S(1)} %get-tuple-element.40.own), channel_id=1, source_target_pairs={{0,2},{2,0},{4,6},{6,4},{8,10},{10,8},{12,14},{14,12},{16,18},{18,... | collective-permute-start | bytes 4718600 | tf_op jit(solution)/shard_map/ppermute | solution.py:423
  2.9 2.6 %collective-permute-start.1 = (bf16[2,64,768]{2,1,0:T(8,128)(2,1)S(1)}, bf16[2,64,768]{2,1,0:T(8,128)(2,1)S(1)}, u32[]{:S(2)}, u32[]{:S(2)}) collective-permute-start(bf16[2,64,768]{2,1,0:T(8,128)(2,1)S(1)} %get-tuple-element.42), channel_id=1, source_target_pairs={{0,1},{1,0},{2,3},{3,2},{4,5},{5,4},{6,7},{7,6},{8,9},{9,8},{10,11... | collective-permute-start | bytes 589832 | tf_op jit(solution)/shard_map/ppermute | solution.py:440
  5.5 0.1 collective-permute-start.6
  5.6 5.4 %collective-permute-done.1.sent_w.refs_3_ = bf16[2,64,768]{2,1,0:T(8,128)(2,1)S(1)} collective-permute-done((bf16[2,64,768]{2,1,0:T(8,128)(2,1)S(1)}, bf16[2,64,768]{2,1,0:T(8,128)(2,1)S(1)}, u32[]{:S(2)}, u32[]{:S(2)}) %collective-permute-start.1) | collective-permute-done | bytes 196640 | tf_op jit(solution)/shard_map/ppermute | solution.py:440
  11.0 0.0 collective-permute-done.mate
  11.0 0.0 copy-start
  11.0 2.1 %shard_map.65 = bf16[4,2,32,768]{3,2,1,0:T(8,128)(2,1)S(1)} custom-call(s32[8]{0:T(128)S(1)} %get-tuple-element.39.spots, bf16[1536,512]{1,0:T(8,128)(2,1)S(1)} %get-tuple-element.40.own, bf16[1536,512]{1,0:T(8,128)(2,1)S(1)} %collective-permute-done.mate, bf16[2,64,768]{2,1,0:T(8,128)(2,1)S(1)} %get-tuple-element.41.own_w, ...), custom_call_target="tpu_custom_call" | custom-call | tf_op jit(solution)/shard_map/pallas_call | solution.py:182
  13.1 2.9 %collective-permute-start.2 = (bf16[1,2,32,768]{3,2,1,0:T(8,128)(2,1)S(1)}, bf16[1,2,32,768]{3,2,1,0:T(8,128)(2,1)S(1)}, u32[]{:S(2)}, u32[]{:S(2)}) collective-permute-start(bf16[1,2,32,768]{3,2,1,0:T(8,128)(2,1)S(1)} %get-tuple-element.75), channel_id=1, source_target_pairs={{0,16},{2,18},{4,20},{6,22},{8,24},{10,26},{12,28},{14,30},{16,0},... | collective-permute-start | bytes 294920 | tf_op jit(solution)/shard_map/ppermute | solution.py:437
  16.0 1.6 %collective-permute-start.3 = (bf16[1,2,32,768]{3,2,1,0:T(8,128)(2,1)S(1)}, bf16[1,2,32,768]{3,2,1,0:T(8,128)(2,1)S(1)}, u32[]{:S(2)}, u32[]{:S(2)}) collective-permute-start(bf16[1,2,32,768]{3,2,1,0:T(8,128)(2,1)S(1)} %get-tuple-element.74), channel_id=1, source_target_pairs={{0,8},{2,10},{4,12},{6,14},{8,0},{10,2},{12,4},{14,6},{16,24},{18,... | collective-permute-start | bytes 294920 | tf_op jit(solution)/shard_map/ppermute | solution.py:437
  17.6 0.0 collective-permute-start.4
  17.6 0.0 copy-done
  17.6 5.0 %shard_map.66 = (bf16[512,512]{1,0:T(8,128)(2,1)S(1)}, bf16[512,256]{1,0:T(8,128)(2,1)S(1)}, f32[512,512]{1,0:T(8,128)S(1)}, f32[4,512,128]{2,1,0:T(8,128)S(1)},...) custom-call(s32[8]{0:T(128)S(1)} %get-tuple-element.39.spots, s32[1,32]{1,0:T(1,128)S(1)} %bitcast.8, ...), custom_call_target="tpu_custom_call" | custom-call | tf_op jit(solution)/shard_map/pallas_call | solution.py:327
  22.6 3.0 %collective-permute-done.2 = bf16[1,2,32,768]{3,2,1,0:T(8,128)(2,1)S(1)} collective-permute-done((bf16[1,2,32,768]{3,2,1,0:T(8,128)(2,1)S(1)}, bf16[1,2,32,768]{3,2,1,0:T(8,128)(2,1)S(1)}, u32[]{:S(2)}, u32[]{:S(2)}) %collective-permute-start.2) | collective-permute-done | bytes 98336 | tf_op jit(solution)/shard_map/ppermute | solution.py:437
  25.5 0.0 collective-permute-done.3
  25.5 1.2 %collective-permute-done.4 = bf16[1,2,32,768]{3,2,1,0:T(8,128)(2,1)S(1)} collective-permute-done((bf16[1,2,32,768]{3,2,1,0:T(8,128)(2,1)S(1)}, bf16[1,2,32,768]{3,2,1,0:T(8,128)(2,1)S(1)}, u32[]{:S(2)}, u32[]{:S(2)}) %collective-permute-start.4) | collective-permute-done | bytes 98336 | tf_op jit(solution)/shard_map/ppermute | solution.py:437
  26.7 0.1 fusion.refs_0_
  26.8 0.1 collective-permute-start.5
  26.8 0.0 collective-permute-done.6.far
  26.9 4.6 %collective-permute-done.5.refs_1_ = bf16[2,32,768]{2,1,0:T(8,128)(2,1)S(1)} collective-permute-done((bf16[2,32,768]{2,1,0:T(8,128)(2,1)S(1)}, bf16[2,32,768]{2,1,0:T(8,128)(2,1)S(1)}, u32[]{:S(2)}, u32[]{:S(2)}) %collective-permute-start.5) | collective-permute-done | bytes 98336 | tf_op jit(solution)/shard_map/ppermute | solution.py:437
  31.4 0.5 %collective-permute-start.10 = (bf16[512,256]{1,0:T(8,128)(2,1)S(1)}, bf16[512,256]{1,0:T(8,128)(2,1)S(1)}, u32[]{:S(2)}, u32[]{:S(2)}) collective-permute-start(bf16[512,256]{1,0:T(8,128)(2,1)S(1)} %get-tuple-element.67), channel_id=1, source_target_pairs={{2,4},{3,5},{4,2},{5,3},{6,8},{7,9},{8,6},{9,7},{10,12},{11,13},{1... | collective-permute-start | bytes 786440 | tf_op jit(solution)/shard_map/ppermute | solution.py:433
  32.0 0.7 %shard_map.67 = bf16[2,32,768]{2,1,0:T(8,128)(2,1)S(1)} custom-call(s32[8]{0:T(128)S(1)} %get-tuple-element.39.spots, bf16[2,32,768]{2,1,0:T(8,128)(2,1)S(1)} %fusion.refs_0_, bf16[2,32,768]{2,1,0:T(8,128)(2,1)S(1)} %collective-permute-done.5.refs_1_, f32[2,64,768]{2,1,0:T(8,128)S(1)} %get-tuple-element.56.refs_2_, ...), custom_call_target="tpu_custom_call" | custom-call | tf_op jit(solution)/shard_map/pallas_call | solution.py:225
  32.7 0.5 collective-permute-start.7
  33.1 1.6 %collective-permute-start.8 = (bf16[1,2,32,768]{3,2,1,0:T(8,128)(2,1)S(1)}, bf16[1,2,32,768]{3,2,1,0:T(8,128)(2,1)S(1)}, u32[]{:S(2)}, u32[]{:S(2)}) collective-permute-start(bf16[1,2,32,768]{3,2,1,0:T(8,128)(2,1)S(1)} %bitcast.5), channel_id=1, source_target_pairs={{0,8},{2,10},{4,12},{6,14},{8,0},{10,2},{12,4},{14,6},{16,24},{18,... | collective-permute-start | bytes 294920 | tf_op jit(solution)/shard_map/ppermute | solution.py:437
  34.7 2.4 %collective-permute-start.9 = (bf16[1,2,32,768]{3,2,1,0:T(8,128)(2,1)S(1)}, bf16[1,2,32,768]{3,2,1,0:T(8,128)(2,1)S(1)}, u32[]{:S(2)}, u32[]{:S(2)}) collective-permute-start(bf16[1,2,32,768]{3,2,1,0:T(8,128)(2,1)S(1)} %bitcast.6), channel_id=1, source_target_pairs={{0,24},{2,26},{4,28},{6,30},{8,16},{10,18},{12,20},{14,22},{16,8},... | collective-permute-start | bytes 294920 | tf_op jit(solution)/shard_map/ppermute | solution.py:437
  37.1 1.7 %shard_map.68.refs_0_ = f32[512,256]{1,0:T(8,128)S(1)} custom-call(s32[8]{0:T(128)S(1)} %get-tuple-element.39.spots, bf16[512,512]{1,0:T(8,128)(2,1)S(1)} %get-tuple-element.44.q_ref, bf16[1536,256]{1,0:T(8,128)(2,1)S(1)} %collective-permute-done.6.far, f32[512,512]{1,0:T(8,128)S(1)} %get-tuple-element.63.rest_0_.mixed_ref, ...), custom_call_target="tpu_custom_call" | custom-call | tf_op jit(solution)/shard_map/pallas_call | solution.py:352
  38.9 0.0 collective-permute-done.10.last
  38.9 1.7 %shard_map.69.refs_1_ = f32[512,256]{1,0:T(8,128)S(1)} custom-call(s32[8]{0:T(128)S(1)} %get-tuple-element.39.spots, bf16[512,512]{1,0:T(8,128)(2,1)S(1)} %get-tuple-element.44.q_ref, bf16[1536,256]{1,0:T(8,128)(2,1)S(1)} %collective-permute-done.6.far, bf16[512,256]{1,0:T(8,128)(2,1)S(1)} %collective-permute-done.10.last, ...), custom_call_target="tpu_custom_call" | custom-call | tf_op jit(solution)/shard_map/pallas_call | solution.py:352
  40.6 1.7 %collective-permute-done.7 = bf16[1,2,32,768]{3,2,1,0:T(8,128)(2,1)S(1)} collective-permute-done((bf16[1,2,32,768]{3,2,1,0:T(8,128)(2,1)S(1)}, bf16[1,2,32,768]{3,2,1,0:T(8,128)(2,1)S(1)}, u32[]{:S(2)}, u32[]{:S(2)}) %collective-permute-start.7) | collective-permute-done | bytes 98336 | tf_op jit(solution)/shard_map/ppermute | solution.py:437
  42.3 0.0 collective-permute-done.8
  42.3 1.8 %collective-permute-done.9 = bf16[1,2,32,768]{3,2,1,0:T(8,128)(2,1)S(1)} collective-permute-done((bf16[1,2,32,768]{3,2,1,0:T(8,128)(2,1)S(1)}, bf16[1,2,32,768]{3,2,1,0:T(8,128)(2,1)S(1)}, u32[]{:S(2)}, u32[]{:S(2)}) %collective-permute-start.9) | collective-permute-done | bytes 98336 | tf_op jit(solution)/shard_map/ppermute | solution.py:437
  44.1 0.1 collective-permute-start.11
  44.2 0.7 %shard_map.70.before = f32[512,512]{1,0:T(8,128)S(1)} custom-call(bf16[512,512]{1,0:T(8,128)(2,1)S(1)} %get-tuple-element.44.q_ref, bf16[4,2,32,768]{3,2,1,0:T(8,128)(2,1)S(1)} %constant_dynamic-update-slice_fusion.w_ref), custom_call_target="tpu_custom_call" | custom-call | tf_op jit(solution)/shard_map/pallas_call | solution.py:393
  44.9 1.0 %collective-permute-done.11.w_ref = bf16[4,2,32,768]{3,2,1,0:T(8,128)(2,1)S(1)} collective-permute-done((bf16[4,2,32,768]{3,2,1,0:T(8,128)(2,1)S(1)}, bf16[4,2,32,768]{3,2,1,0:T(8,128)(2,1)S(1)}, u32[]{:S(2)}, u32[]{:S(2)}) %collective-permute-start.11) | collective-permute-done | bytes 393248 | tf_op jit(solution)/shard_map/ppermute | solution.py:423
  45.9 1.4 %shard_map.71 = bf16[512,512]{1,0:T(8,128)(2,1)} custom-call(bf16[512,512]{1,0:T(8,128)(2,1)S(1)} %get-tuple-element.44.q_ref, bf16[4,2,32,768]{3,2,1,0:T(8,128)(2,1)S(1)} %collective-permute-done.11.w_ref, f32[512,512]{1,0:T(8,128)S(1)} %shard_map.70.before, f32[512,256]{1,0:T(8,128)S(1)} %shard_map.68.refs_0_, f32[512,256]{1,0:T(8,128)S(1)} %shard_map.69.refs_1_), custom_call_target="tpu_custom_call" | custom-call | tf_op jit(solution)/shard_map/pallas_call | solution.py:403
  (5 shorter events, 0.1 us)
Async XLA Ops:
  2.4 8.6 %collective-permute-start = (bf16[1536,512]{1,0:T(8,128)(2,1)S(1)}, bf16[1536,512]{1,0:T(8,128)(2,1)S(1)}, u32[]{:S(2)}, u32[]{:S(2)}) collective-permute-start(bf16[1536,512]{1,0:T(8,128)(2,1)S(1)} %get-tuple-element.40.own), channel_id=1, source_target_pairs={{0,2},{2,0},{4,6},{6,4},{8,10},{10,8},{12,14},{14,12},{16,18},{18,... | collective-permute-start | bytes 4718600 | tf_op jit(solution)/shard_map/ppermute | solution.py:423
  2.9 8.1 %collective-permute-start.1 = (bf16[2,64,768]{2,1,0:T(8,128)(2,1)S(1)}, bf16[2,64,768]{2,1,0:T(8,128)(2,1)S(1)}, u32[]{:S(2)}, u32[]{:S(2)}) collective-permute-start(bf16[2,64,768]{2,1,0:T(8,128)(2,1)S(1)} %get-tuple-element.42), channel_id=1, source_target_pairs={{0,1},{1,0},{2,3},{3,2},{4,5},{5,4},{6,7},{7,6},{8,9},{9,8},{10,11... | collective-permute-start | bytes 589832 | tf_op jit(solution)/shard_map/ppermute | solution.py:440
  5.5 21.4 %collective-permute-start.6 = (bf16[1536,256]{1,0:T(8,128)(2,1)S(1)}, bf16[1536,256]{1,0:T(8,128)(2,1)S(1)}, u32[]{:S(2)}, u32[]{:S(2)}) collective-permute-start(bf16[1536,256]{1,0:T(8,128)(2,1)S(1)} %get-tuple-element.54), channel_id=1, source_target_pairs={{2,4},{3,5},{4,2},{5,3},{6,8},{7,9},{8,6},{9,7},{10,12},{11,13},{1... | collective-permute-start | bytes 2359304 | tf_op jit(solution)/shard_map/ppermute | solution.py:433
  11.0 6.6 %copy-start = (s32[32]{0:T(128)S(1)}, s32[32]{0:T(128)}, u32[]{:S(2)}) copy-start(s32[32]{0:T(128)} %param.11) | copy-start | bytes 388
  13.1 12.4 %collective-permute-start.2 = (bf16[1,2,32,768]{3,2,1,0:T(8,128)(2,1)S(1)}, bf16[1,2,32,768]{3,2,1,0:T(8,128)(2,1)S(1)}, u32[]{:S(2)}, u32[]{:S(2)}) collective-permute-start(bf16[1,2,32,768]{3,2,1,0:T(8,128)(2,1)S(1)} %get-tuple-element.75), channel_id=1, source_target_pairs={{0,16},{2,18},{4,20},{6,22},{8,24},{10,26},{12,28},{14,30},{16,0},... | collective-permute-start | bytes 294920 | tf_op jit(solution)/shard_map/ppermute | solution.py:437
  16.0 9.5 %collective-permute-start.3 = (bf16[1,2,32,768]{3,2,1,0:T(8,128)(2,1)S(1)}, bf16[1,2,32,768]{3,2,1,0:T(8,128)(2,1)S(1)}, u32[]{:S(2)}, u32[]{:S(2)}) collective-permute-start(bf16[1,2,32,768]{3,2,1,0:T(8,128)(2,1)S(1)} %get-tuple-element.74), channel_id=1, source_target_pairs={{0,8},{2,10},{4,12},{6,14},{8,0},{10,2},{12,4},{14,6},{16,24},{18,... | collective-permute-start | bytes 294920 | tf_op jit(solution)/shard_map/ppermute | solution.py:437
  17.6 9.1 %collective-permute-start.4 = (bf16[1,2,32,768]{3,2,1,0:T(8,128)(2,1)S(1)}, bf16[1,2,32,768]{3,2,1,0:T(8,128)(2,1)S(1)}, u32[]{:S(2)}, u32[]{:S(2)}) collective-permute-start(bf16[1,2,32,768]{3,2,1,0:T(8,128)(2,1)S(1)} %get-tuple-element.73), channel_id=1, source_target_pairs={{0,24},{2,26},{4,28},{6,30},{8,16},{10,18},{12,20},{14,22},{16,8},... | collective-permute-start | bytes 294920 | tf_op jit(solution)/shard_map/ppermute | solution.py:437
  26.8 4.7 %collective-permute-start.5 = (bf16[2,32,768]{2,1,0:T(8,128)(2,1)S(1)}, bf16[2,32,768]{2,1,0:T(8,128)(2,1)S(1)}, u32[]{:S(2)}, u32[]{:S(2)}) collective-permute-start(bf16[2,32,768]{2,1,0:T(8,128)(2,1)S(1)} %fusion.refs_0_), channel_id=1, source_target_pairs={{0,4},{2,6},{4,0},{6,2},{8,12},{10,14},{12,8},{14,10},{16,20},{18,... | collective-permute-start | bytes 294920 | tf_op jit(solution)/shard_map/ppermute | solution.py:437
  31.4 7.4 %collective-permute-start.10 = (bf16[512,256]{1,0:T(8,128)(2,1)S(1)}, bf16[512,256]{1,0:T(8,128)(2,1)S(1)}, u32[]{:S(2)}, u32[]{:S(2)}) collective-permute-start(bf16[512,256]{1,0:T(8,128)(2,1)S(1)} %get-tuple-element.67), channel_id=1, source_target_pairs={{2,4},{3,5},{4,2},{5,3},{6,8},{7,9},{8,6},{9,7},{10,12},{11,13},{1... | collective-permute-start | bytes 786440 | tf_op jit(solution)/shard_map/ppermute | solution.py:433
  32.7 9.6 %collective-permute-start.7 = (bf16[1,2,32,768]{3,2,1,0:T(8,128)(2,1)S(1)}, bf16[1,2,32,768]{3,2,1,0:T(8,128)(2,1)S(1)}, u32[]{:S(2)}, u32[]{:S(2)}) collective-permute-start(bf16[1,2,32,768]{3,2,1,0:T(8,128)(2,1)S(1)} %bitcast.4), channel_id=1, source_target_pairs={{0,16},{2,18},{4,20},{6,22},{8,24},{10,26},{12,28},{14,30},{16,0},... | collective-permute-start | bytes 294920 | tf_op jit(solution)/shard_map/ppermute | solution.py:437
  33.1 9.2 %collective-permute-start.8 = (bf16[1,2,32,768]{3,2,1,0:T(8,128)(2,1)S(1)}, bf16[1,2,32,768]{3,2,1,0:T(8,128)(2,1)S(1)}, u32[]{:S(2)}, u32[]{:S(2)}) collective-permute-start(bf16[1,2,32,768]{3,2,1,0:T(8,128)(2,1)S(1)} %bitcast.5), channel_id=1, source_target_pairs={{0,8},{2,10},{4,12},{6,14},{8,0},{10,2},{12,4},{14,6},{16,24},{18,... | collective-permute-start | bytes 294920 | tf_op jit(solution)/shard_map/ppermute | solution.py:437
  34.7 9.4 %collective-permute-start.9 = (bf16[1,2,32,768]{3,2,1,0:T(8,128)(2,1)S(1)}, bf16[1,2,32,768]{3,2,1,0:T(8,128)(2,1)S(1)}, u32[]{:S(2)}, u32[]{:S(2)}) collective-permute-start(bf16[1,2,32,768]{3,2,1,0:T(8,128)(2,1)S(1)} %bitcast.6), channel_id=1, source_target_pairs={{0,24},{2,26},{4,28},{6,30},{8,16},{10,18},{12,20},{14,22},{16,8},... | collective-permute-start | bytes 294920 | tf_op jit(solution)/shard_map/ppermute | solution.py:437
  44.1 1.8 %collective-permute-start.11 = (bf16[4,2,32,768]{3,2,1,0:T(8,128)(2,1)S(1)}, bf16[4,2,32,768]{3,2,1,0:T(8,128)(2,1)S(1)}, u32[]{:S(2)}, u32[]{:S(2)}) collective-permute-start(bf16[4,2,32,768]{3,2,1,0:T(8,128)(2,1)S(1)} %constant_dynamic-update-slice_fusion.w_ref), channel_id=1, source_target_pairs={{0,2},{2,0},{4,6},{6,4},{8,10},{10,8},{12,14},{14,12},{16,18},{18,... | collective-permute-start | bytes 1179656 | tf_op jit(solution)/shard_map/ppermute | solution.py:423
